TPU v7x, 512 devices: a whole 4x4x16 slice. The times are simulated.
512 devices in a mesh: cam: 128 (over x, z, core), sub: 4 (over y).
Axes of the slice: x: 4, y: 4, z: 16, core: 2. Of those that a mesh axis runs over, the one named last changes fastest.
Arguments:
- tokens: bfloat16 [1024, 32, 768], P('cam', 'sub'), may hold values from -6 to 6
- pairs: int32 [4096, 2], P('cam'), may hold values from 0 to 1023, as said below
- confidence: int32 [4096], P('cam'), may hold values from 1 to 15
- w_query: bfloat16 [768, 768], replicated, may hold values from -1 to 1
- w_key: bfloat16 [768, 768], replicated, may hold values from -10 to 10
- w_value: bfloat16 [768, 768], replicated, may hold values from -0.21875 to 0.21875
- w_out: bfloat16 [768, 768], replicated, may hold values from -0.21875 to 0.21875
Outputs:
- decoded: bfloat16 [1024, 32, 768], P('cam', 'sub')
Inputs may be any that keep to these rules, and one draw needn't show every extreme that they name: Pair p belongs to index p // 32 of cam and its first image lies among that index's images (ids 8 * index to 8 * index + 7). The two images of a pair differ. Among the pairs of one index of cam at most 2 have their second image among the images of any one index of cam (ids 8 * k to 8 * k + 7), and every index of cam has such a block with exactly 2.
All inputs are finite; a program needn't handle non-finite values.
Results may differ from a plain program's by a relative error of at most 0.0092.
Values may be sent and summed in bfloat16 or wider, within the bound.
No kernel may reach another device: no remote copies, remote signals or barrier semaphores. Data moves between devices by JAX's collectives and lax.ppermute only.
A program may use at most 128 MiB of HBM per device.

v0:
```python
import jax
import jax.numpy as jnp
from jax import lax
from jax.sharding import PartitionSpec as P

HEADS = 12


def layer_norm(token_rows):
    numbers = token_rows.astype(jnp.float32)
    average = jnp.mean(numbers, axis=-1, keepdims=True)
    centred = numbers - average
    spread = jnp.mean(centred * centred, axis=-1, keepdims=True)
    return (centred * lax.rsqrt(spread + 1e-06)).astype(jnp.bfloat16)


def project(normed, weight):
    return jnp.einsum("...d,de->...e", normed, weight, preferred_element_type=jnp.float32).astype(
        jnp.bfloat16
    )


def attend(queries, key_rows, value_rows, head_size):
    pair_count, row_count, model_width = queries.shape
    head_count = model_width // head_size
    query_split = queries.reshape(pair_count, row_count, head_count, head_size)
    key_split = key_rows.reshape(pair_count, key_rows.shape[1], head_count, head_size)
    value_split = value_rows.reshape(pair_count, key_rows.shape[1], head_count, head_size)
    scores = jnp.einsum(
        "prhe,pkhe->phrk", query_split, key_split, preferred_element_type=jnp.float32
    ) * head_size ** (-0.5)
    row_max = jnp.max(scores, axis=-1, keepdims=True)
    exponent = jnp.exp(scores - row_max)
    probabilities = (exponent / jnp.sum(exponent, axis=-1, keepdims=True)).astype(jnp.bfloat16)
    mixed = jnp.einsum(
        "phrk,pkhe->prhe", probabilities, value_split, preferred_element_type=jnp.float32
    )
    return mixed.astype(jnp.bfloat16).reshape(pair_count, row_count, model_width)


def finish(mixed, residual_rows, w_out, pair_scale):
    projected = jnp.einsum("prd,de->pre", mixed, w_out, preferred_element_type=jnp.float32)
    return (pair_scale * (residual_rows.astype(jnp.float32) + projected)).astype(jnp.bfloat16)


def rank_of(owner_index):
    position = jnp.arange(owner_index.shape[0], dtype=jnp.int32)
    earlier_same = (owner_index[None, :] == owner_index[:, None]) & (
        position[None, :] < position[:, None]
    )
    return jnp.sum(earlier_same.astype(jnp.int32), axis=1)


def body(tokens, pairs, confidence, w_query, w_key, w_value, w_out):
    img_dev, row_count, model_width = tokens.shape
    pair_dev = pairs.shape[0]
    owner_count = lax.axis_size("cam")
    head_size = model_width // HEADS
    capacity = max(2, 2 * pair_dev // owner_count)
    slot_count = owner_count * capacity
    normed = layer_norm(tokens)
    query_local = project(normed, w_query)
    key_local = project(normed, w_key)
    value_local = project(normed, w_value)
    key_whole, value_whole = (
        lax.all_gather(key_local, "sub", axis=1, tiled=True),
        lax.all_gather(value_local, "sub", axis=1, tiled=True),
    )
    first_local = pairs[:, 0] % img_dev
    owner_index = pairs[:, 1] // img_dev
    partner_local = pairs[:, 1] % img_dev
    slot_index = owner_index * capacity + rank_of(owner_index)
    slot_match = slot_index[:, None] == jnp.arange(slot_count, dtype=jnp.int32)[None, :]
    wanted = jnp.sum(jnp.where(slot_match, partner_local[:, None], 0), axis=0).reshape(
        owner_count, capacity
    )
    weight_sent = jnp.sum(jnp.where(slot_match, confidence[:, None], 0), axis=0).reshape(
        owner_count, capacity
    )
    wanted, asked_conf = (
        lax.all_to_all(wanted, "cam", split_axis=0, concat_axis=0, tiled=True),
        lax.all_to_all(weight_sent, "cam", split_axis=0, concat_axis=0, tiled=True),
    )
    wanted_flat = wanted.reshape(-1)
    outgoing = jnp.take(tokens, wanted_flat, axis=0)
    mine_rows = jnp.take(tokens, first_local, axis=0)
    query_mine = jnp.take(query_local, first_local, axis=0)
    key_mine = jnp.take(key_whole, first_local, axis=0)
    value_mine = jnp.take(value_whole, first_local, axis=0)
    arrived = lax.all_to_all(outgoing, "cam", split_axis=0, concat_axis=0, tiled=True)
    partner_rows = jnp.take(arrived, slot_index, axis=0)
    partner_normed = layer_norm(partner_rows)
    key_far, value_far = (
        lax.all_gather(project(partner_normed, w_key), "sub", axis=1, tiled=True),
        lax.all_gather(project(partner_normed, w_value), "sub", axis=1, tiled=True),
    )
    mixed_mine = attend(query_mine, key_far, value_far, head_size)
    query_far = project(partner_normed, w_query)
    pair_scale = confidence.astype(jnp.float32)[:, None, None]
    share_mine = finish(mixed_mine, mine_rows, w_out, pair_scale)
    share_far = finish(
        attend(query_far, key_mine, value_mine, head_size), partner_rows, w_out, pair_scale
    )
    return_buffer = (
        jnp.zeros((slot_count, row_count, model_width), jnp.bfloat16).at[slot_index].set(share_far)
    )
    returned = lax.all_to_all(return_buffer, "cam", split_axis=0, concat_axis=0, tiled=True)
    image_iota = jnp.arange(img_dev, dtype=jnp.int32)
    asked_flat = asked_conf.reshape(-1)
    pick_far = (wanted_flat[None, :] == image_iota[:, None]) & (asked_flat > 0)[None, :]
    pick_mine = first_local[None, :] == image_iota[:, None]
    summed = jnp.einsum(
        "is,srd->ird", pick_far.astype(jnp.bfloat16), returned, preferred_element_type=jnp.float32
    )
    summed = summed + jnp.einsum(
        "ip,prd->ird",
        pick_mine.astype(jnp.bfloat16),
        share_mine,
        preferred_element_type=jnp.float32,
    )
    weight_sum = jnp.sum(jnp.where(pick_far, asked_flat[None, :], 0), axis=1) + jnp.sum(
        jnp.where(pick_mine, confidence[None, :], 0), axis=1
    )
    return (summed / jnp.maximum(weight_sum.astype(jnp.float32), 1.0)[:, None, None]).astype(
        jnp.bfloat16
    )


def solution(mesh):
    in_specs = (P("cam", "sub", None), P("cam", None), P("cam"), P(), P(), P(), P())
    out_specs = P("cam", "sub", None)
    return jax.shard_map(body, mesh=mesh, in_specs=in_specs, out_specs=out_specs, check_vma=False)
```

profile of v0, /device:TPU:1, one launch (start us, length us, event | category | flops | bytes accessed | tf_op | source)
XLA Modules:
  0.0 404.8 jit_solution(6482859891726579752)
XLA Ops:
  6.5 0.8 fusion.88
  7.3 0.7 and_select_fusion.2
  8.0 0.7 and_select_fusion.3
  8.7 0.2 convert_reduce_fusion.2
  8.9 0.7 select_reduce_fusion
  9.6 0.1 all_to_all.18
  9.8 35.2 %all_to_all.28 = s32[128,1,2]{2,1,0:T(1,128)S(1)} all-to-all(s32[128,1,2]{2,1,0:T(1,128)S(1)} %bitcast.71), channel_id=1, replica_groups=mesh['cam'=128,'sub'=4] {'cam'}, dimensions={0} | all-to-all | bytes 2048 | tf_op jit(solution)/shard_map/all_to_all | solution.py:81
  45.0 0.5 broadcast.255
  45.6 0.8 reduce.8
  46.4 0.1 eq.69
  46.5 0.1 reshape.189
  46.7 2.5 gather_fusion
  49.2 3.6 broadcast_select_fusion
  52.8 7.8 %all-to-all-start.2 = ((bf16[256,8,768]{2,1,0:T(8,128)(2,1)}), bf16[256,8,768]{2,1,0:T(8,128)(2,1)}, u32[]{:S(2)}, u32[]{:S(2)}) async-start(bf16[256,8,768]{2,1,0:T(8,128)(2,1)} %broadcast_select_fusion), calls=%async_computation.2 | async-start | bytes 6291456 | tf_op jit(solution)/shard_map/all_to_all | solution.py:90
  60.7 0.2 fusion.71
  60.9 0.4 fusion.50
  61.3 11.8 %all_gather.12 = bf16[8,32,768]{2,1,0:T(8,128)(2,1)S(1)} all-gather(bf16[8,8,768]{2,1,0:T(8,128)(2,1)S(1)} %fusion.50), channel_id=1, replica_groups=mesh['cam'=128,'sub'=4] {'sub'}, dimensions={1}, use_global_device_ids=true | all-gather | bytes 491520 | tf_op jit(solution)/shard_map/all_gather | solution.py:67
  73.1 0.6 gather_fusion.2
  73.8 1.6 fusion.56
  75.4 10.8 %all_gather.13 = bf16[8,32,768]{2,1,0:T(8,128)(2,1)S(1)} all-gather(bf16[8,8,768]{2,1,0:T(8,128)(2,1)S(1)} %fusion.56), channel_id=1, replica_groups=mesh['cam'=128,'sub'=4] {'sub'}, dimensions={1}, use_global_device_ids=true | all-gather | bytes 491520 | tf_op jit(solution)/shard_map/all_gather | solution.py:66
  86.3 1.8 gather_fusion.3
  88.1 3.4 broadcast_select_fusion.1
  91.5 6.0 %reshape.192 = bf16[32,32,12,64]{3,2,1,0:T(8,128)(2,1)} reshape(bf16[32,32,768]{2,1,0:T(8,128)(2,1)} %get-tuple-element.15) | data formatting | bytes 3145728 | tf_op jit(solution)/shard_map/reshape | solution.py:27
  97.5 3.8 reshape.190
  101.3 0.8 all_to_all.20
  102.1 101.0 %all-to-all-done.2 = bf16[256,8,768]{2,1,0:T(8,128)(2,1)} async-done(((bf16[256,8,768]{2,1,0:T(8,128)(2,1)}), bf16[256,8,768]{2,1,0:T(8,128)(2,1)}, u32[]{:S(2)}, u32[]{:S(2)}) %all-to-all-start.2) | async-done | bytes 3145760 | tf_op jit(solution)/shard_map/all_to_all | solution.py:90
  203.2 10.0 %all-to-all-start.1 = ((s32[128,1,2]{2,1,0:T(1,128)}), s32[128,1,2]{2,1,0:T(1,128)S(1)}, u32[]{:S(2)}, u32[]{:S(2)}) async-start(s32[128,1,2]{2,1,0:T(1,128)} %bitcast.6), calls=%async_computation.1 | async-start | bytes 131072 | tf_op jit(solution)/shard_map/all_to_all | solution.py:82
  213.2 2.5 gather_fusion.1
  215.6 0.2 convert_reduce_fusion
  215.9 0.3 fusion.62
  216.2 1.8 convolution_convert_fusion.2
  218.0 0.6 reshape.191
  218.6 5.3 %fusion.92 = (f32[32,12,8]{2,1,0:T(8,128)S(1)}, f32[32,12,8,32]{3,2,1,0:T(8,128)}) fusion(bf16[32,32,12,64]{3,2,1,0:T(8,128)(2,1)} %reshape.192, bf16[32,8,12,64]{3,2,1,0:T(8,128)(2,1)S(1)} %reshape.191), kind=kOutput, calls=%fused_computation.129 | convolution fusion | flops 12877855 | bytes 2371584 | tf_op jit(solution)/shard_map/sub | solution.py:33
  223.9 3.7 fusion.31
  227.5 0.2 copy.47
  227.8 0.6 reshape.193
  228.4 0.5 fusion.36
  228.9 2.0 broadcast_in_dim.113
  230.9 4.3 %scatter_fusion = bf16[256,8,768]{2,1,0:T(8,128)(2,1)} fusion(bf16[256,8,768]{2,1,0:T(8,128)(2,1)} %broadcast_in_dim.113, s32[32]{0:T(128)S(1)} %get-tuple-element.14, bf16[32,8,768]{2,1,0:T(8,128)(2,1)S(1)} %fusion.36), kind=kCustom, calls=%fused_computation.6 | custom fusion | bytes 1179776 | tf_op jit(solution)/shard_map/scatter | solution.py:105
  235.2 16.6 %all-to-all-start.3 = ((bf16[256,8,768]{2,1,0:T(8,128)(2,1)}), bf16[256,8,768]{2,1,0:T(8,128)(2,1)}, u32[]{:S(2)}, u32[]{:S(2)}) async-start(bf16[256,8,768]{2,1,0:T(8,128)(2,1)} %scatter_fusion), calls=%async_computation.3 | async-start | bytes 6291456 | tf_op jit(solution)/shard_map/all_to_all | solution.py:107
  251.8 2.6 convolution_convert_fusion
  254.4 0.3 all-gather.3.cloned.1.call-start
  254.7 2.6 convolution_convert_fusion.1
  257.3 0.6 gather_fusion.4
  257.9 1.6 fusion.53
  259.5 0.6 gather_fusion.5
  260.2 0.6 reshape.195
  260.8 0.1 select_reduce_fusion.3
  260.9 0.8 reduce.9
  261.7 0.1 reshape.188
  261.9 0.1 select_reduce_fusion.2
  262.0 28.1 %all-gather.5.cloned.1.call-done = bf16[32,32,768]{2,1,0:T(8,128)(2,1)} async-done(((bf16[32,8,768]{2,1,0:T(8,128)(2,1)}), bf16[32,32,768]{2,1,0:T(8,128)(2,1)}) %all-gather.5.cloned.1.call-update) | async-done | bytes 1572880 | tf_op jit(solution)/shard_map/all_gather | solution.py:94
  290.1 5.9 %reshape.196 = bf16[32,32,12,64]{3,2,1,0:T(8,128)(2,1)} reshape(bf16[32,32,768]{2,1,0:T(8,128)(2,1)} %all-gather.5.cloned.1.call-done) | data formatting | bytes 3145728 | tf_op jit(solution)/shard_map/reshape | solution.py:27
  296.0 30.6 %all-gather.3.cloned.1.call-done = bf16[32,32,768]{2,1,0:T(8,128)(2,1)} async-done(((bf16[32,8,768]{2,1,0:T(8,128)(2,1)}), bf16[32,32,768]{2,1,0:T(8,128)(2,1)}) %all-gather.3.cloned.1.call-update) | async-done | bytes 1572880 | tf_op jit(solution)/shard_map/all_gather | solution.py:95
  326.6 5.9 %reshape.194 = bf16[32,32,12,64]{3,2,1,0:T(8,128)(2,1)} reshape(bf16[32,32,768]{2,1,0:T(8,128)(2,1)} %all-gather.3.cloned.1.call-done) | data formatting | bytes 3145728 | tf_op jit(solution)/shard_map/reshape | solution.py:28
  332.5 5.2 %fusion.93 = (f32[32,12,8]{2,1,0:T(8,128)S(1)}, f32[32,12,8,32]{3,2,1,0:T(8,128)}) fusion(bf16[32,32,12,64]{3,2,1,0:T(8,128)(2,1)} %reshape.196, bf16[32,8,12,64]{3,2,1,0:T(8,128)(2,1)S(1)} %reshape.195), kind=kOutput, calls=%fused_computation.130 | convolution fusion | flops 12877855 | bytes 2371584 | tf_op jit(solution)/shard_map/sub | solution.py:33
  337.7 3.7 fusion.28
  341.3 0.2 copy.52
  341.6 0.6 reshape.197
  342.2 0.5 fusion.37
  342.7 51.5 %all-to-all-done.3 = bf16[256,8,768]{2,1,0:T(8,128)(2,1)} async-done(((bf16[256,8,768]{2,1,0:T(8,128)(2,1)}), bf16[256,8,768]{2,1,0:T(8,128)(2,1)}, u32[]{:S(2)}, u32[]{:S(2)}) %all-to-all-start.3) | async-done | bytes 3145760 | tf_op jit(solution)/shard_map/all_to_all | solution.py:107
  394.3 2.8 fusion.6
  397.1 0.2 fusion.59
  397.3 0.7 copy.54
  (34 shorter events, 0.4 us)
Async XLA Ops:
  6.5 221.9 %copy-start = (bf16[768,768]{1,0:T(8,128)(2,1)S(1)}, bf16[768,768]{1,0:T(8,128)(2,1)}, u32[]{:S(2)}) copy-start(bf16[768,768]{1,0:T(8,128)(2,1)} %param.17) | copy-start | bytes 3538948
  6.5 40.1 %copy-start.1 = (bf16[8,8,768]{2,1,0:T(8,128)(2,1)S(1)}, bf16[8,8,768]{2,1,0:T(8,128)(2,1)}, u32[]{:S(2)}) copy-start(bf16[8,8,768]{2,1,0:T(8,128)(2,1)} %param.11) | copy-start | bytes 294916
  52.8 7.8 %copy-start.4 = (s32[32]{0:T(128)S(1)}, s32[32]{0:T(128)}, u32[]{:S(2)}) copy-start(s32[32]{0:T(128)} %param.13) | copy-start | bytes 388
  52.8 7.8 %copy-start.5 = (s32[32,2]{0,1:T(2,128)S(1)}, s32[32,2]{0,1:T(2,128)}, u32[]{:S(2)}) copy-start(s32[32,2]{0,1:T(2,128)} %param.12) | copy-start | bytes 772
  52.8 8.1 %copy-start.3 = (bf16[768,768]{1,0:T(8,128)(2,1)S(1)}, bf16[768,768]{1,0:T(8,128)(2,1)}, u32[]{:S(2)}) copy-start(bf16[768,768]{1,0:T(8,128)(2,1)} %param.16) | copy-start | bytes 3538948
  52.8 150.3 %all-to-all-start.2 = ((bf16[256,8,768]{2,1,0:T(8,128)(2,1)}), bf16[256,8,768]{2,1,0:T(8,128)(2,1)}, u32[]{:S(2)}, u32[]{:S(2)}) async-start(bf16[256,8,768]{2,1,0:T(8,128)(2,1)} %broadcast_select_fusion), calls=%async_computation.2 | async-start | bytes 6291456 | tf_op jit(solution)/shard_map/all_to_all | solution.py:90
  91.5 6.0 %copy-start.2 = (bf16[32,32,768]{2,1,0:T(8,128)(2,1)S(1)}, bf16[32,32,768]{2,1,0:T(8,128)(2,1)}, u32[]{:S(2)}) copy-start(bf16[32,32,768]{2,1,0:T(8,128)(2,1)} %get-tuple-element.16) | copy-start | bytes 4718596
  203.2 32.1 %all-to-all-start.1 = ((s32[128,1,2]{2,1,0:T(1,128)}), s32[128,1,2]{2,1,0:T(1,128)S(1)}, u32[]{:S(2)}, u32[]{:S(2)}) async-start(s32[128,1,2]{2,1,0:T(1,128)} %bitcast.6), calls=%async_computation.1 | async-start | bytes 131072 | tf_op jit(solution)/shard_map/all_to_all | solution.py:82
  235.2 159.0 %all-to-all-start.3 = ((bf16[256,8,768]{2,1,0:T(8,128)(2,1)}), bf16[256,8,768]{2,1,0:T(8,128)(2,1)}, u32[]{:S(2)}, u32[]{:S(2)}) async-start(bf16[256,8,768]{2,1,0:T(8,128)(2,1)} %scatter_fusion), calls=%async_computation.3 | async-start | bytes 6291456 | tf_op jit(solution)/shard_map/all_to_all | solution.py:107
  251.8 38.3 %all-gather.5.cloned.1.call-start = ((), (), s32[]{:S(2)}) async-start(), calls=%async_computation.5 | async-start | bytes 1966080 | tf_op jit(solution)/shard_map/all_gather | solution.py:94
  254.4 72.1 %all-gather.3.cloned.1.call-start = ((), (), s32[]{:S(2)}) async-start(), calls=%async_computation.4 | async-start | bytes 1966080 | tf_op jit(solution)/shard_map/all_gather | solution.py:95
Sparse Core Ops, SparseCore 0:
  254.7 35.3 all-gather.4
  292.2 34.3 all-gather.2
where the time goes:
time: 407 us; the launch traced here: 405 us
  waiting for transfers between devices  211 us (52%)
  blocking collectives  57.9 us (14%)
  local copies, waits for them, and re-layouts  42 us (10%)
  starting transfers between devices  34.6 us (9%)
  matrix products  32.4 us (8%)
  between operations  13.7 us (3%)
  other arithmetic  12.9 us (3%)
    all_to_all x1, waiting for transfers between devices, body(): lax.all_to_all(outgoing, 'cam', split_axis=0, concat_axis=0, tiled=True)  101 us
    all_to_all x1, waiting for transfers between devices, body(): lax.all_to_all(return_buffer, 'cam', split_axis=0, concat_axis=0, tiled=T...  51.5 us
    all_to_all x1, blocking collectives, body(): lax.all_to_all(wanted, 'cam', split_axis=0, concat_axis=0, tiled=True)  35.2 us
    all_gather x1, waiting for transfers between devices, body(): lax.all_gather(project(partner_normed, w_value), 'sub', axis=1, tiled=True)  30.6 us
    all_gather x1, waiting for transfers between devices, body(): lax.all_gather(project(partner_normed, w_key), 'sub', axis=1, tiled=True)  28.1 us
    all_to_all x1, starting transfers between devices, body(): lax.all_to_all(return_buffer, 'cam', split_axis=0, concat_axis=0, tiled=T...  16.6 us
    reshape x2, local copies, waits for them, and re-layouts, attend(): key_rows.reshape(pair_count, key_rows.shape[1], head_count, head_size)  11.9 us
    all_gather x1, blocking collectives, body(): lax.all_gather(value_local, 'sub', axis=1, tiled=True)  11.8 us
  transfers between devices with their start and end apart: 5, of which 4 were waited for; matrix products, arithmetic and copies ran while one was open for 18% of the time, Pallas kernels for 0%

commit v1 on v0

v1 whole, which is shorter than its diff:
```python
import jax
import jax.numpy as jnp
from jax import lax
from jax.experimental import pallas as pl
from jax.experimental.pallas import tpu as pltpu
from jax.sharding import Mesh, PartitionSpec as P

HEADS = 12
D = 768
TOK = 32
HEAD = D // HEADS
X, Z, CORE, SUB = 4, 16, 2, 4
IMG = 8
PAIR = 32
ROWS = TOK // SUB
NX = X * IMG
NY = Z * CORE * 2
GROUP = 4
INFO = 8
LIST = NX * NY + GROUP


def layer_norm(token_rows):
    numbers = token_rows.astype(jnp.float32)
    average = jnp.mean(numbers, axis=-1, keepdims=True)
    centred = numbers - average
    spread = jnp.mean(centred * centred, axis=-1, keepdims=True)
    return (centred * lax.rsqrt(spread + 1e-06)).astype(jnp.bfloat16)


def attend_kernel(mask_ref, weight_ref, q_ref, kv_ref, out_ref, acc, sides, scale):
    acc[...] = jnp.zeros_like(acc)

    def list_image(y, count):
        def more(state):
            return state[0] != 0

        def take(state):
            bits, n = state
            x = 31 - lax.clz(bits & -bits)
            sides[n] = y * NX + x
            scale[n] = weight_ref[y * NX + x]
            return bits & (bits - 1), n + 1

        return lax.while_loop(more, take, (mask_ref[y], count))[1]

    count = lax.fori_loop(0, NY, list_image, jnp.int32(0))
    for k in range(GROUP):
        sides[count + k] = 0
        scale[count + k] = 0.0

    low_half = lax.broadcasted_iota(jnp.int32, (TOK, 128), 1) < HEAD
    zeros = jnp.zeros((TOK, 128), jnp.bfloat16)

    def one_side(n):
        side = sides[n]
        y = side // NX
        x = side % NX
        q_row = pl.multiple_of((x % IMG) * TOK, TOK)
        k_row = pl.multiple_of((y % 2) * TOK, TOK)
        query = q_ref[x // IMG, pl.ds(q_row, TOK), :]
        keys = kv_ref[y // 2, pl.ds(k_row, TOK), 0:D]
        values = kv_ref[y // 2, pl.ds(k_row, TOK), D : 2 * D]
        parts = []
        for t in range(HEADS // 4):
            left = query[:, 256 * t : 256 * t + 128]
            right = query[:, 256 * t + 128 : 256 * t + 256]
            spread = jnp.concatenate(
                [
                    jnp.concatenate([jnp.where(low_half, left, 0), zeros], axis=1),
                    jnp.concatenate([jnp.where(low_half, 0, left), zeros], axis=1),
                    jnp.concatenate([zeros, jnp.where(low_half, right, 0)], axis=1),
                    jnp.concatenate([zeros, jnp.where(low_half, 0, right)], axis=1),
                ],
                axis=0,
            )
            scores = lax.dot_general(
                keys[:, 256 * t : 256 * t + 256],
                spread,
                (((1,), (1,)), ((), ())),
                preferred_element_type=jnp.float32,
            )
            exponent = jnp.exp(scores - jnp.max(scores, axis=0, keepdims=True))
            total = jnp.sum(exponent, axis=0, keepdims=True)
            probabilities = (exponent * (1.0 / total)).astype(jnp.bfloat16)
            for j in range(2):
                both = lax.dot_general(
                    probabilities[:, 64 * j : 64 * j + 64],
                    values[:, 256 * t + 128 * j : 256 * t + 128 * j + 128],
                    (((0,), (0,)), ((), ())),
                    preferred_element_type=jnp.float32,
                )
                parts.append(jnp.where(low_half, both[:TOK], both[TOK:]))
        return x, scale[n] * jnp.concatenate(parts, axis=1)

    def step(g, carry):
        results = [one_side(g * GROUP + k) for k in range(GROUP)]
        for x, mixed in results:
            rows = pl.ds(pl.multiple_of(x * TOK, TOK), TOK)
            acc[rows, :] = acc[rows, :] + mixed
        return carry

    lax.fori_loop(0, (count + GROUP - 1) // GROUP, step, jnp.int32(0))

    for xx in range(X):
        for s in range(SUB):
            for i in range(IMG // 2):
                first = (xx * IMG + 2 * i) * TOK + s * ROWS
                block = jnp.concatenate([acc[first : first + ROWS, :], acc[first + TOK : first + TOK + ROWS, :]], axis=0)
                out_ref[xx * SUB + s, 2 * i * ROWS : 2 * (i + 1) * ROWS, :] = block.astype(jnp.bfloat16)


def attend(mask, weight, queries, keys_values):
    vmem = pl.BlockSpec(memory_space=pltpu.VMEM)
    smem = pl.BlockSpec(memory_space=pltpu.SMEM)
    return pl.pallas_call(
        attend_kernel,
        out_shape=jax.ShapeDtypeStruct((X * SUB, IMG * ROWS, D), jnp.bfloat16),
        in_specs=[smem, smem, vmem, vmem],
        out_specs=vmem,
        scratch_shapes=[
            pltpu.VMEM((NX * TOK, D), jnp.float32),
            pltpu.SMEM((LIST,), jnp.int32),
            pltpu.SMEM((LIST,), jnp.float32),
        ],
        compiler_params=pltpu.CompilerParams(vmem_limit_bytes=40 * 1024 * 1024),
    )(mask, weight, queries, keys_values)


def body(tokens, pairs, confidence, w_query, w_key, w_value, w_out):
    x_here, z_here = lax.axis_index("x"), lax.axis_index("z")
    core_here, sub_here = lax.axis_index("core"), lax.axis_index("sub")

    normed = lax.all_gather(layer_norm(tokens), "sub", axis=1, tiled=True)
    second = pairs[:, 1]
    info = jnp.stack([pairs[:, 0] % IMG, second // IMG, second % IMG, confidence]).astype(jnp.bfloat16)
    info = jnp.pad(info, ((0, INFO - 4), (0, D - PAIR)))

    queries = jnp.dot(normed.reshape(IMG * TOK, D), w_query, preferred_element_type=jnp.float32)
    queries = (queries * HEAD ** (-0.5)).astype(jnp.bfloat16)
    queries = lax.all_gather(jnp.concatenate([queries, info]), "x", axis=0, tiled=False)

    mine = lax.dynamic_slice_in_dim(normed, sub_here * 2, 2, axis=0).reshape(2 * TOK, D)
    block = jnp.concatenate([mine, info])
    groups = [[2 * k + parity for k in range(Z // 2)] for parity in range(2)]
    up = [(i, (i + 1) % Z) for i in range(Z)]
    down = [(i, (i - 1) % Z) for i in range(Z)]
    swap = [(0, 1), (1, 0)]
    same = lax.all_gather(block, "z", axis=0, tiled=False, axis_index_groups=groups)
    half = Z // 4
    other_low = lax.ppermute(same[:half], "z", up)
    other_high = lax.ppermute(same[half:], "z", down)
    same_far = lax.ppermute(same, "core", swap)
    other = jnp.concatenate([other_low, other_high])
    other_far = lax.ppermute(other, "core", swap)
    blocks = jnp.concatenate([same, other, same_far, other_far])

    w_both = jnp.concatenate([w_key, w_value], axis=1)
    keys_values = jnp.einsum("brd,de->bre", blocks, w_both, preferred_element_type=jnp.float32).astype(jnp.bfloat16)

    near = queries[:, IMG * TOK : IMG * TOK + 4, :PAIR].astype(jnp.int32)
    near_a, near_owner, near_b, near_weight = near[:, 0], near[:, 1], near[:, 2], near[:, 3]
    near_x = jnp.arange(X, dtype=jnp.int32)[:, None] * IMG + near_a
    near_z, near_core = (near_owner % (Z * CORE)) // CORE, near_owner % CORE
    near_block = near_z // 2 + (Z // 2) * ((near_z + z_here) % 2) + Z * ((near_core + core_here) % 2)
    near_y = near_block * 2 + near_b % 2
    near_ok = (near_owner // (Z * CORE) == x_here) & (near_b // 2 == sub_here)
    far = blocks[:, 2 * TOK : 2 * TOK + 4, :PAIR].astype(jnp.int32)
    far_a, far_owner, far_b, far_weight = far[:, 0], far[:, 1], far[:, 2], far[:, 3]
    far_x = (far_owner // (Z * CORE)) * IMG + far_b
    far_y = jnp.arange(Z * CORE, dtype=jnp.int32)[:, None] * 2 + far_a % 2
    far_ok = (far_owner % (Z * CORE) == z_here * CORE + core_here) & (far_a // 2 == sub_here)

    side_x = jnp.concatenate([near_x.reshape(-1), far_x.reshape(-1)])
    side_y = jnp.concatenate([near_y.reshape(-1), far_y.reshape(-1)])
    side_w = jnp.concatenate(
        [jnp.where(near_ok, near_weight, 0).reshape(-1), jnp.where(far_ok, far_weight, 0).reshape(-1)]
    )
    hot_x = jnp.where(side_x[None, :] == jnp.arange(NX, dtype=jnp.int32)[:, None], side_w[None, :], 0)
    hot_y = side_y[None, :] == jnp.arange(NY, dtype=jnp.int32)[:, None]
    weight = lax.dot_general(
        hot_y.astype(jnp.bfloat16),
        hot_x.astype(jnp.bfloat16),
        (((1,), (1,)), ((), ())),
        preferred_element_type=jnp.float32,
    )
    bits = jnp.left_shift(jnp.int32(1), jnp.arange(NX, dtype=jnp.int32))
    mask = jnp.sum(jnp.where(weight > 0, bits[None, :], 0), axis=1)

    partial = attend(mask, weight.reshape(-1), queries, keys_values)

    weight_sum = jnp.sum(weight, axis=0).astype(jnp.int32).reshape(X, 1, IMG)
    counts = jnp.concatenate([weight_sum // 128, weight_sum % 128], axis=1).astype(jnp.bfloat16)
    counts = jnp.pad(counts, ((0, 0), (0, INFO - 2), (0, D - IMG)))
    counts = jnp.broadcast_to(counts[:, None], (X, SUB, INFO, D)).reshape(X * SUB, INFO, D)
    sent = jnp.concatenate([partial, counts], axis=1)
    arrived = lax.all_to_all(sent, ("x", "sub"), split_axis=0, concat_axis=0, tiled=True)

    summed = jnp.sum(arrived[:, : IMG * ROWS].astype(jnp.float32), axis=0).reshape(IMG, ROWS, D)
    halves = jnp.sum(arrived[:, IMG * ROWS : IMG * ROWS + 2, :IMG].astype(jnp.float32), axis=0)
    total = (halves[0] * 128.0 + halves[1])[:, None, None]
    divisor = jnp.maximum(total, 1.0)
    projected = jnp.einsum(
        "ird,de->ire", (summed / divisor).astype(jnp.bfloat16), w_out, preferred_element_type=jnp.float32
    )
    return (tokens.astype(jnp.float32) * (total / divisor) + projected).astype(jnp.bfloat16)


def solution(mesh):
    grid = Mesh(mesh.devices.reshape(X, Z, CORE, SUB), ("x", "z", "core", "sub"))
    cam = ("x", "z", "core")
    in_specs = (P(cam, "sub", None), P(cam, None), P(cam), P(), P(), P(), P())
    out_specs = P(cam, "sub", None)
    return jax.shard_map(body, mesh=grid, in_specs=in_specs, out_specs=out_specs, check_vma=False)
```

time: 407 us -> 186 us (0.46)
  waiting for transfers between devices: 211 us -> 16.4 us
  local copies, waits for them, and re-layouts: 42 us -> 10.1 us
  Pallas kernels: 0 us -> 27.1 us
  matrix products: 32.4 us -> 11.7 us
  blocking collectives: 57.9 us -> 76.4 us
  starting transfers between devices: 34.6 us -> 22.3 us
  other arithmetic: 12.9 us -> 7.7 us
    all_to_all x3 -> x0, waiting for transfers between devices: 153 us -> none  [the longest x1 101 us: body(): lax.all_to_all(outgoing, 'cam', split_axis=0, concat_axis=0, tiled=True)]
    all_gather x2 -> x1, waiting for transfers between devices: 58.7 us -> 16.4 us  [body(): lax.all_gather(jnp.concatenate([queries, info]), 'x', axis=0, tiled=False)]
    all_to_all x3 -> x0, starting transfers between devices: 34.3 us -> none  [the longest x1 16.6 us: body(): lax.all_to_all(return_buffer, 'cam', split_axis=0, concat_axis=0, tiled=T...]
    pallas_call x0 -> x1, Pallas kernels: none -> 27.1 us  [attend(): pl.pallas_call(attend_kernel, out_shape=jax.ShapeDtypeStruct((X * SUB, IM...]
    reshape x10 -> x1, local copies, waits for them, and re-layouts: 24.3 us -> 0.08 us  [body(): partial = attend(mask, weight.reshape(-1), queries, keys_values)]
    all_gather x2, blocking collectives: 22.6 us -> 46.4 us  [the longest x1 35.5 us: body(): lax.all_gather(block, 'z', axis=0, tiled=False, axis_index_groups=groups)]
    ppermute x0 -> x4, starting transfers between devices: none -> 22.3 us  [the longest x1 9.29 us: body(): same_far = lax.ppermute(same, 'core', swap)]
    sub x2 -> x0, matrix products: 10.5 us -> none  [attend(): exponent = jnp.exp(scores - row_max)]
  transfers between devices with their start and end apart: 5 -> 5, of which waited for: 4 -> 1; matrix products, arithmetic and copies ran while one was open for 18% -> 8% of each run, Pallas kernels for 0% -> 0%
where the time goes in v1:
time: 186 us; the launch traced here: 185 us
  blocking collectives  76.4 us (41%)
  Pallas kernels  27.1 us (15%)
  starting transfers between devices  22.3 us (12%)
  waiting for transfers between devices  16.4 us (9%)
  between operations  13.7 us (7%)
  matrix products  11.7 us (6%)
  local copies, waits for them, and re-layouts  10.1 us (5%)
  other arithmetic  7.7 us (4%)
    all_gather x1, blocking collectives, body(): lax.all_gather(block, 'z', axis=0, tiled=False, axis_index_groups=groups)  35.5 us
    all_to_all x1, blocking collectives, body(): lax.all_to_all(sent, ('x', 'sub'), split_axis=0, concat_axis=0, tiled=True)  30 us
    pallas_call x1, Pallas kernels, attend(): pl.pallas_call(attend_kernel, out_shape=jax.ShapeDtypeStruct((X * SUB, IM...  27.1 us
    all_gather x1, waiting for transfers between devices, body(): lax.all_gather(jnp.concatenate([queries, info]), 'x', axis=0, tiled=False)  16.4 us
    all_gather x1, blocking collectives, body(): normed = lax.all_gather(layer_norm(tokens), 'sub', axis=1, tiled=True)  11 us
    dot_general x1, matrix products, body(): jnp.einsum('brd,de->bre', blocks, w_both, preferred_element_type=jnp.floa...  9.87 us
    ppermute x1, starting transfers between devices, body(): same_far = lax.ppermute(same, 'core', swap)  9.29 us
    unnamed x17, local copies, waits for them, and re-layouts  7.39 us
  transfers between devices with their start and end apart: 5, of which 1 were waited for; matrix products, arithmetic and copies ran while one was open for 8% of the time, Pallas kernels for 0%

profile of v1, /device:TPU:1, one launch (start us, length us, event | category | flops | bytes accessed | tf_op | source)
XLA Modules:
  0.0 185.4 jit_solution(11384925435052983770)
XLA Ops:
  6.5 0.0 copy-start
  6.5 0.0 all-gather.4.cloned.1.call-start
  6.5 1.1 convert_reduce_fusion.1
  7.6 1.1 fusion.14
  8.7 1.0 fusion.15
  9.7 11.0 %all_gather.15 = bf16[8,32,768]{2,1,0:T(8,128)(2,1)S(1)} all-gather(bf16[8,8,768]{2,1,0:T(8,128)(2,1)S(1)} %fusion.15), channel_id=1, replica_groups=mesh['x'=4,'z'=16,'core'=2,'sub'=4] {'sub'}, dimensions={1}, use_global_device_ids=true | all-gather | bytes 491520 | tf_op jit(solution)/shard_map/all_gather | solution.py:134
  20.7 0.8 fusion.59
  21.5 0.7 convert_bitcast_fusion
  22.2 35.5 %all-gather.1 = bf16[576,768]{1,0:T(8,128)(2,1)S(1)} all-gather(bf16[72,768]{1,0:T(8,128)(2,1)S(1)} %pad_maximum_fusion.3), channel_id=3, replica_groups={{0,16,32,48,64,80,96,112},{8,24,40,56,72,88,104,120},{1,17,33,49,65,81,..., dimensions={0}, use_global_device_ids=true | all-gather | bytes 995328 | tf_op jit(solution)/shard_map/all_gather | solution.py:149
  57.6 0.1 fusion.62
  57.7 3.2 %collective-permute-start = (bf16[4,72,768]{2,1,0:T(8,128)(2,1)S(1)}, bf16[4,72,768]{2,1,0:T(8,128)(2,1)S(1)}, u32[]{:S(2)}, u32[]{:S(2)}) collective-permute-start(bf16[4,72,768]{2,1,0:T(8,128)(2,1)S(1)} %bitcast.55), channel_id=1, source_target_pairs={{0,8},{8,16},{16,24},{24,32},{32,40},{40,48},{48,56},{56,64},{64,7... | collective-permute-start | bytes 1327112 | tf_op jit(solution)/shard_map/ppermute | solution.py:151
  60.9 4.0 %collective-permute-start.1 = (bf16[4,72,768]{2,1,0:T(8,128)(2,1)S(1)}, bf16[4,72,768]{2,1,0:T(8,128)(2,1)S(1)}, u32[]{:S(2)}, u32[]{:S(2)}) collective-permute-start(bf16[4,72,768]{2,1,0:T(8,128)(2,1)S(1)} %bitcast.54), channel_id=1, source_target_pairs={{0,120},{8,0},{16,8},{24,16},{32,24},{40,32},{48,40},{56,48},{64,5... | collective-permute-start | bytes 1327112 | tf_op jit(solution)/shard_map/ppermute | solution.py:152
  64.9 9.3 %collective-permute-start.2 = (bf16[8,72,768]{2,1,0:T(8,128)(2,1)S(1)}, bf16[8,72,768]{2,1,0:T(8,128)(2,1)}, u32[]{:S(2)}, u32[]{:S(2)}) collective-permute-start(bf16[8,72,768]{2,1,0:T(8,128)(2,1)S(1)} %bitcast.50), channel_id=1, source_target_pairs={{0,4},{4,0},{1,5},{5,1},{2,6},{6,2},{3,7},{7,3},{8,12},{12,8},{9,1... | collective-permute-start | bytes 2654216 | tf_op jit(solution)/shard_map/ppermute | solution.py:153
  74.2 0.0 copy-done
  74.2 0.5 fusion.2
  74.7 0.0 collective-permute-done
  74.7 0.0 collective-permute-done.1
  74.8 1.0 pad_maximum_fusion.1
  75.8 5.8 %collective-permute-start.3 = (bf16[8,72,768]{2,1,0:T(8,128)(2,1)}, bf16[8,72,768]{2,1,0:T(8,128)(2,1)}, u32[]{:S(2)}, u32[]{:S(2)}) collective-permute-start(bf16[8,72,768]{2,1,0:T(8,128)(2,1)} %pad_maximum_fusion.1), channel_id=1, source_target_pairs={{0,4},{4,0},{1,5},{5,1},{2,6},{6,2},{3,7},{7,3},{8,12},{12,8},{9,1... | collective-permute-start | bytes 2654216 | tf_op jit(solution)/shard_map/ppermute | solution.py:155
  81.6 0.8 pad_maximum_fusion.2
  82.3 0.0 all-gather.4.cloned.1.call-update
  82.4 0.1 add.211
  82.5 0.1 add.212
  82.5 0.1 add.216
  82.6 0.1 add.217
  82.7 0.1 constant_dynamic-update-slice_fusion.4
  82.8 0.0 collective-permute-done.2
  82.9 1.2 constant_dynamic-update-slice_fusion.1
  84.1 0.0 collective-permute-done.3
  84.1 1.2 constant_dynamic-update-slice_fusion
  85.3 0.0 copy-start.4
  85.4 0.2 slice_reduce_fusion.1
  85.6 1.6 copy-done.4
  87.1 0.1 squeeze.36
  87.2 0.1 squeeze.38
  87.3 0.1 squeeze.39
  87.4 0.1 squeeze.41
  87.5 9.9 %convolution_convert_fusion.kv_ref = bf16[32,72,1536]{2,1,0:T(8,128)(2,1)} fusion(bf16[32,72,768]{2,1,0:T(8,128)(2,1)} %copy-done.4, bf16[768,768]{1,0:T(8,128)(2,1)} %param.12, bf16[768,768]{1,0:T(8,128)(2,1)} %param.11), kind=kOutput, calls=%fused_computation | convolution fusion | flops 5444075520 | bytes 12976128 | tf_op jit(solution)/shard_map/brd,de->bre/dot_general | solution.py:159
  97.3 16.4 %all-gather.4.cloned.1.call-done = bf16[1056,768]{1,0:T(8,128)(2,1)} async-done(((bf16[264,768]{1,0:T(8,128)(2,1)}), bf16[1056,768]{1,0:T(8,128)(2,1)}) %all-gather.4.cloned.1.call-update) | async-done | bytes 1622032 | tf_op jit(solution)/shard_map/all_gather | solution.py:141
  113.7 0.7 slice_convert_fusion.1
  114.5 0.1 squeeze.34
  114.6 0.1 squeeze.35
  114.6 0.1 squeeze.40
  114.7 0.1 squeeze.37
  114.9 0.3 fusion.63
  115.2 0.1 copy.9
  115.3 0.1 reshape.370.weight_ref
  115.3 0.1 select_reduce_fusion.mask_ref
  115.4 0.1 convert_element_type.80
  115.6 0.0 copy-start.1
  115.6 3.0 %copy-done.1 = bf16[32,72,1536]{2,1,0:T(8,128)(2,1)S(1)} copy-done((bf16[32,72,1536]{2,1,0:T(8,128)(2,1)S(1)}, bf16[32,72,1536]{2,1,0:T(8,128)(2,1)}, u32[]{:S(2)}) %copy-start.1) | copy-done | bytes 7077912
  118.6 0.0 copy-start.2
  118.6 1.4 copy-done.2
  120.0 27.1 %shard_map.73 = bf16[16,64,768]{2,1,0:T(8,128)(2,1)S(1)} custom-call(s32[64]{0:T(128)S(1)} %select_reduce_fusion.mask_ref, f32[2048]{0:T(1024)S(1)} %reshape.370.weight_ref, bf16[4,264,768]{2,1,0:T(8,128)(2,1)S(1)} %bitcast.49, bf16[32,72,1536]{2,1,0:T(8,128)(2,1)S(1)} %copy-done.1), custom_call_target="tpu_custom_call" | custom-call | tf_op jit(solution)/shard_map/pallas_call | solution.py:116
  147.1 0.1 pad_maximum_fusion
  147.2 0.0 copy-start.3
  147.2 0.0 copy-start.5
  147.3 30.0 %all_to_all.5 = bf16[16,72,768]{2,1,0:T(8,128)(2,1)S(1)} all-to-all(bf16[16,72,768]{2,1,0:T(8,128)(2,1)S(1)} %pad_maximum_fusion), channel_id=1, replica_groups=mesh['x'=4,'z'=16,'core'=2,'sub'=4] {'x','sub'}, dimensions={0} | all-to-all | bytes 3538944 | tf_op jit(solution)/shard_map/all_to_all | solution.py:197
  177.3 0.2 convert_reduce_fusion
  177.5 0.0 copy-done.3
  177.5 0.0 copy-done.5
  177.5 1.0 fusion.8
  (27 shorter events, 0.3 us)
Async XLA Ops:
  6.5 67.7 %copy-start = (bf16[768,768]{1,0:T(8,128)(2,1)S(1)}, bf16[768,768]{1,0:T(8,128)(2,1)}, u32[]{:S(2)}) copy-start(bf16[768,768]{1,0:T(8,128)(2,1)} %param.10) | copy-start | bytes 3538948
  6.5 107.2 %all-gather.4.cloned.1.call-start = ((), (), s32[]{:S(2)}) async-start(), calls=%async_computation.1 | async-start | bytes 2027520 | tf_op jit(solution)/shard_map/all_gather | solution.py:141
  57.7 17.1 %collective-permute-start = (bf16[4,72,768]{2,1,0:T(8,128)(2,1)S(1)}, bf16[4,72,768]{2,1,0:T(8,128)(2,1)S(1)}, u32[]{:S(2)}, u32[]{:S(2)}) collective-permute-start(bf16[4,72,768]{2,1,0:T(8,128)(2,1)S(1)} %bitcast.55), channel_id=1, source_target_pairs={{0,8},{8,16},{16,24},{24,32},{32,40},{40,48},{48,56},{56,64},{64,7... | collective-permute-start | bytes 1327112 | tf_op jit(solution)/shard_map/ppermute | solution.py:151
  60.9 13.8 %collective-permute-start.1 = (bf16[4,72,768]{2,1,0:T(8,128)(2,1)S(1)}, bf16[4,72,768]{2,1,0:T(8,128)(2,1)S(1)}, u32[]{:S(2)}, u32[]{:S(2)}) collective-permute-start(bf16[4,72,768]{2,1,0:T(8,128)(2,1)S(1)} %bitcast.54), channel_id=1, source_target_pairs={{0,120},{8,0},{16,8},{24,16},{32,24},{40,32},{48,40},{56,48},{64,5... | collective-permute-start | bytes 1327112 | tf_op jit(solution)/shard_map/ppermute | solution.py:152
  64.9 17.9 %collective-permute-start.2 = (bf16[8,72,768]{2,1,0:T(8,128)(2,1)S(1)}, bf16[8,72,768]{2,1,0:T(8,128)(2,1)}, u32[]{:S(2)}, u32[]{:S(2)}) collective-permute-start(bf16[8,72,768]{2,1,0:T(8,128)(2,1)S(1)} %bitcast.50), channel_id=1, source_target_pairs={{0,4},{4,0},{1,5},{5,1},{2,6},{6,2},{3,7},{7,3},{8,12},{12,8},{9,1... | collective-permute-start | bytes 2654216 | tf_op jit(solution)/shard_map/ppermute | solution.py:153
  75.8 8.3 %collective-permute-start.3 = (bf16[8,72,768]{2,1,0:T(8,128)(2,1)}, bf16[8,72,768]{2,1,0:T(8,128)(2,1)}, u32[]{:S(2)}, u32[]{:S(2)}) collective-permute-start(bf16[8,72,768]{2,1,0:T(8,128)(2,1)} %pad_maximum_fusion.1), channel_id=1, source_target_pairs={{0,4},{4,0},{1,5},{5,1},{2,6},{6,2},{3,7},{7,3},{8,12},{12,8},{9,1... | collective-permute-start | bytes 2654216 | tf_op jit(solution)/shard_map/ppermute | solution.py:155
  85.3 1.8 copy-start.4
  115.6 3.0 %copy-start.1 = (bf16[32,72,1536]{2,1,0:T(8,128)(2,1)S(1)}, bf16[32,72,1536]{2,1,0:T(8,128)(2,1)}, u32[]{:S(2)}) copy-start(bf16[32,72,1536]{2,1,0:T(8,128)(2,1)} %convolution_convert_fusion.kv_ref) | copy-start | bytes 21233668
  118.6 1.4 copy-start.2
  147.2 30.3 %copy-start.3 = (bf16[8,8,768]{2,1,0:T(8,128)(2,1)S(1)}, bf16[8,8,768]{2,1,0:T(8,128)(2,1)}, u32[]{:S(2)}) copy-start(bf16[8,8,768]{2,1,0:T(8,128)(2,1)} %param.7) | copy-start | bytes 294916
  147.2 30.3 %copy-start.5 = (bf16[768,768]{1,0:T(8,128)(2,1)S(1)}, bf16[768,768]{1,0:T(8,128)(2,1)}, u32[]{:S(2)}) copy-start(bf16[768,768]{1,0:T(8,128)(2,1)} %param.13) | copy-start | bytes 3538948
Sparse Core Ops, SparseCore 0:
  82.5 31.2 all-gather.3

commit v2 on v1

v2 whole, which is shorter than its diff:
```python
import jax
import jax.numpy as jnp
from jax import lax
from jax.experimental import pallas as pl
from jax.experimental.pallas import tpu as pltpu
from jax.sharding import Mesh, PartitionSpec as P

HEADS = 12
D = 768
TOK = 32
HEAD = D // HEADS
X, Z, CORE, SUB = 4, 16, 2, 4
IMG = 8
PAIR = 32
ROWS = TOK // SUB
NX = X * IMG
NY = Z * CORE * 2
GROUP = 8
INFO = 8
BLOCKS = Z
LIST = NX * 2 * BLOCKS + GROUP


def layer_norm(token_rows):
    numbers = token_rows.astype(jnp.float32)
    average = jnp.mean(numbers, axis=-1, keepdims=True)
    centred = numbers - average
    spread = jnp.mean(centred * centred, axis=-1, keepdims=True)
    return (centred * lax.rsqrt(spread + 1e-06)).astype(jnp.bfloat16)


def norm_kernel(tokens_ref, out_ref):
    out_ref[...] = layer_norm(tokens_ref[...])


def attend_pair(query, keys, values, low_half):
    parts = []
    for j in range(HEADS // 2):
        lanes = slice(2 * HEAD * j, 2 * HEAD * (j + 1))
        two = query[:, lanes]
        spread = jnp.concatenate([jnp.where(low_half, two, 0), jnp.where(low_half, 0, two)], axis=0)
        scores = lax.dot_general(
            spread, keys[:, lanes], (((1,), (1,)), ((), ())), preferred_element_type=jnp.float32
        )
        exponent = jnp.exp(scores - jnp.max(scores, axis=1, keepdims=True))
        total = jnp.sum(exponent, axis=1, keepdims=True)
        probabilities = (exponent * (1.0 / total)).astype(jnp.bfloat16)
        both = jnp.dot(probabilities, values[:, lanes], preferred_element_type=jnp.float32)
        parts.append(jnp.where(low_half, both[:TOK], both[TOK:]))
    return jnp.concatenate(parts, axis=1)


def add_sides(mask_ref, weight_ref, query_refs, kv_ref, acc, sides, scale):
    def list_image(y, count):
        def more(state):
            return state[0] != 0

        def take(state):
            bits, n = state
            x = 31 - lax.clz(bits & -bits)
            sides[n] = y * NX + x
            scale[n] = weight_ref[y * NX + x]
            return bits & (bits - 1), n + 1

        return lax.while_loop(more, take, (mask_ref[y], count))[1]

    count = lax.fori_loop(0, 2 * BLOCKS, list_image, jnp.int32(0))
    for k in range(GROUP):
        sides[count + k] = 0
        scale[count + k] = 0.0
    low_half = lax.broadcasted_iota(jnp.int32, (TOK, 2 * HEAD), 1) < HEAD

    def one_side(n):
        side = sides[n]
        y = side // NX
        x = side % NX
        q_row = pl.multiple_of((x % IMG) * TOK, TOK)
        k_row = pl.multiple_of((y % 2) * TOK, TOK)
        query = query_refs[x // IMG, pl.ds(q_row, TOK), :]
        keys = kv_ref[y // 2, pl.ds(k_row, TOK), 0:D]
        values = kv_ref[y // 2, pl.ds(k_row, TOK), D : 2 * D]
        return x, scale[n] * attend_pair(query, keys, values, low_half)

    def step(g, carry):
        results = [one_side(g * GROUP + k) for k in range(GROUP)]
        for x, mixed in results:
            rows = pl.ds(pl.multiple_of(x * TOK, TOK), TOK)
            acc[rows, :] = acc[rows, :] + mixed
        return carry

    lax.fori_loop(0, (count + GROUP - 1) // GROUP, step, jnp.int32(0))


def first_kernel(mask_ref, weight_ref, q_ref, kv_ref, acc, sides, scale):
    acc[...] = jnp.zeros_like(acc)
    add_sides(mask_ref, weight_ref, q_ref, kv_ref, acc, sides, scale)


def last_kernel(place_ref, mask_ref, weight_ref, q_ref, kv_ref, before_ref, counts_ref, out_ref, acc, sides, scale):
    acc[...] = before_ref[...]
    add_sides(mask_ref, weight_ref, q_ref, kv_ref, acc, sides, scale)
    for xx in range(X):
        place = lax.rem(place_ref[0] + (X - xx), X) * SUB
        for s in range(SUB):
            for i in range(IMG // 2):
                first = (xx * IMG + 2 * i) * TOK + s * ROWS
                block = jnp.concatenate([acc[first : first + ROWS, :], acc[first + TOK : first + TOK + ROWS, :]], axis=0)
                out_ref[place + s, 2 * i * ROWS : 2 * (i + 1) * ROWS, :] = block.astype(jnp.bfloat16)
            out_ref[place + s, IMG * ROWS : IMG * ROWS + INFO, :] = counts_ref[xx]


VMEM = pl.BlockSpec(memory_space=pltpu.VMEM)
SMEM = pl.BlockSpec(memory_space=pltpu.SMEM)
LISTS = [pltpu.SMEM((LIST,), jnp.int32), pltpu.SMEM((LIST,), jnp.float32)]
COST = pl.CostEstimate(flops=2_000_000_000, bytes_accessed=8_000_000, transcendentals=400_000)


def attend_first(mask, weight, queries, keys_values):
    return pl.pallas_call(
        first_kernel,
        out_shape=jax.ShapeDtypeStruct((NX * TOK, D), jnp.float32),
        in_specs=[SMEM, SMEM, VMEM, VMEM],
        out_specs=VMEM,
        scratch_shapes=LISTS,
        cost_estimate=COST,
        compiler_params=pltpu.CompilerParams(vmem_limit_bytes=20 * 1024 * 1024),
    )(mask, weight, queries, keys_values)


def attend_last(place, mask, weight, queries, keys_values, before, counts):
    return pl.pallas_call(
        last_kernel,
        out_shape=jax.ShapeDtypeStruct((X * SUB, IMG * ROWS + INFO, D), jnp.bfloat16),
        in_specs=[SMEM, SMEM, SMEM, VMEM, VMEM, VMEM, VMEM],
        out_specs=VMEM,
        scratch_shapes=[pltpu.VMEM((NX * TOK, D), jnp.float32)] + LISTS,
        cost_estimate=COST,
        compiler_params=pltpu.CompilerParams(vmem_limit_bytes=24 * 1024 * 1024),
    )(place, mask, weight, queries, keys_values, before, counts)


def hot(index, size):
    return index.reshape(1, -1) == jnp.arange(size, dtype=jnp.int32)[:, None]


def outer_sum(side_y, size_y, side_x, side_w):
    left = hot(side_y, size_y).astype(jnp.bfloat16)
    right = jnp.where(hot(side_x, NX), side_w.reshape(1, -1), 0).astype(jnp.bfloat16)
    return lax.dot_general(left, right, (((1,), (1,)), ((), ())), preferred_element_type=jnp.float32)


def body(tokens, pairs, confidence, w_query, w_key, w_value, w_out):
    x_here, z_here = lax.axis_index("x"), lax.axis_index("z")
    core_here, sub_here = lax.axis_index("core"), lax.axis_index("sub")

    normed = pl.pallas_call(norm_kernel, out_shape=jax.ShapeDtypeStruct((IMG * ROWS, D), jnp.bfloat16))(
        tokens.reshape(IMG * ROWS, D)
    )
    normed = lax.all_gather(normed.reshape(IMG, ROWS, D), "sub", axis=1, tiled=True)
    second = pairs[:, 1]
    info = jnp.stack([pairs[:, 0] % IMG, second // IMG, second % IMG, confidence]).astype(jnp.bfloat16)
    info = jnp.pad(info, ((0, INFO - 4), (0, D - PAIR)))

    queries = jnp.dot(normed.reshape(IMG * TOK, D), w_query, preferred_element_type=jnp.float32)
    queries = (queries * HEAD ** (-0.5)).astype(jnp.bfloat16)
    queries = jnp.concatenate([queries, info])
    query_list = [queries] + [lax.ppermute(queries, "x", [(i, (i + d) % X) for i in range(X)]) for d in (1, 2, 3)]

    mine = lax.dynamic_slice_in_dim(normed, sub_here * 2, 2, axis=0).reshape(2 * TOK, D)
    block = jnp.concatenate([mine, info])
    groups = [[2 * k + parity for k in range(Z // 2)] for parity in range(2)]
    up = [(i, (i + 1) % Z) for i in range(Z)]
    down = [(i, (i - 1) % Z) for i in range(Z)]
    swap = [(0, 1), (1, 0)]
    same = lax.all_gather(block, "z", axis=0, tiled=False, axis_index_groups=groups)
    half = Z // 4
    other_low = lax.ppermute(same[:half], "z", up)
    other_high = lax.ppermute(same[half:], "z", down)
    same_far = lax.ppermute(same, "core", swap)
    other = jnp.concatenate([other_low, other_high])
    other_far = lax.ppermute(other, "core", swap)

    w_both = jnp.concatenate([w_key, w_value], axis=1)

    def project(blocks):
        return jnp.einsum("brd,de->bre", blocks, w_both, preferred_element_type=jnp.float32).astype(jnp.bfloat16)

    near_blocks = jnp.concatenate([same, other])
    far_blocks = jnp.concatenate([same_far, other_far])
    queries = jnp.stack(query_list)

    own = queries[:, IMG * TOK : IMG * TOK + 4, :PAIR].astype(jnp.int32)
    own_owner = own[:, 1]
    own_x = jnp.arange(X, dtype=jnp.int32)[:, None] * IMG + own[:, 0]
    own_z, own_core = (own_owner % (Z * CORE)) // CORE, own_owner % CORE
    own_block = own_z // 2 + (Z // 2) * ((own_z + z_here) % 2) + Z * ((own_core + core_here) % 2)
    own_y = own_block * 2 + own[:, 2] % 2
    own_w = jnp.where((own_owner // (Z * CORE) == x_here) & (own[:, 2] // 2 == sub_here), own[:, 3], 0)
    weight_own = outer_sum(own_y, NY, own_x, own_w)

    def weights(blocks, before):
        got = blocks[:, 2 * TOK : 2 * TOK + 4, :PAIR].astype(jnp.int32)
        owner = got[:, 1]
        side_x = ((x_here - owner // (Z * CORE)) % X) * IMG + got[:, 2]
        side_y = jnp.arange(BLOCKS, dtype=jnp.int32)[:, None] * 2 + got[:, 0] % 2
        ok = (owner % (Z * CORE) == z_here * CORE + core_here) & (got[:, 0] // 2 == sub_here)
        weight = before + outer_sum(side_y, 2 * BLOCKS, side_x, jnp.where(ok, got[:, 3], 0))
        bits = jnp.left_shift(jnp.int32(1), jnp.arange(NX, dtype=jnp.int32))
        return weight, jnp.sum(jnp.where(weight > 0, bits[None, :], 0), axis=1)

    near_weight, near_mask = weights(near_blocks, weight_own[: 2 * BLOCKS])
    far_weight, far_mask = weights(far_blocks, weight_own[2 * BLOCKS :])

    before = attend_first(near_mask, near_weight.reshape(-1), queries, project(near_blocks))

    weight_sum = jnp.sum(near_weight + far_weight, axis=0).astype(jnp.int32).reshape(X, 1, IMG)
    counts = jnp.concatenate([weight_sum // 128, weight_sum % 128], axis=1).astype(jnp.bfloat16)
    counts = jnp.pad(counts, ((0, 0), (0, INFO - 2), (0, D - IMG)))
    sent = attend_last(
        x_here.reshape(1).astype(jnp.int32), far_mask, far_weight.reshape(-1), queries, project(far_blocks), before, counts
    )
    arrived = lax.all_to_all(sent, ("x", "sub"), split_axis=0, concat_axis=0, tiled=True)

    summed = jnp.sum(arrived[:, : IMG * ROWS].astype(jnp.float32), axis=0).reshape(IMG, ROWS, D)
    halves = jnp.sum(arrived[:, IMG * ROWS : IMG * ROWS + 2, :IMG].astype(jnp.float32), axis=0)
    total = (halves[0] * 128.0 + halves[1])[:, None, None]
    divisor = jnp.maximum(total, 1.0)
    projected = jnp.einsum(
        "ird,de->ire", (summed / divisor).astype(jnp.bfloat16), w_out, preferred_element_type=jnp.float32
    )
    return (tokens.astype(jnp.float32) * (total / divisor) + projected).astype(jnp.bfloat16)


def solution(mesh):
    grid = Mesh(mesh.devices.reshape(X, Z, CORE, SUB), ("x", "z", "core", "sub"))
    cam = ("x", "z", "core")
    in_specs = (P(cam, "sub", None), P(cam, None), P(cam), P(), P(), P(), P())
    out_specs = P(cam, "sub", None)
    return jax.shard_map(body, mesh=grid, in_specs=in_specs, out_specs=out_specs, check_vma=False)
```

time: 186 us -> 153 us (0.82)
  Pallas kernels: 27.1 us -> 10.5 us
  waiting for transfers between devices: 16.4 us -> 0.02 us
  between operations: 13.7 us -> 0.31 us
  starting transfers between devices: 22.3 us -> 32.5 us
  matrix products: 11.7 us -> 15.6 us
  blocking collectives: 76.4 us -> 74.4 us
    pallas_call x1 -> x3, Pallas kernels: 27.1 us -> 10.5 us  [the longest x1 4.45 us: attend_last(): pl.pallas_call(last_kernel, out_shape=jax.ShapeDtypeStruct((X * SUB, IMG...]
    all_gather x1 -> x0, waiting for transfers between devices: 16.4 us -> none  [body(): lax.all_gather(jnp.concatenate([queries, info]), 'x', axis=0, tiled=False)]
    ppermute x0 -> x3, starting transfers between devices: none -> 11 us  [body(): lax.ppermute(queries, 'x', [(i, (i + d) % X) for i in range(X)])]
    dot_general x2 -> x5, matrix products: 10.2 us -> 14.1 us  [the longest x2 13.7 us: project(): jnp.einsum('brd,de->bre', blocks, w_both, preferred_element_type=jnp.floa...]
    all_to_all x1, blocking collectives: 30 us -> 27 us  [body(): lax.all_to_all(sent, ('x', 'sub'), split_axis=0, concat_axis=0, tiled=True)]
    another operation x3 -> x6, other arithmetic: 0.79 us -> 3.38 us  [the longest x2 2.55 us: body(): queries = jnp.stack(query_list)]
    reduce_sum x3 -> x1, other arithmetic: 2.23 us -> 0.11 us  [body(): jnp.sum(near_weight + far_weight, axis=0).astype(jnp.int32)]
    slice x3 -> x4, local copies, waits for them, and re-layouts: 0.28 us -> 2.37 us  [the longest x1 2.15 us: body(): other_low = lax.ppermute(same[:half], 'z', up)]
  transfers between devices with their start and end apart: 5 -> 7, of which waited for: 1 -> 0; matrix products, arithmetic and copies ran while one was open for 8% -> 10% of each run, Pallas kernels for 0% -> 0%
where the time goes in v2:
time: 153 us; the launch traced here: 152 us
  blocking collectives  74.4 us (49%)
  starting transfers between devices  32.5 us (21%)
  matrix products  15.6 us (10%)
  local copies, waits for them, and re-layouts  11.7 us (8%)
  Pallas kernels  10.5 us (7%)
  other arithmetic  7.35 us (5%)
    all_gather x1, blocking collectives, body(): lax.all_gather(block, 'z', axis=0, tiled=False, axis_index_groups=groups)  36.2 us
    all_to_all x1, blocking collectives, body(): lax.all_to_all(sent, ('x', 'sub'), split_axis=0, concat_axis=0, tiled=True)  27 us
    dot_general x2, matrix products, project(): jnp.einsum('brd,de->bre', blocks, w_both, preferred_element_type=jnp.floa...  13.7 us
    ppermute x1, starting transfers between devices, body(): same_far = lax.ppermute(same, 'core', swap)  11.2 us
    all_gather x1, blocking collectives, body(): lax.all_gather(normed.reshape(IMG, ROWS, D), 'sub', axis=1, tiled=True)  11.2 us
    ppermute x3, starting transfers between devices, body(): lax.ppermute(queries, 'x', [(i, (i + d) % X) for i in range(X)])  11 us
    unnamed x19, local copies, waits for them, and re-layouts  6.45 us
    pallas_call x1, Pallas kernels, attend_last(): pl.pallas_call(last_kernel, out_shape=jax.ShapeDtypeStruct((X * SUB, IMG...  4.45 us
  transfers between devices with their start and end apart: 7, of which 0 were waited for; matrix products, arithmetic and copies ran while one was open for 10% of the time, Pallas kernels for 0%

profile of v2, /device:TPU:1, one launch (start us, length us, event | category | flops | bytes accessed | tf_op | source)
XLA Modules:
  0.0 152.3 jit_solution(12916255835475369947)
XLA Ops:
  0.0 0.8 fusion.82
  0.8 0.7 convert_bitcast_fusion
  1.5 1.7 %shard_map.73 = bf16[64,768]{1,0:T(8,128)(2,1)} custom-call(bf16[64,768]{1,0:T(8,128)(2,1)} %bitcast.65), custom_call_target="tpu_custom_call" | custom-call | tf_op jit(solution)/shard_map/pallas_call | solution.py:156
  3.2 11.2 %all_gather.9 = bf16[8,32,768]{2,1,0:T(8,128)(2,1)S(1)} all-gather(bf16[8,8,768]{2,1,0:T(8,128)(2,1)} %bitcast.64), channel_id=1, replica_groups=mesh['x'=4,'z'=16,'core'=2,'sub'=4] {'sub'}, dimensions={1}, use_global_device_ids=true | all-gather | bytes 491520 | tf_op jit(solution)/shard_map/all_gather | solution.py:159
  14.4 0.5 fusion.5
  14.9 1.0 fusion.88
  15.9 5.4 %collective-permute-start.2 = (bf16[264,768]{1,0:T(8,128)(2,1)}, bf16[264,768]{1,0:T(8,128)(2,1)S(1)}, u32[]{:S(2)}, u32[]{:S(2)}) collective-permute-start(bf16[264,768]{1,0:T(8,128)(2,1)} %get-tuple-element.28), channel_id=1, source_target_pairs={{0,384},{128,0},{256,128},{384,256},{1,385},{129,1},{257,129},{385... | collective-permute-start | bytes 1216520 | tf_op jit(solution)/shard_map/ppermute | solution.py:167
  21.3 1.9 %collective-permute-start = (bf16[264,768]{1,0:T(8,128)(2,1)}, bf16[264,768]{1,0:T(8,128)(2,1)S(1)}, u32[]{:S(2)}, u32[]{:S(2)}) collective-permute-start(bf16[264,768]{1,0:T(8,128)(2,1)} %get-tuple-element.28), channel_id=1, source_target_pairs={{0,128},{128,256},{256,384},{384,0},{1,129},{129,257},{257,385},{3... | collective-permute-start | bytes 1216520 | tf_op jit(solution)/shard_map/ppermute | solution.py:167
  23.2 3.6 %collective-permute-start.1 = (bf16[264,768]{1,0:T(8,128)(2,1)}, bf16[264,768]{1,0:T(8,128)(2,1)S(1)}, u32[]{:S(2)}, u32[]{:S(2)}) collective-permute-start(bf16[264,768]{1,0:T(8,128)(2,1)} %get-tuple-element.28), channel_id=1, source_target_pairs={{0,256},{128,384},{256,0},{384,128},{1,257},{129,385},{257,1},{385... | collective-permute-start | bytes 1216520 | tf_op jit(solution)/shard_map/ppermute | solution.py:167
  26.9 36.2 %all-gather = bf16[576,768]{1,0:T(8,128)(2,1)} all-gather(bf16[72,768]{1,0:T(8,128)(2,1)S(1)} %pad_maximum_fusion.3), channel_id=2, replica_groups={{0,16,32,48,64,80,96,112},{8,24,40,56,72,88,104,120},{1,17,33,49,65,81,..., dimensions={0}, use_global_device_ids=true | all-gather | bytes 995328 | tf_op jit(solution)/shard_map/all_gather | solution.py:175
  63.1 2.1 %fusion.89 = (bf16[288,768]{1,0:T(8,128)(2,1)}, bf16[288,768]{1,0:T(8,128)(2,1)}) fusion(bf16[576,768]{1,0:T(8,128)(2,1)} %all-gather), kind=kLoop, calls=%fused_computation.213 | loop fusion | bytes 1769472 | tf_op jit(solution)/shard_map/slice | solution.py:177
  65.2 3.4 %collective-permute-start.4 = (bf16[4,72,768]{2,1,0:T(8,128)(2,1)}, bf16[4,72,768]{2,1,0:T(8,128)(2,1)S(1)}, u32[]{:S(2)}, u32[]{:S(2)}) collective-permute-start(bf16[4,72,768]{2,1,0:T(8,128)(2,1)} %bitcast.13), channel_id=1, source_target_pairs={{0,8},{8,16},{16,24},{24,32},{32,40},{40,48},{48,56},{56,64},{64,7... | collective-permute-start | bytes 1327112 | tf_op jit(solution)/shard_map/ppermute | solution.py:177
  68.7 3.0 %collective-permute-start.5 = (bf16[4,72,768]{2,1,0:T(8,128)(2,1)}, bf16[4,72,768]{2,1,0:T(8,128)(2,1)}, u32[]{:S(2)}, u32[]{:S(2)}) collective-permute-start(bf16[4,72,768]{2,1,0:T(8,128)(2,1)} %bitcast.14), channel_id=1, source_target_pairs={{0,120},{8,0},{16,8},{24,16},{32,24},{40,32},{48,40},{56,48},{64,5... | collective-permute-start | bytes 1327112 | tf_op jit(solution)/shard_map/ppermute | solution.py:178
  71.7 0.1 add.334
  71.8 0.1 add.335
  71.9 0.1 add.337
  72.0 0.1 add.338
  72.1 0.0 collective-permute-done.2
  72.1 11.2 %collective-permute-start.3 = (bf16[8,72,768]{2,1,0:T(8,128)(2,1)}, bf16[8,72,768]{2,1,0:T(8,128)(2,1)}, u32[]{:S(2)}, u32[]{:S(2)}) collective-permute-start(bf16[8,72,768]{2,1,0:T(8,128)(2,1)} %bitcast.12), channel_id=1, source_target_pairs={{0,4},{4,0},{1,5},{5,1},{2,6},{6,2},{3,7},{7,3},{8,12},{12,8},{9,1... | collective-permute-start | bytes 2654216 | tf_op jit(solution)/shard_map/ppermute | solution.py:179
  83.3 0.0 collective-permute-done
  83.3 0.0 collective-permute-done.1
  83.4 0.7 copy-done.5
  84.1 0.2 copy-done.6
  84.2 1.6 %pad_maximum_fusion.q_ref = bf16[4,264,768]{2,1,0:T(8,128)(2,1)S(1)} fusion(bf16[1,264,768]{2,1,0:T(8,128)(2,1)} %bitcast.60, bf16[1,264,768]{2,1,0:T(8,128)(2,1)} %bitcast.62, bf16[1,264,768]{2,1,0:T(8,128)(2,1)} %bitcast.61, bf16[1,264,768]{2,1,0:T(8,128)(2,1)} %get-tuple-element.27), kind=kLoop, calls=%fused_computation.9 | loop fusion | flops 2433024 | bytes 3244032 | tf_op jit(solution)/shard_map/stack | solution.py:190
  85.9 0.1 squeeze.49
  85.9 0.1 squeeze.50
  86.0 0.1 squeeze.52
  86.1 0.1 squeeze.51
  86.2 0.0 collective-permute-done.4
  86.2 2.0 %pad_maximum_fusion.1 = bf16[8,72,768]{2,1,0:T(8,128)(2,1)} fusion(bf16[4,72,768]{2,1,0:T(8,128)(2,1)} %collective-permute-done.5, bf16[4,72,768]{2,1,0:T(8,128)(2,1)S(1)} %collective-permute-done.4), kind=kLoop, calls=%fused_computation.18 | loop fusion | flops 442368 | bytes 1769472 | tf_op jit(solution)/shard_map/concatenate | solution.py:180
  88.3 3.9 %collective-permute-start.6 = (bf16[8,72,768]{2,1,0:T(8,128)(2,1)}, bf16[8,72,768]{2,1,0:T(8,128)(2,1)}, u32[]{:S(2)}, u32[]{:S(2)}) collective-permute-start(bf16[8,72,768]{2,1,0:T(8,128)(2,1)} %pad_maximum_fusion.1), channel_id=1, source_target_pairs={{0,4},{4,0},{1,5},{5,1},{2,6},{6,2},{3,7},{7,3},{8,12},{12,8},{9,1... | collective-permute-start | bytes 2654216 | tf_op jit(solution)/shard_map/ppermute | solution.py:181
  92.2 0.1 fusion.31
  92.3 0.8 maximum_convert_fusion
  93.0 0.1 slice_reduce_fusion.1
  93.1 0.1 squeeze.57
  93.2 0.1 squeeze.58
  93.3 0.1 squeeze.59
  93.4 0.1 squeeze.60
  93.5 6.7 %convolution_convert_fusion.kv_ref = bf16[16,72,1536]{2,1,0:T(8,128)(2,1)} fusion(bf16[4,72,768]{2,1,0:T(8,128)(2,1)} %collective-permute-done.5, bf16[4,72,768]{2,1,0:T(8,128)(2,1)S(1)} %collective-permute-done.4, bf16[8,72,768]{2,1,0:T(8,128)(2,1)} %bitcast.12, bf16[768,768]{1,0:T(8,128)(2,1)} %param.12, bf16[768,768]{1,0:T(8,128)(2,1)} %param.11), kind=kOutput, calls=%fused_computation | convolution fusion | flops 2726166528 | bytes 7667712 | tf_op jit(solution)/shard_map/brd,de->bre/dot_general | solution.py:186
  100.2 1.2 constant_dynamic-update-slice_fusion.1
  101.4 1.2 constant_dynamic-update-slice_fusion
  102.7 1.3 copy-done.3
  104.0 0.1 slice_reduce_fusion.5
  104.1 0.1 squeeze.53
  104.2 0.1 squeeze.54
  104.2 0.1 squeeze.55
  104.3 0.1 squeeze.56
  104.4 0.1 convolution_add_fusion.1
  104.5 0.2 select_reduce_fusion
  104.7 0.1 add_reduce_fusion
  104.8 0.1 copy.17
  104.9 0.1 copy.15
  105.0 6.9 %convolution_convert_fusion.1.kv_ref = bf16[16,72,1536]{2,1,0:T(8,128)(2,1)} fusion(bf16[16,72,768]{2,1,0:T(8,128)(2,1)} %copy-done.3, bf16[768,768]{1,0:T(8,128)(2,1)} %param.12, bf16[768,768]{1,0:T(8,128)(2,1)} %param.11), kind=kOutput, calls=%fused_computation.1 | convolution fusion | flops 2724397056 | bytes 7667712 | tf_op jit(solution)/shard_map/brd,de->bre/dot_general | solution.py:186
  111.9 0.1 convert_element_type.93
  112.0 0.1 reshape.815.weight_ref
  112.1 0.1 reshape.814.weight_ref
  112.2 2.0 %copy-done.2 = bf16[16,72,1536]{2,1,0:T(8,128)(2,1)S(1)} copy-done((bf16[16,72,1536]{2,1,0:T(8,128)(2,1)S(1)}, bf16[16,72,1536]{2,1,0:T(8,128)(2,1)}, u32[]{:S(2)}) %copy-start.2) | copy-done | bytes 3538968
  114.2 4.3 %shard_map.74.before_ref = f32[1024,768]{1,0:T(8,128)S(1)} custom-call(s32[32]{0:T(128)S(1)} %get-tuple-element.17.mask_ref, f32[1024]{0:T(1024)S(1)} %reshape.815.weight_ref, bf16[4,264,768]{2,1,0:T(8,128)(2,1)S(1)} %pad_maximum_fusion.q_ref, bf16[16,72,1536]{2,1,0:T(8,128)(2,1)S(1)} %copy-done.2), custom_call_target="tpu_custom_call" | custom-call | flops 2000000000 | bytes 8000000 | tf_op jit(solution)/shard_map/pallas_call | solution.py:119
  118.5 4.5 %shard_map.75 = bf16[16,72,768]{2,1,0:T(8,128)(2,1)S(1)} custom-call(s32[1]{0:T(128)} %bitcast.place_ref, s32[32]{0:T(128)S(1)} %get-tuple-element.18.mask_ref, f32[1024]{0:T(1024)S(1)} %reshape.814.weight_ref, bf16[4,264,768]{2,1,0:T(8,128)(2,1)S(1)} %pad_maximum_fusion.q_ref, bf16[16,72,1536]{2,1,0:T(8,128)(2,1)S(1)} %copy-done.1, ...), custom_call_target="tpu_custom_call" | custom-call | flops 2000000000 | bytes 8000000 | tf_op jit(solution)/shard_map/pallas_call | solution.py:131
  122.9 27.0 %all_to_all.5 = bf16[16,72,768]{2,1,0:T(8,128)(2,1)S(1)} all-to-all(bf16[16,72,768]{2,1,0:T(8,128)(2,1)S(1)} %shard_map.75), channel_id=1, replica_groups=mesh['x'=4,'z'=16,'core'=2,'sub'=4] {'x','sub'}, dimensions={0} | all-to-all | bytes 3538944 | tf_op jit(solution)/shard_map/all_to_all | solution.py:222
  150.0 0.2 convert_reduce_fusion
  150.2 0.6 copy-done.7
  150.8 0.4 copy-done.8
  151.3 1.0 fusion.11
  (35 shorter events, 0.3 us)
Async XLA Ops:
  0.0 14.4 %copy-start = (bf16[768,768]{1,0:T(8,128)(2,1)S(1)}, bf16[768,768]{1,0:T(8,128)(2,1)}, u32[]{:S(2)}) copy-start(bf16[768,768]{1,0:T(8,128)(2,1)} %param.10) | copy-start | bytes 3538948
  15.9 56.2 %collective-permute-start.2 = (bf16[264,768]{1,0:T(8,128)(2,1)}, bf16[264,768]{1,0:T(8,128)(2,1)S(1)}, u32[]{:S(2)}, u32[]{:S(2)}) collective-permute-start(bf16[264,768]{1,0:T(8,128)(2,1)} %get-tuple-element.28), channel_id=1, source_target_pairs={{0,384},{128,0},{256,128},{384,256},{1,385},{129,1},{257,129},{385... | collective-permute-start | bytes 1216520 | tf_op jit(solution)/shard_map/ppermute | solution.py:167
  21.3 62.0 %collective-permute-start = (bf16[264,768]{1,0:T(8,128)(2,1)}, bf16[264,768]{1,0:T(8,128)(2,1)S(1)}, u32[]{:S(2)}, u32[]{:S(2)}) collective-permute-start(bf16[264,768]{1,0:T(8,128)(2,1)} %get-tuple-element.28), channel_id=1, source_target_pairs={{0,128},{128,256},{256,384},{384,0},{1,129},{129,257},{257,385},{3... | collective-permute-start | bytes 1216520 | tf_op jit(solution)/shard_map/ppermute | solution.py:167
  23.2 60.1 %collective-permute-start.1 = (bf16[264,768]{1,0:T(8,128)(2,1)}, bf16[264,768]{1,0:T(8,128)(2,1)S(1)}, u32[]{:S(2)}, u32[]{:S(2)}) collective-permute-start(bf16[264,768]{1,0:T(8,128)(2,1)} %get-tuple-element.28), channel_id=1, source_target_pairs={{0,256},{128,384},{256,0},{384,128},{1,257},{129,385},{257,1},{385... | collective-permute-start | bytes 1216520 | tf_op jit(solution)/shard_map/ppermute | solution.py:167
  65.2 21.0 %collective-permute-start.4 = (bf16[4,72,768]{2,1,0:T(8,128)(2,1)}, bf16[4,72,768]{2,1,0:T(8,128)(2,1)S(1)}, u32[]{:S(2)}, u32[]{:S(2)}) collective-permute-start(bf16[4,72,768]{2,1,0:T(8,128)(2,1)} %bitcast.13), channel_id=1, source_target_pairs={{0,8},{8,16},{16,24},{24,32},{32,40},{40,48},{48,56},{56,64},{64,7... | collective-permute-start | bytes 1327112 | tf_op jit(solution)/shard_map/ppermute | solution.py:177
  68.7 17.6 %collective-permute-start.5 = (bf16[4,72,768]{2,1,0:T(8,128)(2,1)}, bf16[4,72,768]{2,1,0:T(8,128)(2,1)}, u32[]{:S(2)}, u32[]{:S(2)}) collective-permute-start(bf16[4,72,768]{2,1,0:T(8,128)(2,1)} %bitcast.14), channel_id=1, source_target_pairs={{0,120},{8,0},{16,8},{24,16},{32,24},{40,32},{48,40},{56,48},{64,5... | collective-permute-start | bytes 1327112 | tf_op jit(solution)/shard_map/ppermute | solution.py:178
  72.1 11.3 %copy-start.4 = (bf16[264,768]{1,0:T(8,128)(2,1)}, bf16[264,768]{1,0:T(8,128)(2,1)S(1)}, u32[]{:S(2)}) copy-start(bf16[264,768]{1,0:T(8,128)(2,1)S(1)} %collective-permute-done.2) | copy-start | bytes 1216516
  72.1 28.1 %collective-permute-start.3 = (bf16[8,72,768]{2,1,0:T(8,128)(2,1)}, bf16[8,72,768]{2,1,0:T(8,128)(2,1)}, u32[]{:S(2)}, u32[]{:S(2)}) collective-permute-start(bf16[8,72,768]{2,1,0:T(8,128)(2,1)} %bitcast.12), channel_id=1, source_target_pairs={{0,4},{4,0},{1,5},{5,1},{2,6},{6,2},{3,7},{7,3},{8,12},{12,8},{9,1... | collective-permute-start | bytes 2654216 | tf_op jit(solution)/shard_map/ppermute | solution.py:179
  83.3 0.8 copy-start.5
  83.3 0.9 copy-start.6
  88.3 13.1 %collective-permute-start.6 = (bf16[8,72,768]{2,1,0:T(8,128)(2,1)}, bf16[8,72,768]{2,1,0:T(8,128)(2,1)}, u32[]{:S(2)}, u32[]{:S(2)}) collective-permute-start(bf16[8,72,768]{2,1,0:T(8,128)(2,1)} %pad_maximum_fusion.1), channel_id=1, source_target_pairs={{0,4},{4,0},{1,5},{5,1},{2,6},{6,2},{3,7},{7,3},{8,12},{12,8},{9,1... | collective-permute-start | bytes 2654216 | tf_op jit(solution)/shard_map/ppermute | solution.py:181
  102.7 1.3 copy-start.3
  112.2 2.0 %copy-start.2 = (bf16[16,72,1536]{2,1,0:T(8,128)(2,1)S(1)}, bf16[16,72,1536]{2,1,0:T(8,128)(2,1)}, u32[]{:S(2)}) copy-start(bf16[16,72,1536]{2,1,0:T(8,128)(2,1)} %convolution_convert_fusion.kv_ref) | copy-start | bytes 10616836
  114.2 4.3 %copy-start.1 = (bf16[16,72,1536]{2,1,0:T(8,128)(2,1)S(1)}, bf16[16,72,1536]{2,1,0:T(8,128)(2,1)}, u32[]{:S(2)}) copy-start(bf16[16,72,1536]{2,1,0:T(8,128)(2,1)} %convolution_convert_fusion.1.kv_ref) | copy-start | bytes 10616836
  150.0 0.9 copy-start.7
  150.0 1.3 copy-start.8

commit v3 on v2

v3 whole, which is shorter than its diff:
```python
import jax
import jax.numpy as jnp
from jax import lax
from jax.experimental import pallas as pl
from jax.experimental.pallas import tpu as pltpu
from jax.sharding import Mesh, PartitionSpec as P

HEADS = 12
D = 768
TOK = 32
HEAD = D // HEADS
X, Z, CORE, SUB = 4, 16, 2, 4
IMG = 8
PAIR = 32
ROWS = TOK // SUB
OWN = IMG * ROWS
NX = X * IMG
BLOCKS = Z * CORE
NY = 2 * BLOCKS
GROUP = 8
TILE = 8
INFO = 8
LIST = NX * NY + GROUP
LANES = 128
VMEM = pl.BlockSpec(memory_space=pltpu.VMEM)
SMEM = pl.BlockSpec(memory_space=pltpu.SMEM)
INT = jnp.int32


def iota(rows, axis):
    return lax.broadcasted_iota(INT, (rows, LANES), axis)


def norm_kernel(tokens_ref, pairs_ref, weight_ref, normed_ref, info_ref, rows):
    numbers = tokens_ref[...].astype(jnp.float32)
    centred = numbers - jnp.mean(numbers, axis=-1, keepdims=True)
    spread = jnp.mean(centred * centred, axis=-1, keepdims=True)
    normed_ref[...] = (centred * lax.rsqrt(spread + 1e-06)).astype(jnp.bfloat16)
    rows[...] = jnp.zeros_like(rows)
    second = pairs_ref[1:2, :]
    rows[0:1, 0:PAIR] = (pairs_ref[0:1, :] & (IMG - 1)).astype(jnp.float32)
    rows[1:2, 0:PAIR] = (second // IMG).astype(jnp.float32)
    rows[2:3, 0:PAIR] = (second & (IMG - 1)).astype(jnp.float32)
    rows[3:4, 0:PAIR] = weight_ref[...].astype(jnp.float32)
    info_ref[...] = rows[...].astype(jnp.bfloat16)


def query_kernel(place_ref, normed_ref, info_ref, w_ref, queries_ref, block_ref):
    queries = jnp.dot(normed_ref[...], w_ref[...], preferred_element_type=jnp.float32)
    queries_ref[0 : IMG * TOK, :] = (queries * HEAD ** (-0.5)).astype(jnp.bfloat16)
    queries_ref[IMG * TOK : IMG * TOK + INFO, :] = info_ref[...]
    first = pl.multiple_of(place_ref[3] * (2 * TOK), 2 * TOK)
    block_ref[0 : 2 * TOK, :] = normed_ref[pl.ds(first, 2 * TOK), :]
    block_ref[2 * TOK : 2 * TOK + INFO, :] = info_ref[...]


def side_weights(place_ref, query_refs, pieces, fields):
    x_here, z_here, core_here, sub_here = (place_ref[k] for k in range(4))
    left, right = [], []
    for d, ref in enumerate(query_refs):
        info = ref[IMG * TOK : IMG * TOK + INFO, 0:LANES].astype(jnp.float32).astype(INT)
        a, owner, b, weight = (info[f : f + 1, :] for f in range(4))
        there = (owner & (BLOCKS - 1)) >> 1
        block = (there >> 1) + (Z // 2) * ((there ^ z_here) & 1) + Z * ((owner & 1) ^ core_here)
        weight = jnp.where(((owner >> 5) == x_here) & ((b >> 1) == sub_here), weight, 0).astype(jnp.float32)
        left.append(jnp.where(iota(BLOCKS, 0) == block, 1.0, 0.0))
        right.append(jnp.where(iota(LANES, 0) == (b & 1) * NX + d * IMG + a, weight, 0.0))
    total = lax.dot_general(
        jnp.concatenate(left, axis=1).astype(jnp.bfloat16),
        jnp.concatenate(right, axis=1).astype(jnp.bfloat16),
        (((1,), (1,)), ((), ())),
        preferred_element_type=jnp.float32,
    )
    block = 0
    for ref in pieces:
        for j in range(ref.shape[0]):
            fields[block * INFO : (block + 1) * INFO, :] = ref[j, 2 * TOK : 2 * TOK + INFO, 0:LANES].astype(jnp.float32)
            block += 1
    a, owner, b, weight = (fields[pl.ds(f, BLOCKS, stride=INFO), :].astype(INT) for f in range(4))
    ok = ((owner & (BLOCKS - 1)) == z_here * CORE + core_here) & ((a >> 1) == sub_here)
    weight = jnp.where(ok, weight, 0).astype(jnp.float32)
    code = (a & 1) * NX + ((x_here - (owner >> 5)) & (X - 1)) * IMG + b
    lane = iota(BLOCKS, 1)
    for c in range(2 * NX):
        column = jnp.sum(jnp.where(code == c, weight, 0.0), axis=1, keepdims=True)
        total = total + jnp.where(lane == c, column, 0.0)
    return total


def attend_pair(query, keys, values, low_half):
    parts = []
    for j in range(HEADS // 2):
        lanes = slice(2 * HEAD * j, 2 * HEAD * (j + 1))
        two = query[:, lanes]
        spread = jnp.concatenate([jnp.where(low_half, two, 0), jnp.where(low_half, 0, two)], axis=0)
        scores = lax.dot_general(
            spread, keys[:, lanes], (((1,), (1,)), ((), ())), preferred_element_type=jnp.float32
        )
        exponent = jnp.exp(scores - jnp.max(scores, axis=1, keepdims=True))
        total = jnp.sum(exponent, axis=1, keepdims=True)
        probabilities = (exponent * (1.0 / total)).astype(jnp.bfloat16)
        both = jnp.dot(probabilities, values[:, lanes], preferred_element_type=jnp.float32)
        parts.append(jnp.where(low_half, both[:TOK], both[TOK:]))
    return jnp.concatenate(parts, axis=1)


def attend_kernel(place_ref, *refs):
    query_refs, pieces, (w_key_ref, w_value_ref, out_ref) = refs[:X], refs[X : X + 4], refs[X + 4 : X + 7]
    all_queries, acc, rows, keys_values, fields, table, listed, sides, scale, count, sem = refs[X + 7 :]
    total = side_weights(place_ref, query_refs, pieces, fields)
    lane = iota(BLOCKS, 1)
    bits = jnp.where(total > 0, jnp.left_shift(1, lane & 15).astype(jnp.float32), 0.0)
    masks = jnp.zeros_like(total)
    for g in range(4):
        part = jnp.sum(jnp.where((lane >> 4) == g, bits, 0.0), axis=1, keepdims=True)
        masks = masks + jnp.where(lane == 2 * NX + g, part, 0.0)
    table[...] = (total + masks).astype(INT)
    copy = pltpu.make_async_copy(table, listed, sem)
    copy.start()

    sums = jnp.sum(total, axis=0, keepdims=True)
    sums = (sums + pltpu.roll(sums, LANES - NX, 1)).astype(INT)
    halves = jnp.concatenate([sums >> 7, sums & 127, jnp.zeros((INFO - 2, LANES), INT)], axis=0).astype(jnp.float32)
    for d in range(X):
        shifted = pltpu.roll(halves, (LANES - d * IMG) % LANES, 1)
        place = ((place_ref[0] + (X - d)) & (X - 1)) * SUB
        wide = jnp.concatenate([shifted, jnp.zeros((INFO, D - LANES), jnp.float32)], axis=1).astype(jnp.bfloat16)
        for s in range(SUB):
            out_ref[place + s, OWN : OWN + INFO, :] = wide

    acc[...] = jnp.zeros_like(acc)
    for d, ref in enumerate(query_refs):
        all_queries[d * IMG * TOK : (d + 1) * IMG * TOK, :] = ref[0 : IMG * TOK, :]
    count[0] = 0
    count[1] = 0
    copy.wait()

    first_block = 0
    for ref in pieces:

        def look(j, carry, ref=ref, first_block=first_block):
            block = first_block + j
            for k in range(2):
                mask = listed[block, 2 * NX + 2 * k] | (listed[block, 2 * NX + 2 * k + 1] << 16)

                @pl.when(mask != 0)
                def _():
                    slot = count[0]
                    count[0] = slot + 1
                    rows[pl.ds(pl.multiple_of(slot * TOK, TOK), TOK), :] = ref[j, k * TOK : (k + 1) * TOK, :]

                    def more(state):
                        return state[0] != 0

                    def take(state):
                        left, n = state
                        x = 31 - lax.clz(left & -left)
                        sides[n] = slot * NX + x
                        scale[n] = listed[block, k * NX + x].astype(jnp.float32)
                        return left & (left - 1), n + 1

                    count[1] = lax.while_loop(more, take, (mask, count[1]))[1]

            return carry

        lax.fori_loop(0, ref.shape[0], look, 0)
        first_block += ref.shape[0]
    found = count[1]
    for k in range(GROUP):
        sides[found + k] = 0
        scale[found + k] = 0.0

    def project(t, carry):
        some = pl.ds(pl.multiple_of(t * (TILE * TOK), TILE * TOK), TILE * TOK)
        normed = rows[some, :]
        keys_values[some, 0:D] = jnp.dot(normed, w_key_ref[...], preferred_element_type=jnp.float32).astype(jnp.bfloat16)
        keys_values[some, D : 2 * D] = jnp.dot(normed, w_value_ref[...], preferred_element_type=jnp.float32).astype(
            jnp.bfloat16
        )
        return carry

    lax.fori_loop(0, (count[0] + TILE - 1) // TILE, project, 0)
    low_half = lax.broadcasted_iota(INT, (TOK, 2 * HEAD), 1) < HEAD

    def one_side(n):
        side = sides[n]
        slot = pl.ds(pl.multiple_of((side // NX) * TOK, TOK), TOK)
        mine = pl.ds(pl.multiple_of((side % NX) * TOK, TOK), TOK)
        mixed = attend_pair(all_queries[mine, :], keys_values[slot, 0:D], keys_values[slot, D : 2 * D], low_half)
        return mine, scale[n] * mixed

    def step(g, carry):
        results = [one_side(g * GROUP + k) for k in range(GROUP)]
        for mine, mixed in results:
            acc[mine, :] = acc[mine, :] + mixed
        return carry

    lax.fori_loop(0, (found + GROUP - 1) // GROUP, step, 0)

    for d in range(X):
        place = ((place_ref[0] + (X - d)) & (X - 1)) * SUB
        for s in range(SUB):
            for i in range(IMG // 2):
                first = (d * IMG + 2 * i) * TOK + s * ROWS
                block = jnp.concatenate([acc[first : first + ROWS, :], acc[first + TOK : first + TOK + ROWS, :]], axis=0)
                out_ref[place + s, 2 * i * ROWS : 2 * (i + 1) * ROWS, :] = block.astype(jnp.bfloat16)


def attend(place, queries, pieces, w_key, w_value):
    return pl.pallas_call(
        attend_kernel,
        out_shape=jax.ShapeDtypeStruct((X * SUB, OWN + INFO, D), jnp.bfloat16),
        in_specs=[SMEM] + [VMEM] * (len(queries) + len(pieces) + 2),
        out_specs=VMEM,
        scratch_shapes=[
            pltpu.VMEM((NX * TOK, D), jnp.bfloat16),
            pltpu.VMEM((NX * TOK, D), jnp.float32),
            pltpu.VMEM((NY * TOK, D), jnp.bfloat16),
            pltpu.VMEM((NY * TOK, 2 * D), jnp.bfloat16),
            pltpu.VMEM((BLOCKS * INFO, LANES), jnp.float32),
            pltpu.VMEM((BLOCKS, LANES), INT),
            pltpu.SMEM((BLOCKS, LANES), INT),
            pltpu.SMEM((LIST,), INT),
            pltpu.SMEM((LIST,), jnp.float32),
            pltpu.SMEM((2,), INT),
            pltpu.SemaphoreType.DMA,
        ],
        cost_estimate=pl.CostEstimate(flops=4_000_000_000, bytes_accessed=10_000_000, transcendentals=800_000),
        compiler_params=pltpu.CompilerParams(vmem_limit_bytes=36 * 1024 * 1024),
    )(place, *queries, *pieces, w_key, w_value)


def finish_kernel(arrived_ref, tokens_ref, w_ref, out_ref):
    summed = arrived_ref[0, 0:OWN, :].astype(jnp.float32)
    halves = arrived_ref[0, OWN : OWN + INFO, 0:LANES].astype(jnp.float32)
    for k in range(1, X * SUB):
        summed = summed + arrived_ref[k, 0:OWN, :].astype(jnp.float32)
        halves = halves + arrived_ref[k, OWN : OWN + INFO, 0:LANES].astype(jnp.float32)
    totals = halves[0:1, :] * 128.0 + halves[1:2, :]
    inverse = 1.0 / jnp.maximum(totals, 1.0)
    keep = totals * inverse
    scaled, kept = [], []
    for i in range(IMG):
        rows = slice(i * ROWS, (i + 1) * ROWS)
        scaled.append(summed[rows] * inverse[0:1, i : i + 1])
        kept.append(tokens_ref[rows, :].astype(jnp.float32) * keep[0:1, i : i + 1])
    mixed = jnp.concatenate(scaled, axis=0).astype(jnp.bfloat16)
    projected = jnp.dot(mixed, w_ref[...], preferred_element_type=jnp.float32)
    out_ref[...] = (jnp.concatenate(kept, axis=0) + projected).astype(jnp.bfloat16)


def body(tokens, pairs, confidence, w_query, w_key, w_value, w_out):
    place = jnp.stack([lax.axis_index(name) for name in ("x", "z", "core", "sub")]).astype(INT)
    tokens = tokens.reshape(OWN, D)
    normed, info = pl.pallas_call(
        norm_kernel,
        out_shape=[jax.ShapeDtypeStruct((OWN, D), jnp.bfloat16), jax.ShapeDtypeStruct((INFO, D), jnp.bfloat16)],
        scratch_shapes=[pltpu.VMEM((INFO, D), jnp.float32)],
    )(tokens, pairs.T, confidence.reshape(1, PAIR))
    normed = lax.all_gather(normed.reshape(IMG, ROWS, D), "sub", axis=1, tiled=True).reshape(IMG * TOK, D)
    queries, block = pl.pallas_call(
        query_kernel,
        in_specs=[SMEM, VMEM, VMEM, VMEM],
        out_shape=[
            jax.ShapeDtypeStruct((IMG * TOK + INFO, D), jnp.bfloat16),
            jax.ShapeDtypeStruct((2 * TOK + INFO, D), jnp.bfloat16),
        ],
        compiler_params=pltpu.CompilerParams(vmem_limit_bytes=16 * 1024 * 1024),
    )(place, normed, info, w_query)
    queries = [queries] + [lax.ppermute(queries, "x", [(i, (i + d) % X) for i in range(X)]) for d in (1, 2, 3)]

    groups = [[2 * k + parity for k in range(Z // 2)] for parity in range(2)]
    same = lax.all_gather(block, "z", axis=0, tiled=False, axis_index_groups=groups)
    same, *queries = lax.optimization_barrier((same, *queries))
    there = [(z * CORE + c, (z + 1 - 2 * c) % Z * CORE + c) for z in range(Z) for c in range(CORE)]
    other = lax.ppermute(same, ("z", "core"), there)
    pieces = [same, other] + [lax.ppermute(piece, "core", [(0, 1), (1, 0)]) for piece in (same, other)]
    sent = attend(place, queries, pieces, w_key, w_value)
    arrived = lax.all_to_all(sent, ("x", "sub"), split_axis=0, concat_axis=0, tiled=True)
    decoded = pl.pallas_call(
        finish_kernel,
        out_shape=jax.ShapeDtypeStruct((OWN, D), jnp.bfloat16),
        compiler_params=pltpu.CompilerParams(vmem_limit_bytes=16 * 1024 * 1024),
    )(arrived, tokens, w_out)
    return decoded.reshape(IMG, ROWS, D)


def solution(mesh):
    grid = Mesh(mesh.devices.reshape(X, Z, CORE, SUB), ("x", "z", "core", "sub"))
    cam = ("x", "z", "core")
    in_specs = (P(cam, "sub", None), P(cam, None), P(cam), P(), P(), P(), P())
    out_specs = P(cam, "sub", None)
    return jax.shard_map(body, mesh=grid, in_specs=in_specs, out_specs=out_specs, check_vma=False)
```

time: 153 us -> 132 us (0.86)
  matrix products: 15.6 us -> 0 us
  local copies, waits for them, and re-layouts: 11.7 us -> 2 us
  other arithmetic: 7.35 us -> 0.08 us
  waiting for transfers between devices: 0.02 us -> 3.62 us
  Pallas kernels: 10.5 us -> 14 us
  blocking collectives: 74.4 us -> 77.1 us
  starting transfers between devices: 32.5 us -> 35 us
    dot_general x7 -> x0, matrix products: 15.6 us -> none  [the longest x2 13.7 us: project(): jnp.einsum('brd,de->bre', blocks, w_both, preferred_element_type=jnp.floa...]
    unnamed x19 -> x12, local copies, waits for them, and re-layouts: 6.45 us -> 2 us
    all_to_all x1, blocking collectives: 27 us -> 31 us  [body(): lax.all_to_all(sent, ('x', 'sub'), split_axis=0, concat_axis=0, tiled=True)]
    another operation x8 -> x1, other arithmetic: 4.06 us -> 0.08 us  [body(): jnp.stack([lax.axis_index(name) for name in ('x', 'z', 'core', 'sub')])]
    ppermute x4 -> x3, waiting for transfers between devices: 0.01 us -> 3.61 us  [the longest x2 2.02 us: body(): lax.ppermute(piece, 'core', [(0, 1), (1, 0)])]
    pallas_call x3 -> x4, Pallas kernels: 10.5 us -> 14 us  [the longest x1 10.1 us: attend(): pl.pallas_call(attend_kernel, out_shape=jax.ShapeDtypeStruct((X * SUB, OW...]
    ppermute x4 -> x3, starting transfers between devices: 21.6 us -> 24.6 us  [the longest x2 21.1 us: body(): lax.ppermute(piece, 'core', [(0, 1), (1, 0)])]
    slice x4 -> x0, local copies, waits for them, and re-layouts: 2.37 us -> none  [the longest x1 2.15 us: body(): other_low = lax.ppermute(same[:half], 'z', up)]
  transfers between devices with their start and end apart: 7 -> 6, of which waited for: 0 -> 2; matrix products, arithmetic and copies ran while one was open for 10% -> 0% of each run, Pallas kernels for 0% -> 0%
where the time goes in v3:
time: 132 us
  blocking collectives  77.1 us (58%)
  starting transfers between devices  35 us (27%)
  Pallas kernels  14 us (11%)
  waiting for transfers between devices  3.62 us (3%)
  local copies, waits for them, and re-layouts  2 us (2%)
    all_gather x1, blocking collectives, body(): lax.all_gather(block, 'z', axis=0, tiled=False, axis_index_groups=groups)  34.9 us
    all_to_all x1, blocking collectives, body(): lax.all_to_all(sent, ('x', 'sub'), split_axis=0, concat_axis=0, tiled=True)  31 us
    ppermute x2, starting transfers between devices, body(): lax.ppermute(piece, 'core', [(0, 1), (1, 0)])  21.1 us
    all_gather x1, blocking collectives, body(): lax.all_gather(normed.reshape(IMG, ROWS, D), 'sub', axis=1, tiled=True)  11.2 us
    ppermute x3, starting transfers between devices, body(): lax.ppermute(queries, 'x', [(i, (i + d) % X) for i in range(X)])  10.4 us
    pallas_call x1, Pallas kernels, attend(): pl.pallas_call(attend_kernel, out_shape=jax.ShapeDtypeStruct((X * SUB, OW...  10.1 us
    ppermute x1, starting transfers between devices, body(): other = lax.ppermute(same, ('z', 'core'), there)  3.46 us
  transfers between devices with their start and end apart: 6, of which 2 were waited for; matrix products, arithmetic and copies ran while one was open for 0% of the time, Pallas kernels for 0%

profile of v3, /device:TPU:1, one launch (start us, length us, event | category | flops | bytes accessed | tf_op | source)
XLA Modules:
  0.0 131.9 jit_solution(1485578255246884898)
XLA Ops:
  0.0 1.7 %shard_map.73 = (bf16[64,768]{1,0:T(8,128)(2,1)}, bf16[8,768]{1,0:T(8,128)(2,1)}) custom-call(bf16[64,768]{1,0:T(8,128)(2,1)} %bitcast.15, s32[2,32]{1,0:T(2,128)} %bitcast.18, s32[1,32]{1,0:T(1,128)} %bitcast.19), custom_call_target="tpu_custom_call" | custom-call | tf_op jit(solution)/shard_map/pallas_call | solution.py:255
  1.7 11.2 %all_gather.9 = bf16[8,32,768]{2,1,0:T(8,128)(2,1)S(1)} all-gather(bf16[8,8,768]{2,1,0:T(8,128)(2,1)} %bitcast.17), channel_id=1, replica_groups=mesh['x'=4,'z'=16,'core'=2,'sub'=4] {'sub'}, dimensions={1}, use_global_device_ids=true | all-gather | bytes 491520 | tf_op jit(solution)/shard_map/all_gather | solution.py:260
  12.9 0.1 pad_add_fusion.place_ref
  13.0 0.0 copy-start.1
  13.0 1.3 copy-done.1
  14.3 0.0 copy-start.3
  14.3 0.7 copy-done.3
  15.0 0.0 copy-start.4
  15.0 0.0 copy-start.5
  15.0 1.0 shard_map.74
  16.0 5.4 %collective-permute-start.2 = (bf16[264,768]{1,0:T(8,128)(2,1)S(1)}, bf16[264,768]{1,0:T(8,128)(2,1)S(1)}, u32[]{:S(2)}, u32[]{:S(2)}) collective-permute-start(bf16[264,768]{1,0:T(8,128)(2,1)S(1)} %get-tuple-element.18.refs_0_), channel_id=1, source_target_pairs={{0,384},{128,0},{256,128},{384,256},{1,385},{129,1},{257,129},{385... | collective-permute-start | bytes 1216520 | tf_op jit(solution)/shard_map/ppermute | solution.py:270
  21.5 2.4 %collective-permute-start.1 = (bf16[264,768]{1,0:T(8,128)(2,1)S(1)}, bf16[264,768]{1,0:T(8,128)(2,1)S(1)}, u32[]{:S(2)}, u32[]{:S(2)}) collective-permute-start(bf16[264,768]{1,0:T(8,128)(2,1)S(1)} %get-tuple-element.18.refs_0_), channel_id=1, source_target_pairs={{0,256},{128,384},{256,0},{384,128},{1,257},{129,385},{257,1},{385... | collective-permute-start | bytes 1216520 | tf_op jit(solution)/shard_map/ppermute | solution.py:270
  23.9 2.5 %collective-permute-start = (bf16[264,768]{1,0:T(8,128)(2,1)S(1)}, bf16[264,768]{1,0:T(8,128)(2,1)S(1)}, u32[]{:S(2)}, u32[]{:S(2)}) collective-permute-start(bf16[264,768]{1,0:T(8,128)(2,1)S(1)} %get-tuple-element.18.refs_0_), channel_id=1, source_target_pairs={{0,128},{128,256},{256,384},{384,0},{1,129},{129,257},{257,385},{3... | collective-permute-start | bytes 1216520 | tf_op jit(solution)/shard_map/ppermute | solution.py:270
  26.4 34.9 %all-gather = bf16[576,768]{1,0:T(8,128)(2,1)S(1)} all-gather(bf16[72,768]{1,0:T(8,128)(2,1)S(1)} %get-tuple-element.16), channel_id=2, replica_groups={{0,16,32,48,64,80,96,112},{8,24,40,56,72,88,104,120},{1,17,33,49,65,81,..., dimensions={0}, use_global_device_ids=true | all-gather | bytes 995328 | tf_op jit(solution)/shard_map/all_gather | solution.py:273
  61.3 0.0 collective-permute-done.2.refs_3_
  61.3 0.0 collective-permute-done.1.refs_2_
  61.3 0.0 collective-permute-done.refs_1_
  61.3 3.5 %collective-permute-start.3 = (bf16[8,72,768]{2,1,0:T(8,128)(2,1)S(1)}, bf16[8,72,768]{2,1,0:T(8,128)(2,1)S(1)}, u32[]{:S(2)}, u32[]{:S(2)}) collective-permute-start(bf16[8,72,768]{2,1,0:T(8,128)(2,1)S(1)} %bitcast.12), channel_id=1, source_target_pairs={{0,8},{4,124},{8,16},{12,4},{16,24},{20,12},{24,32},{28,20},{32,40... | collective-permute-start | bytes 2654216 | tf_op jit(solution)/shard_map/ppermute | solution.py:276
  64.8 10.1 %collective-permute-start.4 = (bf16[8,72,768]{2,1,0:T(8,128)(2,1)S(1)}, bf16[8,72,768]{2,1,0:T(8,128)(2,1)S(1)}, u32[]{:S(2)}, u32[]{:S(2)}) collective-permute-start(bf16[8,72,768]{2,1,0:T(8,128)(2,1)S(1)} %bitcast.13), channel_id=1, source_target_pairs={{0,4},{4,0},{1,5},{5,1},{2,6},{6,2},{3,7},{7,3},{8,12},{12,8},{9,1... | collective-permute-start | bytes 2654216 | tf_op jit(solution)/shard_map/ppermute | solution.py:277
  74.8 1.6 %collective-permute-done.3.refs_5_ = bf16[8,72,768]{2,1,0:T(8,128)(2,1)S(1)} collective-permute-done((bf16[8,72,768]{2,1,0:T(8,128)(2,1)S(1)}, bf16[8,72,768]{2,1,0:T(8,128)(2,1)S(1)}, u32[]{:S(2)}, u32[]{:S(2)}) %collective-permute-start.3) | collective-permute-done | bytes 884768 | tf_op jit(solution)/shard_map/ppermute | solution.py:276
  76.4 11.1 %collective-permute-start.5 = (bf16[8,72,768]{2,1,0:T(8,128)(2,1)S(1)}, bf16[8,72,768]{2,1,0:T(8,128)(2,1)S(1)}, u32[]{:S(2)}, u32[]{:S(2)}) collective-permute-start(bf16[8,72,768]{2,1,0:T(8,128)(2,1)S(1)} %collective-permute-done.3.refs_5_), channel_id=1, source_target_pairs={{0,4},{4,0},{1,5},{5,1},{2,6},{6,2},{3,7},{7,3},{8,12},{12,8},{9,1... | collective-permute-start | bytes 2654216 | tf_op jit(solution)/shard_map/ppermute | solution.py:277
  87.5 0.0 collective-permute-done.4.refs_6_
  87.5 2.0 %collective-permute-done.5.refs_7_ = bf16[8,72,768]{2,1,0:T(8,128)(2,1)S(1)} collective-permute-done((bf16[8,72,768]{2,1,0:T(8,128)(2,1)S(1)}, bf16[8,72,768]{2,1,0:T(8,128)(2,1)S(1)}, u32[]{:S(2)}, u32[]{:S(2)}) %collective-permute-start.5) | collective-permute-done | bytes 884768 | tf_op jit(solution)/shard_map/ppermute | solution.py:277
  89.5 0.0 copy-done.4
  89.6 0.0 copy-done.5
  89.6 10.1 %shard_map.75 = bf16[16,72,768]{2,1,0:T(8,128)(2,1)S(1)} custom-call(s32[4]{0:T(128)S(1)} %pad_add_fusion.place_ref, bf16[264,768]{1,0:T(8,128)(2,1)S(1)} %get-tuple-element.18.refs_0_, bf16[264,768]{1,0:T(8,128)(2,1)S(1)} %collective-permute-done.refs_1_, bf16[264,768]{1,0:T(8,128)(2,1)S(1)} %collective-permute-done.1.refs_2_, ...), custom_call_target="tpu_custom_call" | custom-call | flops 4000000000 | bytes 10000000 | tf_op jit(solution)/shard_map/pallas_call | solution.py:210
  99.7 0.0 copy-start
  99.7 0.0 copy-start.2
  99.7 31.0 %all_to_all.5.arrived_ref = bf16[16,72,768]{2,1,0:T(8,128)(2,1)S(1)} all-to-all(bf16[16,72,768]{2,1,0:T(8,128)(2,1)S(1)} %shard_map.75), channel_id=1, replica_groups=mesh['x'=4,'z'=16,'core'=2,'sub'=4] {'x','sub'}, dimensions={0} | all-to-all | bytes 3538944 | tf_op jit(solution)/shard_map/all_to_all | solution.py:279
  130.7 0.0 copy-done
  130.7 0.0 copy-done.2
  130.8 1.1 shard_map.76
Async XLA Ops:
  13.0 1.3 copy-start.1
  14.3 0.7 copy-start.3
  15.0 74.6 %copy-start.4 = (bf16[768,768]{1,0:T(8,128)(2,1)S(1)}, bf16[768,768]{1,0:T(8,128)(2,1)}, u32[]{:S(2)}) copy-start(bf16[768,768]{1,0:T(8,128)(2,1)} %refs_8_.1) | copy-start | bytes 3538948
  15.0 74.6 %copy-start.5 = (bf16[768,768]{1,0:T(8,128)(2,1)S(1)}, bf16[768,768]{1,0:T(8,128)(2,1)}, u32[]{:S(2)}) copy-start(bf16[768,768]{1,0:T(8,128)(2,1)} %refs_9_.1) | copy-start | bytes 3538948
  16.0 45.3 %collective-permute-start.2 = (bf16[264,768]{1,0:T(8,128)(2,1)S(1)}, bf16[264,768]{1,0:T(8,128)(2,1)S(1)}, u32[]{:S(2)}, u32[]{:S(2)}) collective-permute-start(bf16[264,768]{1,0:T(8,128)(2,1)S(1)} %get-tuple-element.18.refs_0_), channel_id=1, source_target_pairs={{0,384},{128,0},{256,128},{384,256},{1,385},{129,1},{257,129},{385... | collective-permute-start | bytes 1216520 | tf_op jit(solution)/shard_map/ppermute | solution.py:270
  21.5 39.9 %collective-permute-start.1 = (bf16[264,768]{1,0:T(8,128)(2,1)S(1)}, bf16[264,768]{1,0:T(8,128)(2,1)S(1)}, u32[]{:S(2)}, u32[]{:S(2)}) collective-permute-start(bf16[264,768]{1,0:T(8,128)(2,1)S(1)} %get-tuple-element.18.refs_0_), channel_id=1, source_target_pairs={{0,256},{128,384},{256,0},{384,128},{1,257},{129,385},{257,1},{385... | collective-permute-start | bytes 1216520 | tf_op jit(solution)/shard_map/ppermute | solution.py:270
  23.9 37.4 %collective-permute-start = (bf16[264,768]{1,0:T(8,128)(2,1)S(1)}, bf16[264,768]{1,0:T(8,128)(2,1)S(1)}, u32[]{:S(2)}, u32[]{:S(2)}) collective-permute-start(bf16[264,768]{1,0:T(8,128)(2,1)S(1)} %get-tuple-element.18.refs_0_), channel_id=1, source_target_pairs={{0,128},{128,256},{256,384},{384,0},{1,129},{129,257},{257,385},{3... | collective-permute-start | bytes 1216520 | tf_op jit(solution)/shard_map/ppermute | solution.py:270
  61.3 15.1 %collective-permute-start.3 = (bf16[8,72,768]{2,1,0:T(8,128)(2,1)S(1)}, bf16[8,72,768]{2,1,0:T(8,128)(2,1)S(1)}, u32[]{:S(2)}, u32[]{:S(2)}) collective-permute-start(bf16[8,72,768]{2,1,0:T(8,128)(2,1)S(1)} %bitcast.12), channel_id=1, source_target_pairs={{0,8},{4,124},{8,16},{12,4},{16,24},{20,12},{24,32},{28,20},{32,40... | collective-permute-start | bytes 2654216 | tf_op jit(solution)/shard_map/ppermute | solution.py:276
  64.8 22.7 %collective-permute-start.4 = (bf16[8,72,768]{2,1,0:T(8,128)(2,1)S(1)}, bf16[8,72,768]{2,1,0:T(8,128)(2,1)S(1)}, u32[]{:S(2)}, u32[]{:S(2)}) collective-permute-start(bf16[8,72,768]{2,1,0:T(8,128)(2,1)S(1)} %bitcast.13), channel_id=1, source_target_pairs={{0,4},{4,0},{1,5},{5,1},{2,6},{6,2},{3,7},{7,3},{8,12},{12,8},{9,1... | collective-permute-start | bytes 2654216 | tf_op jit(solution)/shard_map/ppermute | solution.py:277
  76.4 13.1 %collective-permute-start.5 = (bf16[8,72,768]{2,1,0:T(8,128)(2,1)S(1)}, bf16[8,72,768]{2,1,0:T(8,128)(2,1)S(1)}, u32[]{:S(2)}, u32[]{:S(2)}) collective-permute-start(bf16[8,72,768]{2,1,0:T(8,128)(2,1)S(1)} %collective-permute-done.3.refs_5_), channel_id=1, source_target_pairs={{0,4},{4,0},{1,5},{5,1},{2,6},{6,2},{3,7},{7,3},{8,12},{12,8},{9,1... | collective-permute-start | bytes 2654216 | tf_op jit(solution)/shard_map/ppermute | solution.py:277
  99.7 31.0 %copy-start = (bf16[768,768]{1,0:T(8,128)(2,1)S(1)}, bf16[768,768]{1,0:T(8,128)(2,1)}, u32[]{:S(2)}) copy-start(bf16[768,768]{1,0:T(8,128)(2,1)} %w_ref.3) | copy-start | bytes 3538948
  99.7 31.0 %copy-start.2 = (bf16[8,8,768]{2,1,0:T(8,128)(2,1)S(1)}, bf16[8,8,768]{2,1,0:T(8,128)(2,1)}, u32[]{:S(2)}) copy-start(bf16[8,8,768]{2,1,0:T(8,128)(2,1)} %param.7) | copy-start | bytes 294916

commit v4 on v3

--- a/solution.py
+++ b/solution.py
@@ -22,6 +22,9 @@
 INFO = 8
 LIST = NX * NY + GROUP
 LANES = 128
+SLABS = D // LANES
+SLAB = 2 * TOK
+FILL = SLABS * SLAB
 VMEM = pl.BlockSpec(memory_space=pltpu.VMEM)
 SMEM = pl.BlockSpec(memory_space=pltpu.SMEM)
 INT = jnp.int32
@@ -31,11 +34,13 @@
     return lax.broadcasted_iota(INT, (rows, LANES), axis)
 
 
-def norm_kernel(tokens_ref, pairs_ref, weight_ref, normed_ref, info_ref, rows):
+def norm_kernel(tokens_ref, pairs_ref, weight_ref, copies_ref, info_ref, rows):
     numbers = tokens_ref[...].astype(jnp.float32)
     centred = numbers - jnp.mean(numbers, axis=-1, keepdims=True)
     spread = jnp.mean(centred * centred, axis=-1, keepdims=True)
-    normed_ref[...] = (centred * lax.rsqrt(spread + 1e-06)).astype(jnp.bfloat16)
+    normed = (centred * lax.rsqrt(spread + 1e-06)).astype(jnp.bfloat16)
+    for s in range(SUB):
+        copies_ref[s] = normed
     rows[...] = jnp.zeros_like(rows)
     second = pairs_ref[1:2, :]
     rows[0:1, 0:PAIR] = (pairs_ref[0:1, :] & (IMG - 1)).astype(jnp.float32)
@@ -45,13 +50,28 @@
     info_ref[...] = rows[...].astype(jnp.bfloat16)
 
 
-def query_kernel(place_ref, normed_ref, info_ref, w_ref, queries_ref, block_ref):
-    queries = jnp.dot(normed_ref[...], w_ref[...], preferred_element_type=jnp.float32)
-    queries_ref[0 : IMG * TOK, :] = (queries * HEAD ** (-0.5)).astype(jnp.bfloat16)
-    queries_ref[IMG * TOK : IMG * TOK + INFO, :] = info_ref[...]
-    first = pl.multiple_of(place_ref[3] * (2 * TOK), 2 * TOK)
-    block_ref[0 : 2 * TOK, :] = normed_ref[pl.ds(first, 2 * TOK), :]
-    block_ref[2 * TOK : 2 * TOK + INFO, :] = info_ref[...]
+def image_rows(parts, i):
+    return jnp.concatenate([part[i * ROWS : (i + 1) * ROWS] for part in parts], axis=0).astype(jnp.bfloat16)
+
+
+def query_kernel(place_ref, normed_ref, info_ref, w_ref, queries_ref, block_ref, weight, sem):
+    copy = pltpu.make_async_copy(w_ref, weight, sem)
+    copy.start()
+    first = pl.multiple_of(place_ref[3] * (2 * ROWS), 2 * ROWS)
+    parts = [normed_ref[s, pl.ds(first, 2 * ROWS), :].astype(jnp.float32) for s in range(SUB)]
+    for k in range(2):
+        rows = image_rows(parts, k)
+        for j in range(SLABS):
+            block_ref[SLAB * j + TOK * k : SLAB * j + TOK * (k + 1), :] = rows[:, LANES * j : LANES * (j + 1)]
+    block_ref[FILL : FILL + INFO, :] = info_ref[...]
+    queries_ref[IMG * TOK : IMG * TOK + INFO, 0:LANES] = info_ref[...]
+    queries_ref[IMG * TOK : IMG * TOK + INFO, LANES:D] = jnp.zeros((INFO, D - LANES), jnp.bfloat16)
+    copy.wait()
+    parts = [
+        jnp.dot(normed_ref[s], weight[...], preferred_element_type=jnp.float32) * HEAD ** (-0.5) for s in range(SUB)
+    ]
+    for i in range(IMG):
+        queries_ref[i * TOK : (i + 1) * TOK, :] = image_rows(parts, i)
 
 
 def side_weights(place_ref, query_refs, pieces, fields):
@@ -74,7 +94,7 @@
     block = 0
     for ref in pieces:
         for j in range(ref.shape[0]):
-            fields[block * INFO : (block + 1) * INFO, :] = ref[j, 2 * TOK : 2 * TOK + INFO, 0:LANES].astype(jnp.float32)
+            fields[block * INFO : (block + 1) * INFO, :] = ref[j, FILL : FILL + INFO, :].astype(jnp.float32)
             block += 1
     a, owner, b, weight = (fields[pl.ds(f, BLOCKS, stride=INFO), :].astype(INT) for f in range(4))
     ok = ((owner & (BLOCKS - 1)) == z_here * CORE + core_here) & ((a >> 1) == sub_here)
@@ -124,9 +144,8 @@
     for d in range(X):
         shifted = pltpu.roll(halves, (LANES - d * IMG) % LANES, 1)
         place = ((place_ref[0] + (X - d)) & (X - 1)) * SUB
-        wide = jnp.concatenate([shifted, jnp.zeros((INFO, D - LANES), jnp.float32)], axis=1).astype(jnp.bfloat16)
         for s in range(SUB):
-            out_ref[place + s, OWN : OWN + INFO, :] = wide
+            out_ref[place + s, FILL : FILL + INFO, :] = shifted.astype(jnp.bfloat16)
 
     acc[...] = jnp.zeros_like(acc)
     for d, ref in enumerate(query_refs):
@@ -147,7 +166,10 @@
                 def _():
                     slot = count[0]
                     count[0] = slot + 1
-                    rows[pl.ds(pl.multiple_of(slot * TOK, TOK), TOK), :] = ref[j, k * TOK : (k + 1) * TOK, :]
+                    here = pl.ds(pl.multiple_of(slot * TOK, TOK), TOK)
+                    for slab in range(SLABS):
+                        first = SLAB * slab + TOK * k
+                        rows[here, LANES * slab : LANES * (slab + 1)] = ref[j, first : first + TOK, :]
 
                     def more(state):
                         return state[0] != 0
@@ -203,13 +225,16 @@
             for i in range(IMG // 2):
                 first = (d * IMG + 2 * i) * TOK + s * ROWS
                 block = jnp.concatenate([acc[first : first + ROWS, :], acc[first + TOK : first + TOK + ROWS, :]], axis=0)
-                out_ref[place + s, 2 * i * ROWS : 2 * (i + 1) * ROWS, :] = block.astype(jnp.bfloat16)
+                block = block.astype(jnp.bfloat16)
+                for slab in range(SLABS):
+                    row = SLAB * slab + 2 * ROWS * i
+                    out_ref[place + s, row : row + 2 * ROWS, :] = block[:, LANES * slab : LANES * (slab + 1)]
 
 
 def attend(place, queries, pieces, w_key, w_value):
     return pl.pallas_call(
         attend_kernel,
-        out_shape=jax.ShapeDtypeStruct((X * SUB, OWN + INFO, D), jnp.bfloat16),
+        out_shape=jax.ShapeDtypeStruct((X * SUB, FILL + INFO, LANES), jnp.bfloat16),
         in_specs=[SMEM] + [VMEM] * (len(queries) + len(pieces) + 2),
         out_specs=VMEM,
         scratch_shapes=[
@@ -231,12 +256,11 @@
 
 
 def finish_kernel(arrived_ref, tokens_ref, w_ref, out_ref):
-    summed = arrived_ref[0, 0:OWN, :].astype(jnp.float32)
-    halves = arrived_ref[0, OWN : OWN + INFO, 0:LANES].astype(jnp.float32)
+    arrived = arrived_ref[0].astype(jnp.float32)
     for k in range(1, X * SUB):
-        summed = summed + arrived_ref[k, 0:OWN, :].astype(jnp.float32)
-        halves = halves + arrived_ref[k, OWN : OWN + INFO, 0:LANES].astype(jnp.float32)
-    totals = halves[0:1, :] * 128.0 + halves[1:2, :]
+        arrived = arrived + arrived_ref[k].astype(jnp.float32)
+    summed = jnp.concatenate([arrived[SLAB * j : SLAB * (j + 1)] for j in range(SLABS)], axis=1)
+    totals = arrived[FILL : FILL + 1] * 128.0 + arrived[FILL + 1 : FILL + 2]
     inverse = 1.0 / jnp.maximum(totals, 1.0)
     keep = totals * inverse
     scaled, kept = [], []
@@ -252,29 +276,39 @@
 def body(tokens, pairs, confidence, w_query, w_key, w_value, w_out):
     place = jnp.stack([lax.axis_index(name) for name in ("x", "z", "core", "sub")]).astype(INT)
     tokens = tokens.reshape(OWN, D)
-    normed, info = pl.pallas_call(
+    copies, info = pl.pallas_call(
         norm_kernel,
-        out_shape=[jax.ShapeDtypeStruct((OWN, D), jnp.bfloat16), jax.ShapeDtypeStruct((INFO, D), jnp.bfloat16)],
-        scratch_shapes=[pltpu.VMEM((INFO, D), jnp.float32)],
+        out_shape=[
+            jax.ShapeDtypeStruct((SUB, OWN, D), jnp.bfloat16),
+            jax.ShapeDtypeStruct((INFO, LANES), jnp.bfloat16),
+        ],
+        scratch_shapes=[pltpu.VMEM((INFO, LANES), jnp.float32)],
     )(tokens, pairs.T, confidence.reshape(1, PAIR))
-    normed = lax.all_gather(normed.reshape(IMG, ROWS, D), "sub", axis=1, tiled=True).reshape(IMG * TOK, D)
+    normed = lax.all_to_all(copies, "sub", split_axis=0, concat_axis=0, tiled=True)
     queries, block = pl.pallas_call(
         query_kernel,
-        in_specs=[SMEM, VMEM, VMEM, VMEM],
+        in_specs=[SMEM, VMEM, VMEM, pl.BlockSpec(memory_space=pltpu.HBM)],
         out_shape=[
             jax.ShapeDtypeStruct((IMG * TOK + INFO, D), jnp.bfloat16),
-            jax.ShapeDtypeStruct((2 * TOK + INFO, D), jnp.bfloat16),
+            jax.ShapeDtypeStruct((FILL + INFO, LANES), jnp.bfloat16),
         ],
+        scratch_shapes=[pltpu.VMEM((D, D), jnp.bfloat16), pltpu.SemaphoreType.DMA],
         compiler_params=pltpu.CompilerParams(vmem_limit_bytes=16 * 1024 * 1024),
     )(place, normed, info, w_query)
-    queries = [queries] + [lax.ppermute(queries, "x", [(i, (i + d) % X) for i in range(X)]) for d in (1, 2, 3)]
-
+
+    def along_x(rows, d):
+        return lax.ppermute(rows, "x", [(i, (i + d) % X) for i in range(X)])
+
+    below, above = along_x(queries, 1), along_x(queries, X - 1)
     groups = [[2 * k + parity for k in range(Z // 2)] for parity in range(2)]
     same = lax.all_gather(block, "z", axis=0, tiled=False, axis_index_groups=groups)
-    same, *queries = lax.optimization_barrier((same, *queries))
+    same, queries, below, above = lax.optimization_barrier((same, queries, below, above))
     there = [(z * CORE + c, (z + 1 - 2 * c) % Z * CORE + c) for z in range(Z) for c in range(CORE)]
     other = lax.ppermute(same, ("z", "core"), there)
-    pieces = [same, other] + [lax.ppermute(piece, "core", [(0, 1), (1, 0)]) for piece in (same, other)]
+    same_far = lax.ppermute(same, "core", [(0, 1), (1, 0)])
+    other, across = lax.optimization_barrier((other, along_x(below, 1)))
+    pieces = [same, other, same_far, lax.ppermute(other, "core", [(0, 1), (1, 0)])]
+    queries = [queries, below, across, above]
     sent = attend(place, queries, pieces, w_key, w_value)
     arrived = lax.all_to_all(sent, ("x", "sub"), split_axis=0, concat_axis=0, tiled=True)
     decoded = pl.pallas_call(

time: 132 us -> 123 us (0.932)
  blocking collectives: 77.1 us -> 60.2 us
  waiting for transfers between devices: 3.62 us -> 9.06 us
    all_gather x1 -> x0, blocking collectives: 11.2 us -> none  [body(): lax.all_gather(normed.reshape(IMG, ROWS, D), 'sub', axis=1, tiled=True)]
    ppermute x5, starting transfers between devices: 31.5 us -> 24.5 us  [the longest x3 8.86 us: along_x(): return lax.ppermute(rows, 'x', [(i, (i + d) % X) for i in range(X)])]
    all_to_all x0 -> x1, waiting for transfers between devices: none -> 6.15 us  [body(): lax.all_to_all(copies, 'sub', split_axis=0, concat_axis=0, tiled=True)]
    all_to_all x1, blocking collectives: 31 us -> 25.8 us  [body(): lax.all_to_all(sent, ('x', 'sub'), split_axis=0, concat_axis=0, tiled=True)]
    all_to_all x0 -> x1, starting transfers between devices: none -> 5.01 us  [body(): lax.all_to_all(copies, 'sub', split_axis=0, concat_axis=0, tiled=True)]
    ppermute x1, starting transfers between devices: 3.46 us -> 6.08 us  [body(): other = lax.ppermute(same, ('z', 'core'), there)]
    ppermute x1, waiting for transfers between devices: 1.59 us -> 0.01 us  [body(): other = lax.ppermute(same, ('z', 'core'), there)]
  transfers between devices with their start and end apart: 6 -> 7, of which waited for: 2 -> 3; matrix products, arithmetic and copies ran while one was open for 0% -> 0% of each run, Pallas kernels for 0% -> 0%
where the time goes in v4:
time: 123 us; the launch traced here: 122 us
  blocking collectives  60.2 us (49%)
  starting transfers between devices  35.6 us (29%)
  Pallas kernels  14.9 us (12%)
  waiting for transfers between devices  9.06 us (7%)
  local copies, waits for them, and re-layouts  1.97 us (2%)
    all_gather x1, blocking collectives, body(): lax.all_gather(block, 'z', axis=0, tiled=False, axis_index_groups=groups)  34.4 us
    all_to_all x1, blocking collectives, body(): lax.all_to_all(sent, ('x', 'sub'), split_axis=0, concat_axis=0, tiled=True)  25.8 us
    pallas_call x1, Pallas kernels, attend(): pl.pallas_call(attend_kernel, out_shape=jax.ShapeDtypeStruct((X * SUB, FI...  10.2 us
    ppermute x3, starting transfers between devices, along_x(): return lax.ppermute(rows, 'x', [(i, (i + d) % X) for i in range(X)])  8.86 us
    ppermute x1, starting transfers between devices, body(): lax.ppermute(other, 'core', [(0, 1), (1, 0)])  8.41 us
    ppermute x1, starting transfers between devices, body(): same_far = lax.ppermute(same, 'core', [(0, 1), (1, 0)])  7.23 us
    all_to_all x1, waiting for transfers between devices, body(): lax.all_to_all(copies, 'sub', split_axis=0, concat_axis=0, tiled=True)  6.15 us
    ppermute x1, starting transfers between devices, body(): other = lax.ppermute(same, ('z', 'core'), there)  6.08 us
  transfers between devices with their start and end apart: 7, of which 3 were waited for; matrix products, arithmetic and copies ran while one was open for 0% of the time, Pallas kernels for 0%

profile of v4, /device:TPU:1, one launch (start us, length us, event | category | flops | bytes accessed | tf_op | source)
XLA Modules:
  0.0 121.9 jit_solution(5835129743255443988)
XLA Ops:
  0.0 1.9 %shard_map.73 = (bf16[4,64,768]{2,1,0:T(8,128)(2,1)}, bf16[8,128]{1,0:T(8,128)(2,1)}) custom-call(bf16[64,768]{1,0:T(8,128)(2,1)} %bitcast.12, s32[2,32]{1,0:T(2,128)} %bitcast.14, s32[1,32]{1,0:T(1,128)} %bitcast.15), custom_call_target="tpu_custom_call" | custom-call | tf_op jit(solution)/shard_map/pallas_call | solution.py:279
  1.9 5.0 %all-to-all-start = ((bf16[4,64,768]{2,1,0:T(8,128)(2,1)}), bf16[4,64,768]{2,1,0:T(8,128)(2,1)S(1)}, u32[]{:S(2)}, u32[]{:S(2)}) async-start(bf16[4,64,768]{2,1,0:T(8,128)(2,1)} %get-tuple-element.15), calls=%async_computation | async-start | bytes 786432 | tf_op jit(solution)/shard_map/all_to_all | solution.py:287
  6.9 0.1 pad_add_fusion.place_ref
  6.9 6.2 %all-to-all-done.normed_ref = bf16[4,64,768]{2,1,0:T(8,128)(2,1)S(1)} async-done(((bf16[4,64,768]{2,1,0:T(8,128)(2,1)}), bf16[4,64,768]{2,1,0:T(8,128)(2,1)S(1)}, u32[]{:S(2)}, u32[]{:S(2)}) %all-to-all-start) | async-done | bytes 393248 | tf_op jit(solution)/shard_map/all_to_all | solution.py:287
  13.1 0.0 copy-start
  13.1 1.3 %copy-done = bf16[768,768]{1,0:T(8,128)(2,1)S(1)} copy-done((bf16[768,768]{1,0:T(8,128)(2,1)S(1)}, bf16[768,768]{1,0:T(8,128)(2,1)}, u32[]{:S(2)}) %copy-start) | copy-done | bytes 1179672
  14.4 0.0 copy-start.3
  14.4 0.7 copy-done.3
  15.1 0.0 copy-start.4
  15.1 0.0 copy-start.5
  15.1 1.7 %shard_map.74 = (bf16[264,768]{1,0:T(8,128)(2,1)S(1)}, bf16[392,128]{1,0:T(8,128)(2,1)S(1)}) custom-call(s32[4]{0:T(128)S(1)} %pad_add_fusion.place_ref, bf16[4,64,768]{2,1,0:T(8,128)(2,1)S(1)} %all-to-all-done.normed_ref, bf16[8,128]{1,0:T(8,128)(2,1)S(1)} %copy-done.3, bf16[768,768]{1,0:T(8,128)(2,1)S(1)} %copy-done), custom_call_target="tpu_custom_call" | custom-call | tf_op jit(solution)/shard_map/pallas_call | solution.py:288
  16.8 5.0 %collective-permute-start.1 = (bf16[264,768]{1,0:T(8,128)(2,1)S(1)}, bf16[264,768]{1,0:T(8,128)(2,1)S(1)}, u32[]{:S(2)}, u32[]{:S(2)}) collective-permute-start(bf16[264,768]{1,0:T(8,128)(2,1)S(1)} %get-tuple-element.19.refs_0_), channel_id=1, source_target_pairs={{0,384},{128,0},{256,128},{384,256},{1,385},{129,1},{257,129},{385... | collective-permute-start | bytes 1216520 | tf_op jit(solution)/shard_map/ppermute | solution.py:300
  21.8 1.9 %collective-permute-start = (bf16[264,768]{1,0:T(8,128)(2,1)S(1)}, bf16[264,768]{1,0:T(8,128)(2,1)S(1)}, u32[]{:S(2)}, u32[]{:S(2)}) collective-permute-start(bf16[264,768]{1,0:T(8,128)(2,1)S(1)} %get-tuple-element.19.refs_0_), channel_id=1, source_target_pairs={{0,128},{128,256},{256,384},{384,0},{1,129},{129,257},{257,385},{3... | collective-permute-start | bytes 1216520 | tf_op jit(solution)/shard_map/ppermute | solution.py:300
  23.8 34.4 %all-gather = bf16[3136,128]{1,0:T(8,128)(2,1)S(1)} all-gather(bf16[392,128]{1,0:T(8,128)(2,1)S(1)} %get-tuple-element.17), channel_id=2, replica_groups={{0,16,32,48,64,80,96,112},{8,24,40,56,72,88,104,120},{1,17,33,49,65,81,..., dimensions={0}, use_global_device_ids=true | all-gather | bytes 903168 | tf_op jit(solution)/shard_map/all_gather | solution.py:304
  58.2 0.0 collective-permute-done.1.refs_3_
  58.2 0.0 collective-permute-done.refs_1_
  58.2 6.1 %collective-permute-start.2 = (bf16[8,392,128]{2,1,0:T(8,128)(2,1)S(1)}, bf16[8,392,128]{2,1,0:T(8,128)(2,1)S(1)}, u32[]{:S(2)}, u32[]{:S(2)}) collective-permute-start(bf16[8,392,128]{2,1,0:T(8,128)(2,1)S(1)} %bitcast.9), channel_id=1, source_target_pairs={{0,8},{4,124},{8,16},{12,4},{16,24},{20,12},{24,32},{28,20},{32,40... | collective-permute-start | bytes 2408456 | tf_op jit(solution)/shard_map/ppermute | solution.py:307
  64.3 1.9 %collective-permute-start.3 = (bf16[264,768]{1,0:T(8,128)(2,1)S(1)}, bf16[264,768]{1,0:T(8,128)(2,1)S(1)}, u32[]{:S(2)}, u32[]{:S(2)}) collective-permute-start(bf16[264,768]{1,0:T(8,128)(2,1)S(1)} %collective-permute-done.refs_1_), channel_id=1, source_target_pairs={{0,128},{128,256},{256,384},{384,0},{1,129},{129,257},{257,385},{3... | collective-permute-start | bytes 1216520 | tf_op jit(solution)/shard_map/ppermute | solution.py:300
  66.2 7.2 %collective-permute-start.4 = (bf16[8,392,128]{2,1,0:T(8,128)(2,1)S(1)}, bf16[8,392,128]{2,1,0:T(8,128)(2,1)S(1)}, u32[]{:S(2)}, u32[]{:S(2)}) collective-permute-start(bf16[8,392,128]{2,1,0:T(8,128)(2,1)S(1)} %bitcast.10), channel_id=1, source_target_pairs={{0,4},{4,0},{1,5},{5,1},{2,6},{6,2},{3,7},{7,3},{8,12},{12,8},{9,1... | collective-permute-start | bytes 2408456 | tf_op jit(solution)/shard_map/ppermute | solution.py:308
  73.5 1.0 collective-permute-done.3.refs_2_
  74.5 0.0 collective-permute-done.2.refs_5_
  74.5 8.4 %collective-permute-start.5 = (bf16[8,392,128]{2,1,0:T(8,128)(2,1)S(1)}, bf16[8,392,128]{2,1,0:T(8,128)(2,1)S(1)}, u32[]{:S(2)}, u32[]{:S(2)}) collective-permute-start(bf16[8,392,128]{2,1,0:T(8,128)(2,1)S(1)} %collective-permute-done.2.refs_5_), channel_id=1, source_target_pairs={{0,4},{4,0},{1,5},{5,1},{2,6},{6,2},{3,7},{7,3},{8,12},{12,8},{9,1... | collective-permute-start | bytes 2408456 | tf_op jit(solution)/shard_map/ppermute | solution.py:310
  82.9 0.0 collective-permute-done.4.refs_6_
  82.9 1.9 %collective-permute-done.5.refs_7_ = bf16[8,392,128]{2,1,0:T(8,128)(2,1)S(1)} collective-permute-done((bf16[8,392,128]{2,1,0:T(8,128)(2,1)S(1)}, bf16[8,392,128]{2,1,0:T(8,128)(2,1)S(1)}, u32[]{:S(2)}, u32[]{:S(2)}) %collective-permute-start.5) | collective-permute-done | bytes 802848 | tf_op jit(solution)/shard_map/ppermute | solution.py:310
  84.8 0.0 copy-done.4
  84.8 0.0 copy-done.5
  84.8 10.2 %shard_map.75 = bf16[16,392,128]{2,1,0:T(8,128)(2,1)S(1)} custom-call(s32[4]{0:T(128)S(1)} %pad_add_fusion.place_ref, bf16[264,768]{1,0:T(8,128)(2,1)S(1)} %get-tuple-element.19.refs_0_, bf16[264,768]{1,0:T(8,128)(2,1)S(1)} %collective-permute-done.refs_1_, bf16[264,768]{1,0:T(8,128)(2,1)S(1)} %collective-permute-done.3.refs_2_, ...), custom_call_target="tpu_custom_call" | custom-call | flops 4000000000 | bytes 10000000 | tf_op jit(solution)/shard_map/pallas_call | solution.py:235
  95.0 0.0 copy-start.1
  95.0 0.0 copy-start.2
  95.0 25.8 %all_to_all.10.arrived_ref = bf16[16,392,128]{2,1,0:T(8,128)(2,1)S(1)} all-to-all(bf16[16,392,128]{2,1,0:T(8,128)(2,1)S(1)} %shard_map.75), channel_id=1, replica_groups=mesh['x'=4,'z'=16,'core'=2,'sub'=4] {'x','sub'}, dimensions={0} | all-to-all | bytes 3211264 | tf_op jit(solution)/shard_map/all_to_all | solution.py:313
  120.8 0.0 copy-done.1
  120.8 0.0 copy-done.2
  120.8 1.1 shard_map.76
Async XLA Ops:
  1.9 11.2 %all-to-all-start = ((bf16[4,64,768]{2,1,0:T(8,128)(2,1)}), bf16[4,64,768]{2,1,0:T(8,128)(2,1)S(1)}, u32[]{:S(2)}, u32[]{:S(2)}) async-start(bf16[4,64,768]{2,1,0:T(8,128)(2,1)} %get-tuple-element.15), calls=%async_computation | async-start | bytes 786432 | tf_op jit(solution)/shard_map/all_to_all | solution.py:287
  13.1 1.3 %copy-start = (bf16[768,768]{1,0:T(8,128)(2,1)S(1)}, bf16[768,768]{1,0:T(8,128)(2,1)}, u32[]{:S(2)}) copy-start(bf16[768,768]{1,0:T(8,128)(2,1)} %w_ref.2) | copy-start | bytes 3538948
  14.4 0.7 copy-start.3
  15.1 69.7 %copy-start.4 = (bf16[768,768]{1,0:T(8,128)(2,1)S(1)}, bf16[768,768]{1,0:T(8,128)(2,1)}, u32[]{:S(2)}) copy-start(bf16[768,768]{1,0:T(8,128)(2,1)} %refs_8_.1) | copy-start | bytes 3538948
  15.1 69.7 %copy-start.5 = (bf16[768,768]{1,0:T(8,128)(2,1)S(1)}, bf16[768,768]{1,0:T(8,128)(2,1)}, u32[]{:S(2)}) copy-start(bf16[768,768]{1,0:T(8,128)(2,1)} %refs_9_.1) | copy-start | bytes 3538948
  16.8 41.4 %collective-permute-start.1 = (bf16[264,768]{1,0:T(8,128)(2,1)S(1)}, bf16[264,768]{1,0:T(8,128)(2,1)S(1)}, u32[]{:S(2)}, u32[]{:S(2)}) collective-permute-start(bf16[264,768]{1,0:T(8,128)(2,1)S(1)} %get-tuple-element.19.refs_0_), channel_id=1, source_target_pairs={{0,384},{128,0},{256,128},{384,256},{1,385},{129,1},{257,129},{385... | collective-permute-start | bytes 1216520 | tf_op jit(solution)/shard_map/ppermute | solution.py:300
  21.8 36.4 %collective-permute-start = (bf16[264,768]{1,0:T(8,128)(2,1)S(1)}, bf16[264,768]{1,0:T(8,128)(2,1)S(1)}, u32[]{:S(2)}, u32[]{:S(2)}) collective-permute-start(bf16[264,768]{1,0:T(8,128)(2,1)S(1)} %get-tuple-element.19.refs_0_), channel_id=1, source_target_pairs={{0,128},{128,256},{256,384},{384,0},{1,129},{129,257},{257,385},{3... | collective-permute-start | bytes 1216520 | tf_op jit(solution)/shard_map/ppermute | solution.py:300
  58.2 16.2 %collective-permute-start.2 = (bf16[8,392,128]{2,1,0:T(8,128)(2,1)S(1)}, bf16[8,392,128]{2,1,0:T(8,128)(2,1)S(1)}, u32[]{:S(2)}, u32[]{:S(2)}) collective-permute-start(bf16[8,392,128]{2,1,0:T(8,128)(2,1)S(1)} %bitcast.9), channel_id=1, source_target_pairs={{0,8},{4,124},{8,16},{12,4},{16,24},{20,12},{24,32},{28,20},{32,40... | collective-permute-start | bytes 2408456 | tf_op jit(solution)/shard_map/ppermute | solution.py:307
  64.3 10.2 %collective-permute-start.3 = (bf16[264,768]{1,0:T(8,128)(2,1)S(1)}, bf16[264,768]{1,0:T(8,128)(2,1)S(1)}, u32[]{:S(2)}, u32[]{:S(2)}) collective-permute-start(bf16[264,768]{1,0:T(8,128)(2,1)S(1)} %collective-permute-done.refs_1_), channel_id=1, source_target_pairs={{0,128},{128,256},{256,384},{384,0},{1,129},{129,257},{257,385},{3... | collective-permute-start | bytes 1216520 | tf_op jit(solution)/shard_map/ppermute | solution.py:300
  66.2 16.6 %collective-permute-start.4 = (bf16[8,392,128]{2,1,0:T(8,128)(2,1)S(1)}, bf16[8,392,128]{2,1,0:T(8,128)(2,1)S(1)}, u32[]{:S(2)}, u32[]{:S(2)}) collective-permute-start(bf16[8,392,128]{2,1,0:T(8,128)(2,1)S(1)} %bitcast.10), channel_id=1, source_target_pairs={{0,4},{4,0},{1,5},{5,1},{2,6},{6,2},{3,7},{7,3},{8,12},{12,8},{9,1... | collective-permute-start | bytes 2408456 | tf_op jit(solution)/shard_map/ppermute | solution.py:308
  74.5 10.3 %collective-permute-start.5 = (bf16[8,392,128]{2,1,0:T(8,128)(2,1)S(1)}, bf16[8,392,128]{2,1,0:T(8,128)(2,1)S(1)}, u32[]{:S(2)}, u32[]{:S(2)}) collective-permute-start(bf16[8,392,128]{2,1,0:T(8,128)(2,1)S(1)} %collective-permute-done.2.refs_5_), channel_id=1, source_target_pairs={{0,4},{4,0},{1,5},{5,1},{2,6},{6,2},{3,7},{7,3},{8,12},{12,8},{9,1... | collective-permute-start | bytes 2408456 | tf_op jit(solution)/shard_map/ppermute | solution.py:310
  95.0 25.8 %copy-start.1 = (bf16[768,768]{1,0:T(8,128)(2,1)S(1)}, bf16[768,768]{1,0:T(8,128)(2,1)}, u32[]{:S(2)}) copy-start(bf16[768,768]{1,0:T(8,128)(2,1)} %w_ref.3) | copy-start | bytes 3538948
  95.0 25.8 %copy-start.2 = (bf16[8,8,768]{2,1,0:T(8,128)(2,1)S(1)}, bf16[8,8,768]{2,1,0:T(8,128)(2,1)}, u32[]{:S(2)}) copy-start(bf16[8,8,768]{2,1,0:T(8,128)(2,1)} %param.7) | copy-start | bytes 294916

commit v5 on v4

--- a/solution.py
+++ b/solution.py
@@ -34,41 +34,40 @@
     return lax.broadcasted_iota(INT, (rows, LANES), axis)
 
 
-def norm_kernel(tokens_ref, pairs_ref, weight_ref, copies_ref, info_ref, rows):
+def norm_kernel(tokens_ref, pairs_ref, weight_ref, copies_ref, info):
     numbers = tokens_ref[...].astype(jnp.float32)
     centred = numbers - jnp.mean(numbers, axis=-1, keepdims=True)
     spread = jnp.mean(centred * centred, axis=-1, keepdims=True)
     normed = (centred * lax.rsqrt(spread + 1e-06)).astype(jnp.bfloat16)
+    info[...] = jnp.zeros_like(info)
+    second = pairs_ref[1:2, :]
+    info[0:1, 0:PAIR] = (pairs_ref[0:1, :] & (IMG - 1)).astype(jnp.float32)
+    info[1:2, 0:PAIR] = (second // IMG).astype(jnp.float32)
+    info[2:3, 0:PAIR] = (second & (IMG - 1)).astype(jnp.float32)
+    info[3:4, 0:PAIR] = weight_ref[...].astype(jnp.float32)
+    pair_rows = info[...].astype(jnp.bfloat16)
     for s in range(SUB):
-        copies_ref[s] = normed
-    rows[...] = jnp.zeros_like(rows)
-    second = pairs_ref[1:2, :]
-    rows[0:1, 0:PAIR] = (pairs_ref[0:1, :] & (IMG - 1)).astype(jnp.float32)
-    rows[1:2, 0:PAIR] = (second // IMG).astype(jnp.float32)
-    rows[2:3, 0:PAIR] = (second & (IMG - 1)).astype(jnp.float32)
-    rows[3:4, 0:PAIR] = weight_ref[...].astype(jnp.float32)
-    info_ref[...] = rows[...].astype(jnp.bfloat16)
+        copies_ref[s, 0:OWN, :] = normed
+        copies_ref[s, OWN : OWN + INFO, :] = pair_rows
 
 
 def image_rows(parts, i):
     return jnp.concatenate([part[i * ROWS : (i + 1) * ROWS] for part in parts], axis=0).astype(jnp.bfloat16)
 
 
-def query_kernel(place_ref, normed_ref, info_ref, w_ref, queries_ref, block_ref, weight, sem):
-    copy = pltpu.make_async_copy(w_ref, weight, sem)
-    copy.start()
+def query_kernel(place_ref, normed_ref, w_ref, queries_ref, block_ref):
     first = pl.multiple_of(place_ref[3] * (2 * ROWS), 2 * ROWS)
     parts = [normed_ref[s, pl.ds(first, 2 * ROWS), :].astype(jnp.float32) for s in range(SUB)]
     for k in range(2):
         rows = image_rows(parts, k)
         for j in range(SLABS):
             block_ref[SLAB * j + TOK * k : SLAB * j + TOK * (k + 1), :] = rows[:, LANES * j : LANES * (j + 1)]
-    block_ref[FILL : FILL + INFO, :] = info_ref[...]
-    queries_ref[IMG * TOK : IMG * TOK + INFO, 0:LANES] = info_ref[...]
-    queries_ref[IMG * TOK : IMG * TOK + INFO, LANES:D] = jnp.zeros((INFO, D - LANES), jnp.bfloat16)
-    copy.wait()
+    pair_rows = normed_ref[0, OWN : OWN + INFO, :]
+    block_ref[FILL : FILL + INFO, :] = pair_rows[:, 0:LANES]
+    queries_ref[IMG * TOK : IMG * TOK + INFO, :] = pair_rows
     parts = [
-        jnp.dot(normed_ref[s], weight[...], preferred_element_type=jnp.float32) * HEAD ** (-0.5) for s in range(SUB)
+        jnp.dot(normed_ref[s, 0:OWN, :], w_ref[...], preferred_element_type=jnp.float32) * HEAD ** (-0.5)
+        for s in range(SUB)
     ]
     for i in range(IMG):
         queries_ref[i * TOK : (i + 1) * TOK, :] = image_rows(parts, i)
@@ -117,9 +116,8 @@
             spread, keys[:, lanes], (((1,), (1,)), ((), ())), preferred_element_type=jnp.float32
         )
         exponent = jnp.exp(scores - jnp.max(scores, axis=1, keepdims=True))
-        total = jnp.sum(exponent, axis=1, keepdims=True)
-        probabilities = (exponent * (1.0 / total)).astype(jnp.bfloat16)
-        both = jnp.dot(probabilities, values[:, lanes], preferred_element_type=jnp.float32)
+        inverse = 1.0 / jnp.sum(exponent, axis=1, keepdims=True)
+        both = jnp.dot(exponent.astype(jnp.bfloat16), values[:, lanes], preferred_element_type=jnp.float32) * inverse
         parts.append(jnp.where(low_half, both[:TOK], both[TOK:]))
     return jnp.concatenate(parts, axis=1)
 
@@ -276,25 +274,22 @@
 def body(tokens, pairs, confidence, w_query, w_key, w_value, w_out):
     place = jnp.stack([lax.axis_index(name) for name in ("x", "z", "core", "sub")]).astype(INT)
     tokens = tokens.reshape(OWN, D)
-    copies, info = pl.pallas_call(
+    copies = pl.pallas_call(
         norm_kernel,
-        out_shape=[
-            jax.ShapeDtypeStruct((SUB, OWN, D), jnp.bfloat16),
-            jax.ShapeDtypeStruct((INFO, LANES), jnp.bfloat16),
-        ],
-        scratch_shapes=[pltpu.VMEM((INFO, LANES), jnp.float32)],
+        out_shape=jax.ShapeDtypeStruct((SUB, OWN + INFO, D), jnp.bfloat16),
+        scratch_shapes=[pltpu.VMEM((INFO, D), jnp.float32)],
+        cost_estimate=pl.CostEstimate(flops=2_000_000_000, bytes_accessed=8_000_000, transcendentals=64),
     )(tokens, pairs.T, confidence.reshape(1, PAIR))
     normed = lax.all_to_all(copies, "sub", split_axis=0, concat_axis=0, tiled=True)
     queries, block = pl.pallas_call(
         query_kernel,
-        in_specs=[SMEM, VMEM, VMEM, pl.BlockSpec(memory_space=pltpu.HBM)],
+        in_specs=[SMEM, VMEM, VMEM],
         out_shape=[
             jax.ShapeDtypeStruct((IMG * TOK + INFO, D), jnp.bfloat16),
             jax.ShapeDtypeStruct((FILL + INFO, LANES), jnp.bfloat16),
         ],
-        scratch_shapes=[pltpu.VMEM((D, D), jnp.bfloat16), pltpu.SemaphoreType.DMA],
         compiler_params=pltpu.CompilerParams(vmem_limit_bytes=16 * 1024 * 1024),
-    )(place, normed, info, w_query)
+    )(place, normed, w_query)
 
     def along_x(rows, d):
         return lax.ppermute(rows, "x", [(i, (i + d) % X) for i in range(X)])

time: 123 us -> 120 us (0.976)
  Pallas kernels: 14.9 us -> 12 us
  local copies, waits for them, and re-layouts: 1.97 us -> 0.02 us
  blocking collectives: 60.2 us -> 62.1 us
    pallas_call x1, Pallas kernels: 10.2 us -> 7.36 us  [attend(): pl.pallas_call(attend_kernel, out_shape=jax.ShapeDtypeStruct((X * SUB, FI...]
    unnamed x12 -> x10, local copies, waits for them, and re-layouts: 1.97 us -> 0.02 us
    all_to_all x1, blocking collectives: 25.8 us -> 27.6 us  [body(): lax.all_to_all(sent, ('x', 'sub'), split_axis=0, concat_axis=0, tiled=True)]
where the time goes in v5:
time: 120 us; the launch traced here: 119 us
  blocking collectives  62.1 us (52%)
  starting transfers between devices  36.1 us (30%)
  Pallas kernels  12 us (10%)
  waiting for transfers between devices  8.66 us (7%)
    all_gather x1, blocking collectives, body(): lax.all_gather(block, 'z', axis=0, tiled=False, axis_index_groups=groups)  34.5 us
    all_to_all x1, blocking collectives, body(): lax.all_to_all(sent, ('x', 'sub'), split_axis=0, concat_axis=0, tiled=True)  27.6 us
    ppermute x3, starting transfers between devices, along_x(): return lax.ppermute(rows, 'x', [(i, (i + d) % X) for i in range(X)])  9.13 us
    ppermute x1, starting transfers between devices, body(): lax.ppermute(other, 'core', [(0, 1), (1, 0)])  8.91 us
    ppermute x1, starting transfers between devices, body(): same_far = lax.ppermute(same, 'core', [(0, 1), (1, 0)])  7.89 us
    pallas_call x1, Pallas kernels, attend(): pl.pallas_call(attend_kernel, out_shape=jax.ShapeDtypeStruct((X * SUB, FI...  7.36 us
    all_to_all x1, waiting for transfers between devices, body(): lax.all_to_all(copies, 'sub', split_axis=0, concat_axis=0, tiled=True)  6.42 us
    ppermute x1, starting transfers between devices, body(): other = lax.ppermute(same, ('z', 'core'), there)  5.2 us
  transfers between devices with their start and end apart: 7, of which 3 were waited for; matrix products, arithmetic and copies ran while one was open for 0% of the time, Pallas kernels for 0%

profile of v5, /device:TPU:1, one launch (start us, length us, event | category | flops | bytes accessed | tf_op | source)
XLA Modules:
  0.0 119.1 jit_solution(3474597144291762099)
XLA Ops:
  0.0 0.0 copy-start
  0.0 2.0 %shard_map.73 = bf16[4,72,768]{2,1,0:T(8,128)(2,1)} custom-call(bf16[64,768]{1,0:T(8,128)(2,1)} %bitcast.12, s32[2,32]{1,0:T(2,128)} %bitcast.14, s32[1,32]{1,0:T(1,128)} %bitcast.15), custom_call_target="tpu_custom_call" | custom-call | flops 2000000000 | bytes 8000000 | tf_op jit(solution)/shard_map/pallas_call | solution.py:277
  2.0 5.0 %all-to-all-start = ((bf16[4,72,768]{2,1,0:T(8,128)(2,1)}), bf16[4,72,768]{2,1,0:T(8,128)(2,1)S(1)}, u32[]{:S(2)}, u32[]{:S(2)}) async-start(bf16[4,72,768]{2,1,0:T(8,128)(2,1)} %shard_map.73), calls=%async_computation | async-start | bytes 884736 | tf_op jit(solution)/shard_map/all_to_all | solution.py:283
  7.0 0.1 pad_add_fusion.place_ref
  7.1 0.0 copy-start.3
  7.1 6.4 %all-to-all-done.normed_ref = bf16[4,72,768]{2,1,0:T(8,128)(2,1)S(1)} async-done(((bf16[4,72,768]{2,1,0:T(8,128)(2,1)}), bf16[4,72,768]{2,1,0:T(8,128)(2,1)S(1)}, u32[]{:S(2)}, u32[]{:S(2)}) %all-to-all-start) | async-done | bytes 442400 | tf_op jit(solution)/shard_map/all_to_all | solution.py:283
  13.5 0.0 copy-done
  13.5 0.0 copy-start.4
  13.5 1.5 %shard_map.74 = (bf16[264,768]{1,0:T(8,128)(2,1)S(1)}, bf16[392,128]{1,0:T(8,128)(2,1)S(1)}) custom-call(s32[4]{0:T(128)S(1)} %pad_add_fusion.place_ref, bf16[4,72,768]{2,1,0:T(8,128)(2,1)S(1)} %all-to-all-done.normed_ref, bf16[768,768]{1,0:T(8,128)(2,1)S(1)} %copy-done), custom_call_target="tpu_custom_call" | custom-call | tf_op jit(solution)/shard_map/pallas_call | solution.py:284
  15.0 5.3 %collective-permute-start.1 = (bf16[264,768]{1,0:T(8,128)(2,1)S(1)}, bf16[264,768]{1,0:T(8,128)(2,1)S(1)}, u32[]{:S(2)}, u32[]{:S(2)}) collective-permute-start(bf16[264,768]{1,0:T(8,128)(2,1)S(1)} %get-tuple-element.15.refs_0_), channel_id=1, source_target_pairs={{0,384},{128,0},{256,128},{384,256},{1,385},{129,1},{257,129},{385... | collective-permute-start | bytes 1216520 | tf_op jit(solution)/shard_map/ppermute | solution.py:295
  20.3 1.9 %collective-permute-start = (bf16[264,768]{1,0:T(8,128)(2,1)S(1)}, bf16[264,768]{1,0:T(8,128)(2,1)S(1)}, u32[]{:S(2)}, u32[]{:S(2)}) collective-permute-start(bf16[264,768]{1,0:T(8,128)(2,1)S(1)} %get-tuple-element.15.refs_0_), channel_id=1, source_target_pairs={{0,128},{128,256},{256,384},{384,0},{1,129},{129,257},{257,385},{3... | collective-permute-start | bytes 1216520 | tf_op jit(solution)/shard_map/ppermute | solution.py:295
  22.2 34.5 %all-gather = bf16[3136,128]{1,0:T(8,128)(2,1)S(1)} all-gather(bf16[392,128]{1,0:T(8,128)(2,1)S(1)} %get-tuple-element.13), channel_id=2, replica_groups={{0,16,32,48,64,80,96,112},{8,24,40,56,72,88,104,120},{1,17,33,49,65,81,..., dimensions={0}, use_global_device_ids=true | all-gather | bytes 903168 | tf_op jit(solution)/shard_map/all_gather | solution.py:299
  56.7 0.0 collective-permute-done.1.refs_3_
  56.7 0.0 collective-permute-done.refs_1_
  56.7 5.2 %collective-permute-start.2 = (bf16[8,392,128]{2,1,0:T(8,128)(2,1)S(1)}, bf16[8,392,128]{2,1,0:T(8,128)(2,1)S(1)}, u32[]{:S(2)}, u32[]{:S(2)}) collective-permute-start(bf16[8,392,128]{2,1,0:T(8,128)(2,1)S(1)} %bitcast.9), channel_id=1, source_target_pairs={{0,8},{4,124},{8,16},{12,4},{16,24},{20,12},{24,32},{28,20},{32,40... | collective-permute-start | bytes 2408456 | tf_op jit(solution)/shard_map/ppermute | solution.py:302
  61.9 1.9 %collective-permute-start.3 = (bf16[264,768]{1,0:T(8,128)(2,1)S(1)}, bf16[264,768]{1,0:T(8,128)(2,1)S(1)}, u32[]{:S(2)}, u32[]{:S(2)}) collective-permute-start(bf16[264,768]{1,0:T(8,128)(2,1)S(1)} %collective-permute-done.refs_1_), channel_id=1, source_target_pairs={{0,128},{128,256},{256,384},{384,0},{1,129},{129,257},{257,385},{3... | collective-permute-start | bytes 1216520 | tf_op jit(solution)/shard_map/ppermute | solution.py:295
  63.8 7.9 %collective-permute-start.4 = (bf16[8,392,128]{2,1,0:T(8,128)(2,1)S(1)}, bf16[8,392,128]{2,1,0:T(8,128)(2,1)S(1)}, u32[]{:S(2)}, u32[]{:S(2)}) collective-permute-start(bf16[8,392,128]{2,1,0:T(8,128)(2,1)S(1)} %bitcast.10), channel_id=1, source_target_pairs={{0,4},{4,0},{1,5},{5,1},{2,6},{6,2},{3,7},{7,3},{8,12},{12,8},{9,1... | collective-permute-start | bytes 2408456 | tf_op jit(solution)/shard_map/ppermute | solution.py:303
  71.7 0.3 collective-permute-done.3.refs_2_
  72.1 0.0 collective-permute-done.2.refs_5_
  72.1 8.9 %collective-permute-start.5 = (bf16[8,392,128]{2,1,0:T(8,128)(2,1)S(1)}, bf16[8,392,128]{2,1,0:T(8,128)(2,1)S(1)}, u32[]{:S(2)}, u32[]{:S(2)}) collective-permute-start(bf16[8,392,128]{2,1,0:T(8,128)(2,1)S(1)} %collective-permute-done.2.refs_5_), channel_id=1, source_target_pairs={{0,4},{4,0},{1,5},{5,1},{2,6},{6,2},{3,7},{7,3},{8,12},{12,8},{9,1... | collective-permute-start | bytes 2408456 | tf_op jit(solution)/shard_map/ppermute | solution.py:305
  81.0 0.0 collective-permute-done.4.refs_6_
  81.0 1.9 %collective-permute-done.5.refs_7_ = bf16[8,392,128]{2,1,0:T(8,128)(2,1)S(1)} collective-permute-done((bf16[8,392,128]{2,1,0:T(8,128)(2,1)S(1)}, bf16[8,392,128]{2,1,0:T(8,128)(2,1)S(1)}, u32[]{:S(2)}, u32[]{:S(2)}) %collective-permute-start.5) | collective-permute-done | bytes 802848 | tf_op jit(solution)/shard_map/ppermute | solution.py:305
  82.9 0.0 copy-done.3
  82.9 0.0 copy-done.4
  82.9 7.4 %shard_map.75 = bf16[16,392,128]{2,1,0:T(8,128)(2,1)S(1)} custom-call(s32[4]{0:T(128)S(1)} %pad_add_fusion.place_ref, bf16[264,768]{1,0:T(8,128)(2,1)S(1)} %get-tuple-element.15.refs_0_, bf16[264,768]{1,0:T(8,128)(2,1)S(1)} %collective-permute-done.refs_1_, bf16[264,768]{1,0:T(8,128)(2,1)S(1)} %collective-permute-done.3.refs_2_, ...), custom_call_target="tpu_custom_call" | custom-call | flops 4000000000 | bytes 10000000 | tf_op jit(solution)/shard_map/pallas_call | solution.py:233
  90.3 0.0 copy-start.1
  90.3 0.0 copy-start.2
  90.3 27.6 %all_to_all.10.arrived_ref = bf16[16,392,128]{2,1,0:T(8,128)(2,1)S(1)} all-to-all(bf16[16,392,128]{2,1,0:T(8,128)(2,1)S(1)} %shard_map.75), channel_id=1, replica_groups=mesh['x'=4,'z'=16,'core'=2,'sub'=4] {'x','sub'}, dimensions={0} | all-to-all | bytes 3211264 | tf_op jit(solution)/shard_map/all_to_all | solution.py:308
  117.9 0.0 copy-done.1
  117.9 0.0 copy-done.2
  117.9 1.1 shard_map.76
Async XLA Ops:
  0.0 13.5 %copy-start = (bf16[768,768]{1,0:T(8,128)(2,1)S(1)}, bf16[768,768]{1,0:T(8,128)(2,1)}, u32[]{:S(2)}) copy-start(bf16[768,768]{1,0:T(8,128)(2,1)} %w_ref.2) | copy-start | bytes 3538948
  2.0 11.5 %all-to-all-start = ((bf16[4,72,768]{2,1,0:T(8,128)(2,1)}), bf16[4,72,768]{2,1,0:T(8,128)(2,1)S(1)}, u32[]{:S(2)}, u32[]{:S(2)}) async-start(bf16[4,72,768]{2,1,0:T(8,128)(2,1)} %shard_map.73), calls=%async_computation | async-start | bytes 884736 | tf_op jit(solution)/shard_map/all_to_all | solution.py:283
  7.1 75.8 %copy-start.3 = (bf16[768,768]{1,0:T(8,128)(2,1)S(1)}, bf16[768,768]{1,0:T(8,128)(2,1)}, u32[]{:S(2)}) copy-start(bf16[768,768]{1,0:T(8,128)(2,1)} %refs_8_.1) | copy-start | bytes 3538948
  13.5 69.4 %copy-start.4 = (bf16[768,768]{1,0:T(8,128)(2,1)S(1)}, bf16[768,768]{1,0:T(8,128)(2,1)}, u32[]{:S(2)}) copy-start(bf16[768,768]{1,0:T(8,128)(2,1)} %refs_9_.1) | copy-start | bytes 3538948
  15.0 41.7 %collective-permute-start.1 = (bf16[264,768]{1,0:T(8,128)(2,1)S(1)}, bf16[264,768]{1,0:T(8,128)(2,1)S(1)}, u32[]{:S(2)}, u32[]{:S(2)}) collective-permute-start(bf16[264,768]{1,0:T(8,128)(2,1)S(1)} %get-tuple-element.15.refs_0_), channel_id=1, source_target_pairs={{0,384},{128,0},{256,128},{384,256},{1,385},{129,1},{257,129},{385... | collective-permute-start | bytes 1216520 | tf_op jit(solution)/shard_map/ppermute | solution.py:295
  20.3 36.4 %collective-permute-start = (bf16[264,768]{1,0:T(8,128)(2,1)S(1)}, bf16[264,768]{1,0:T(8,128)(2,1)S(1)}, u32[]{:S(2)}, u32[]{:S(2)}) collective-permute-start(bf16[264,768]{1,0:T(8,128)(2,1)S(1)} %get-tuple-element.15.refs_0_), channel_id=1, source_target_pairs={{0,128},{128,256},{256,384},{384,0},{1,129},{129,257},{257,385},{3... | collective-permute-start | bytes 1216520 | tf_op jit(solution)/shard_map/ppermute | solution.py:295
  56.7 15.4 %collective-permute-start.2 = (bf16[8,392,128]{2,1,0:T(8,128)(2,1)S(1)}, bf16[8,392,128]{2,1,0:T(8,128)(2,1)S(1)}, u32[]{:S(2)}, u32[]{:S(2)}) collective-permute-start(bf16[8,392,128]{2,1,0:T(8,128)(2,1)S(1)} %bitcast.9), channel_id=1, source_target_pairs={{0,8},{4,124},{8,16},{12,4},{16,24},{20,12},{24,32},{28,20},{32,40... | collective-permute-start | bytes 2408456 | tf_op jit(solution)/shard_map/ppermute | solution.py:302
  61.9 10.2 %collective-permute-start.3 = (bf16[264,768]{1,0:T(8,128)(2,1)S(1)}, bf16[264,768]{1,0:T(8,128)(2,1)S(1)}, u32[]{:S(2)}, u32[]{:S(2)}) collective-permute-start(bf16[264,768]{1,0:T(8,128)(2,1)S(1)} %collective-permute-done.refs_1_), channel_id=1, source_target_pairs={{0,128},{128,256},{256,384},{384,0},{1,129},{129,257},{257,385},{3... | collective-permute-start | bytes 1216520 | tf_op jit(solution)/shard_map/ppermute | solution.py:295
  63.8 17.2 %collective-permute-start.4 = (bf16[8,392,128]{2,1,0:T(8,128)(2,1)S(1)}, bf16[8,392,128]{2,1,0:T(8,128)(2,1)S(1)}, u32[]{:S(2)}, u32[]{:S(2)}) collective-permute-start(bf16[8,392,128]{2,1,0:T(8,128)(2,1)S(1)} %bitcast.10), channel_id=1, source_target_pairs={{0,4},{4,0},{1,5},{5,1},{2,6},{6,2},{3,7},{7,3},{8,12},{12,8},{9,1... | collective-permute-start | bytes 2408456 | tf_op jit(solution)/shard_map/ppermute | solution.py:303
  72.1 10.8 %collective-permute-start.5 = (bf16[8,392,128]{2,1,0:T(8,128)(2,1)S(1)}, bf16[8,392,128]{2,1,0:T(8,128)(2,1)S(1)}, u32[]{:S(2)}, u32[]{:S(2)}) collective-permute-start(bf16[8,392,128]{2,1,0:T(8,128)(2,1)S(1)} %collective-permute-done.2.refs_5_), channel_id=1, source_target_pairs={{0,4},{4,0},{1,5},{5,1},{2,6},{6,2},{3,7},{7,3},{8,12},{12,8},{9,1... | collective-permute-start | bytes 2408456 | tf_op jit(solution)/shard_map/ppermute | solution.py:305
  90.3 27.7 %copy-start.1 = (bf16[768,768]{1,0:T(8,128)(2,1)S(1)}, bf16[768,768]{1,0:T(8,128)(2,1)}, u32[]{:S(2)}) copy-start(bf16[768,768]{1,0:T(8,128)(2,1)} %w_ref.3) | copy-start | bytes 3538948
  90.3 27.6 %copy-start.2 = (bf16[8,8,768]{2,1,0:T(8,128)(2,1)S(1)}, bf16[8,8,768]{2,1,0:T(8,128)(2,1)}, u32[]{:S(2)}) copy-start(bf16[8,8,768]{2,1,0:T(8,128)(2,1)} %param.7) | copy-start | bytes 294916

commit v6 on v5

--- a/solution.py
+++ b/solution.py
@@ -19,6 +19,8 @@
 NY = 2 * BLOCKS
 GROUP = 8
 TILE = 8
+PIECE = BLOCKS // 4
+FIRST_LATE = 2 * PIECE * 3
 INFO = 8
 LIST = NX * NY + GROUP
 LANES = 128
@@ -106,6 +108,26 @@
     return total
 
 
+def project_kernel(piece_ref, w_ref, out_ref):
+    slabs = [
+        jnp.concatenate([piece_ref[j, SLAB * slab : SLAB * (slab + 1), :] for j in range(PIECE)], axis=0)
+        for slab in range(SLABS)
+    ]
+    normed = jnp.concatenate(slabs, axis=1)
+    for columns in (slice(0, D), slice(D, 2 * D)):
+        part = jnp.dot(normed, w_ref[:, columns], preferred_element_type=jnp.float32)
+        out_ref[:, columns] = part.astype(jnp.bfloat16)
+
+
+def project(piece, w_both):
+    return pl.pallas_call(
+        project_kernel,
+        out_shape=jax.ShapeDtypeStruct((PIECE * SLAB, 2 * D), jnp.bfloat16),
+        cost_estimate=pl.CostEstimate(flops=1_200_000_000, bytes_accessed=5_000_000, transcendentals=0),
+        compiler_params=pltpu.CompilerParams(vmem_limit_bytes=16 * 1024 * 1024),
+    )(piece, w_both)
+
+
 def attend_pair(query, keys, values, low_half):
     parts = []
     for j in range(HEADS // 2):
@@ -123,8 +145,9 @@
 
 
 def attend_kernel(place_ref, *refs):
-    query_refs, pieces, (w_key_ref, w_value_ref, out_ref) = refs[:X], refs[X : X + 4], refs[X + 4 : X + 7]
-    all_queries, acc, rows, keys_values, fields, table, listed, sides, scale, count, sem = refs[X + 7 :]
+    query_refs, pieces, ready_refs, refs = refs[:X], refs[X : X + 4], refs[X + 4 : X + 7], refs[X + 7 :]
+    w_ref, out_ref = refs[:2]
+    all_queries, acc, rows, keys_values, fields, table, listed, sides, scale, count, sem = refs[2:]
     total = side_weights(place_ref, query_refs, pieces, fields)
     lane = iota(BLOCKS, 1)
     bits = jnp.where(total > 0, jnp.left_shift(1, lane & 15).astype(jnp.float32), 0.0)
@@ -148,26 +171,34 @@
     acc[...] = jnp.zeros_like(acc)
     for d, ref in enumerate(query_refs):
         all_queries[d * IMG * TOK : (d + 1) * IMG * TOK, :] = ref[0 : IMG * TOK, :]
-    count[0] = 0
-    count[1] = 0
+    for k in range(3):
+        count[k] = 0
     copy.wait()
 
     first_block = 0
-    for ref in pieces:
-
-        def look(j, carry, ref=ref, first_block=first_block):
+    for number, ref in enumerate(pieces):
+
+        def look(j, carry, number=number, ref=ref, first_block=first_block):
             block = first_block + j
             for k in range(2):
                 mask = listed[block, 2 * NX + 2 * k] | (listed[block, 2 * NX + 2 * k + 1] << 16)
 
                 @pl.when(mask != 0)
                 def _():
-                    slot = count[0]
-                    count[0] = slot + 1
-                    here = pl.ds(pl.multiple_of(slot * TOK, TOK), TOK)
-                    for slab in range(SLABS):
-                        first = SLAB * slab + TOK * k
-                        rows[here, LANES * slab : LANES * (slab + 1)] = ref[j, first : first + TOK, :]
+                    if number < len(ready_refs):
+                        slot = count[0]
+                        count[0] = slot + 1
+                        here = pl.ds(pl.multiple_of(slot * TOK, TOK), TOK)
+                        there = pl.ds(pl.multiple_of(j * SLAB + k * TOK, TOK), TOK)
+                        keys_values[here, :] = ready_refs[number][there, :]
+                    else:
+                        late = count[2]
+                        count[2] = late + 1
+                        slot = FIRST_LATE + late
+                        here = pl.ds(pl.multiple_of(late * TOK, TOK), TOK)
+                        for slab in range(SLABS):
+                            first = SLAB * slab + TOK * k
+                            rows[here, LANES * slab : LANES * (slab + 1)] = ref[j, first : first + TOK, :]
 
                     def more(state):
                         return state[0] != 0
@@ -191,15 +222,15 @@
         scale[found + k] = 0.0
 
     def project(t, carry):
-        some = pl.ds(pl.multiple_of(t * (TILE * TOK), TILE * TOK), TILE * TOK)
-        normed = rows[some, :]
-        keys_values[some, 0:D] = jnp.dot(normed, w_key_ref[...], preferred_element_type=jnp.float32).astype(jnp.bfloat16)
-        keys_values[some, D : 2 * D] = jnp.dot(normed, w_value_ref[...], preferred_element_type=jnp.float32).astype(
-            jnp.bfloat16
-        )
+        start = pl.multiple_of(t * (TILE * TOK), TILE * TOK)
+        normed = rows[pl.ds(start, TILE * TOK), :]
+        some = pl.ds(FIRST_LATE * TOK + start, TILE * TOK)
+        for columns in (slice(0, D), slice(D, 2 * D)):
+            part = jnp.dot(normed, w_ref[:, columns], preferred_element_type=jnp.float32)
+            keys_values[some, columns] = part.astype(jnp.bfloat16)
         return carry
 
-    lax.fori_loop(0, (count[0] + TILE - 1) // TILE, project, 0)
+    lax.fori_loop(0, (count[2] + TILE - 1) // TILE, project, 0)
     low_half = lax.broadcasted_iota(INT, (TOK, 2 * HEAD), 1) < HEAD
 
     def one_side(n):
@@ -229,28 +260,28 @@
                     out_ref[place + s, row : row + 2 * ROWS, :] = block[:, LANES * slab : LANES * (slab + 1)]
 
 
-def attend(place, queries, pieces, w_key, w_value):
+def attend(place, queries, pieces, ready, w_both):
     return pl.pallas_call(
         attend_kernel,
         out_shape=jax.ShapeDtypeStruct((X * SUB, FILL + INFO, LANES), jnp.bfloat16),
-        in_specs=[SMEM] + [VMEM] * (len(queries) + len(pieces) + 2),
+        in_specs=[SMEM] + [VMEM] * (len(queries) + len(pieces) + len(ready) + 1),
         out_specs=VMEM,
         scratch_shapes=[
             pltpu.VMEM((NX * TOK, D), jnp.bfloat16),
             pltpu.VMEM((NX * TOK, D), jnp.float32),
-            pltpu.VMEM((NY * TOK, D), jnp.bfloat16),
+            pltpu.VMEM((2 * PIECE * TOK, D), jnp.bfloat16),
             pltpu.VMEM((NY * TOK, 2 * D), jnp.bfloat16),
             pltpu.VMEM((BLOCKS * INFO, LANES), jnp.float32),
             pltpu.VMEM((BLOCKS, LANES), INT),
             pltpu.SMEM((BLOCKS, LANES), INT),
             pltpu.SMEM((LIST,), INT),
             pltpu.SMEM((LIST,), jnp.float32),
-            pltpu.SMEM((2,), INT),
+            pltpu.SMEM((3,), INT),
             pltpu.SemaphoreType.DMA,
         ],
         cost_estimate=pl.CostEstimate(flops=4_000_000_000, bytes_accessed=10_000_000, transcendentals=800_000),
         compiler_params=pltpu.CompilerParams(vmem_limit_bytes=36 * 1024 * 1024),
-    )(place, *queries, *pieces, w_key, w_value)
+    )(place, *queries, *pieces, *ready, w_both)
 
 
 def finish_kernel(arrived_ref, tokens_ref, w_ref, out_ref):
@@ -280,6 +311,7 @@
         scratch_shapes=[pltpu.VMEM((INFO, D), jnp.float32)],
         cost_estimate=pl.CostEstimate(flops=2_000_000_000, bytes_accessed=8_000_000, transcendentals=64),
     )(tokens, pairs.T, confidence.reshape(1, PAIR))
+    w_both = jnp.concatenate([w_key, w_value], axis=1)
     normed = lax.all_to_all(copies, "sub", split_axis=0, concat_axis=0, tiled=True)
     queries, block = pl.pallas_call(
         query_kernel,
@@ -301,10 +333,12 @@
     there = [(z * CORE + c, (z + 1 - 2 * c) % Z * CORE + c) for z in range(Z) for c in range(CORE)]
     other = lax.ppermute(same, ("z", "core"), there)
     same_far = lax.ppermute(same, "core", [(0, 1), (1, 0)])
-    other, across = lax.optimization_barrier((other, along_x(below, 1)))
-    pieces = [same, other, same_far, lax.ppermute(other, "core", [(0, 1), (1, 0)])]
+    other, across, ready = lax.optimization_barrier((other, along_x(below, 1), project(same, w_both)))
+    other_far = lax.ppermute(other, "core", [(0, 1), (1, 0)])
+    pieces = [same, other, same_far, other_far]
+    ready = [ready, project(other, w_both), project(same_far, w_both)]
     queries = [queries, below, across, above]
-    sent = attend(place, queries, pieces, w_key, w_value)
+    sent = attend(place, queries, pieces, ready, w_both)
     arrived = lax.all_to_all(sent, ("x", "sub"), split_axis=0, concat_axis=0, tiled=True)
     decoded = pl.pallas_call(
         finish_kernel,

time: 120 us -> 122 us (1.017)
  Pallas kernels: 12 us -> 18 us
  waiting for transfers between devices: 8.66 us -> 6.43 us
    pallas_call x0 -> x3, Pallas kernels: none -> 4.18 us  [project(): pl.pallas_call(project_kernel, out_shape=jax.ShapeDtypeStruct((PIECE * SL...]
    ppermute x1, waiting for transfers between devices: 1.9 us -> 0.01 us  [body(): other_far = lax.ppermute(other, 'core', [(0, 1), (1, 0)])]
    pallas_call x1, Pallas kernels: 7.36 us -> 9.21 us  [attend(): pl.pallas_call(attend_kernel, out_shape=jax.ShapeDtypeStruct((X * SUB, FI...]
  transfers between devices with their start and end apart: 7 -> 7, of which waited for: 3 -> 1; matrix products, arithmetic and copies ran while one was open for 0% -> 0% of each run, Pallas kernels for 0% -> 3%
where the time goes in v6:
time: 122 us
  blocking collectives  61 us (50%)
  starting transfers between devices  35.9 us (29%)
  Pallas kernels  18 us (15%)
  waiting for transfers between devices  6.43 us (5%)
    all_gather x1, blocking collectives, body(): lax.all_gather(block, 'z', axis=0, tiled=False, axis_index_groups=groups)  34.4 us
    all_to_all x1, blocking collectives, body(): lax.all_to_all(sent, ('x', 'sub'), split_axis=0, concat_axis=0, tiled=True)  26.6 us
    ppermute x3, starting transfers between devices, along_x(): return lax.ppermute(rows, 'x', [(i, (i + d) % X) for i in range(X)])  9.81 us
    pallas_call x1, Pallas kernels, attend(): pl.pallas_call(attend_kernel, out_shape=jax.ShapeDtypeStruct((X * SUB, FI...  9.21 us
    ppermute x1, starting transfers between devices, body(): same_far = lax.ppermute(same, 'core', [(0, 1), (1, 0)])  8.21 us
    ppermute x1, starting transfers between devices, body(): other_far = lax.ppermute(other, 'core', [(0, 1), (1, 0)])  8.09 us
    all_to_all x1, waiting for transfers between devices, body(): lax.all_to_all(copies, 'sub', split_axis=0, concat_axis=0, tiled=True)  6.42 us
    all_to_all x1, starting transfers between devices, body(): lax.all_to_all(copies, 'sub', split_axis=0, concat_axis=0, tiled=True)  5.14 us
  transfers between devices with their start and end apart: 7, of which 1 were waited for; matrix products, arithmetic and copies ran while one was open for 0% of the time, Pallas kernels for 3%

profile of v6, /device:TPU:1, one launch (start us, length us, event | category | flops | bytes accessed | tf_op | source)
XLA Modules:
  0.0 121.8 jit_solution(3842439634370499488)
XLA Ops:
  0.0 0.0 copy-start
  0.0 2.0 %shard_map.73 = bf16[4,72,768]{2,1,0:T(8,128)(2,1)} custom-call(bf16[64,768]{1,0:T(8,128)(2,1)} %bitcast.13, s32[2,32]{1,0:T(2,128)} %bitcast.15, s32[1,32]{1,0:T(1,128)} %bitcast.16), custom_call_target="tpu_custom_call" | custom-call | flops 2000000000 | bytes 8000000 | tf_op jit(solution)/shard_map/pallas_call | solution.py:308
  2.0 0.0 copy-start.3
  2.0 5.1 %all-to-all-start = ((bf16[4,72,768]{2,1,0:T(8,128)(2,1)}), bf16[4,72,768]{2,1,0:T(8,128)(2,1)S(1)}, u32[]{:S(2)}, u32[]{:S(2)}) async-start(bf16[4,72,768]{2,1,0:T(8,128)(2,1)} %shard_map.73), calls=%async_computation | async-start | bytes 884736 | tf_op jit(solution)/shard_map/all_to_all | solution.py:315
  7.1 0.1 pad_add_fusion.place_ref
  7.2 6.4 %all-to-all-done.normed_ref = bf16[4,72,768]{2,1,0:T(8,128)(2,1)S(1)} async-done(((bf16[4,72,768]{2,1,0:T(8,128)(2,1)}), bf16[4,72,768]{2,1,0:T(8,128)(2,1)S(1)}, u32[]{:S(2)}, u32[]{:S(2)}) %all-to-all-start) | async-done | bytes 442400 | tf_op jit(solution)/shard_map/all_to_all | solution.py:315
  13.6 0.0 copy-done
  13.6 1.5 %shard_map.74 = (bf16[264,768]{1,0:T(8,128)(2,1)S(1)}, bf16[392,128]{1,0:T(8,128)(2,1)S(1)}) custom-call(s32[4]{0:T(128)S(1)} %pad_add_fusion.place_ref, bf16[4,72,768]{2,1,0:T(8,128)(2,1)S(1)} %all-to-all-done.normed_ref, bf16[768,768]{1,0:T(8,128)(2,1)S(1)} %copy-done), custom_call_target="tpu_custom_call" | custom-call | tf_op jit(solution)/shard_map/pallas_call | solution.py:316
  15.1 5.3 %collective-permute-start.1 = (bf16[264,768]{1,0:T(8,128)(2,1)S(1)}, bf16[264,768]{1,0:T(8,128)(2,1)S(1)}, u32[]{:S(2)}, u32[]{:S(2)}) collective-permute-start(bf16[264,768]{1,0:T(8,128)(2,1)S(1)} %get-tuple-element.16.refs_0_), channel_id=1, source_target_pairs={{0,384},{128,0},{256,128},{384,256},{1,385},{129,1},{257,129},{385... | collective-permute-start | bytes 1216520 | tf_op jit(solution)/shard_map/ppermute | solution.py:327
  20.4 1.9 %collective-permute-start = (bf16[264,768]{1,0:T(8,128)(2,1)S(1)}, bf16[264,768]{1,0:T(8,128)(2,1)S(1)}, u32[]{:S(2)}, u32[]{:S(2)}) collective-permute-start(bf16[264,768]{1,0:T(8,128)(2,1)S(1)} %get-tuple-element.16.refs_0_), channel_id=1, source_target_pairs={{0,128},{128,256},{256,384},{384,0},{1,129},{129,257},{257,385},{3... | collective-permute-start | bytes 1216520 | tf_op jit(solution)/shard_map/ppermute | solution.py:327
  22.4 0.0 copy-start.4
  22.4 34.4 %all-gather = bf16[3136,128]{1,0:T(8,128)(2,1)S(1)} all-gather(bf16[392,128]{1,0:T(8,128)(2,1)S(1)} %get-tuple-element.14), channel_id=2, replica_groups={{0,16,32,48,64,80,96,112},{8,24,40,56,72,88,104,120},{1,17,33,49,65,81,..., dimensions={0}, use_global_device_ids=true | all-gather | bytes 903168 | tf_op jit(solution)/shard_map/all_gather | solution.py:331
  56.8 0.0 collective-permute-done.1.refs_3_
  56.8 0.0 collective-permute-done.refs_1_
  56.8 4.6 %collective-permute-start.2 = (bf16[8,392,128]{2,1,0:T(8,128)(2,1)S(1)}, bf16[8,392,128]{2,1,0:T(8,128)(2,1)S(1)}, u32[]{:S(2)}, u32[]{:S(2)}) collective-permute-start(bf16[8,392,128]{2,1,0:T(8,128)(2,1)S(1)} %bitcast.9), channel_id=1, source_target_pairs={{0,8},{4,124},{8,16},{12,4},{16,24},{20,12},{24,32},{28,20},{32,40... | collective-permute-start | bytes 2408456 | tf_op jit(solution)/shard_map/ppermute | solution.py:334
  61.4 2.6 %collective-permute-start.3 = (bf16[264,768]{1,0:T(8,128)(2,1)S(1)}, bf16[264,768]{1,0:T(8,128)(2,1)S(1)}, u32[]{:S(2)}, u32[]{:S(2)}) collective-permute-start(bf16[264,768]{1,0:T(8,128)(2,1)S(1)} %collective-permute-done.refs_1_), channel_id=1, source_target_pairs={{0,128},{128,256},{256,384},{384,0},{1,129},{129,257},{257,385},{3... | collective-permute-start | bytes 1216520 | tf_op jit(solution)/shard_map/ppermute | solution.py:327
  64.0 0.0 copy-done.3
  64.1 0.1 constant_dynamic-update-slice_fusion.1
  64.1 0.0 copy-done.4
  64.2 0.1 constant_dynamic-update-slice_fusion.w_ref.refs_11_
  64.2 8.2 %collective-permute-start.4 = (bf16[8,392,128]{2,1,0:T(8,128)(2,1)S(1)}, bf16[8,392,128]{2,1,0:T(8,128)(2,1)S(1)}, u32[]{:S(2)}, u32[]{:S(2)}) collective-permute-start(bf16[8,392,128]{2,1,0:T(8,128)(2,1)S(1)} %bitcast.10), channel_id=1, source_target_pairs={{0,4},{4,0},{1,5},{5,1},{2,6},{6,2},{3,7},{7,3},{8,12},{12,8},{9,1... | collective-permute-start | bytes 2408456 | tf_op jit(solution)/shard_map/ppermute | solution.py:335
  72.5 1.4 %shard_map.75.refs_8_ = bf16[512,1536]{1,0:T(8,128)(2,1)S(1)} custom-call(bf16[8,392,128]{2,1,0:T(8,128)(2,1)S(1)} %bitcast.11, bf16[768,1536]{1,0:T(8,128)(2,1)S(1)} %constant_dynamic-update-slice_fusion.w_ref.refs_11_), custom_call_target="tpu_custom_call" | custom-call | flops 1200000000 | bytes 5000000 | tf_op jit(solution)/shard_map/pallas_call | solution.py:123
  73.9 0.0 collective-permute-done.3.refs_2_
  73.9 0.0 collective-permute-done.2.piece_ref.refs_5_
  73.9 8.1 %collective-permute-start.5 = (bf16[8,392,128]{2,1,0:T(8,128)(2,1)S(1)}, bf16[8,392,128]{2,1,0:T(8,128)(2,1)S(1)}, u32[]{:S(2)}, u32[]{:S(2)}) collective-permute-start(bf16[8,392,128]{2,1,0:T(8,128)(2,1)S(1)} %collective-permute-done.2.piece_ref.refs_5_), channel_id=1, source_target_pairs={{0,4},{4,0},{1,5},{5,1},{2,6},{6,2},{3,7},{7,3},{8,12},{12,8},{9,1... | collective-permute-start | bytes 2408456 | tf_op jit(solution)/shard_map/ppermute | solution.py:337
  82.0 1.4 %shard_map.76.refs_9_ = bf16[512,1536]{1,0:T(8,128)(2,1)S(1)} custom-call(bf16[8,392,128]{2,1,0:T(8,128)(2,1)S(1)} %collective-permute-done.2.piece_ref.refs_5_, bf16[768,1536]{1,0:T(8,128)(2,1)S(1)} %constant_dynamic-update-slice_fusion.w_ref.refs_11_), custom_call_target="tpu_custom_call" | custom-call | flops 1200000000 | bytes 5000000 | tf_op jit(solution)/shard_map/pallas_call | solution.py:123
  83.4 0.0 collective-permute-done.4.piece_ref.refs_6_
  83.4 1.4 %shard_map.77.refs_10_ = bf16[512,1536]{1,0:T(8,128)(2,1)S(1)} custom-call(bf16[8,392,128]{2,1,0:T(8,128)(2,1)S(1)} %collective-permute-done.4.piece_ref.refs_6_, bf16[768,1536]{1,0:T(8,128)(2,1)S(1)} %constant_dynamic-update-slice_fusion.w_ref.refs_11_), custom_call_target="tpu_custom_call" | custom-call | flops 1200000000 | bytes 5000000 | tf_op jit(solution)/shard_map/pallas_call | solution.py:123
  84.8 0.0 collective-permute-done.5.refs_7_
  84.8 9.2 %shard_map.78 = bf16[16,392,128]{2,1,0:T(8,128)(2,1)S(1)} custom-call(s32[4]{0:T(128)S(1)} %pad_add_fusion.place_ref, bf16[264,768]{1,0:T(8,128)(2,1)S(1)} %get-tuple-element.16.refs_0_, bf16[264,768]{1,0:T(8,128)(2,1)S(1)} %collective-permute-done.refs_1_, bf16[264,768]{1,0:T(8,128)(2,1)S(1)} %collective-permute-done.3.refs_2_, ...), custom_call_target="tpu_custom_call" | custom-call | flops 4000000000 | bytes 10000000 | tf_op jit(solution)/shard_map/pallas_call | solution.py:264
  94.0 0.0 copy-start.1
  94.0 0.0 copy-start.2
  94.0 26.6 %all_to_all.10.arrived_ref = bf16[16,392,128]{2,1,0:T(8,128)(2,1)S(1)} all-to-all(bf16[16,392,128]{2,1,0:T(8,128)(2,1)S(1)} %shard_map.78), channel_id=1, replica_groups=mesh['x'=4,'z'=16,'core'=2,'sub'=4] {'x','sub'}, dimensions={0} | all-to-all | bytes 3211264 | tf_op jit(solution)/shard_map/all_to_all | solution.py:342
  120.6 0.0 copy-done.1
  120.6 0.0 copy-done.2
  120.6 1.1 shard_map.79
Async XLA Ops:
  0.0 13.6 %copy-start = (bf16[768,768]{1,0:T(8,128)(2,1)S(1)}, bf16[768,768]{1,0:T(8,128)(2,1)}, u32[]{:S(2)}) copy-start(bf16[768,768]{1,0:T(8,128)(2,1)} %w_ref.2) | copy-start | bytes 3538948
  2.0 62.1 %copy-start.3 = (bf16[768,768]{1,0:T(8,128)(2,1)S(1)}, bf16[768,768]{1,0:T(8,128)(2,1)}, u32[]{:S(2)}) copy-start(bf16[768,768]{1,0:T(8,128)(2,1)} %param.11) | copy-start | bytes 3538948
  2.0 11.6 %all-to-all-start = ((bf16[4,72,768]{2,1,0:T(8,128)(2,1)}), bf16[4,72,768]{2,1,0:T(8,128)(2,1)S(1)}, u32[]{:S(2)}, u32[]{:S(2)}) async-start(bf16[4,72,768]{2,1,0:T(8,128)(2,1)} %shard_map.73), calls=%async_computation | async-start | bytes 884736 | tf_op jit(solution)/shard_map/all_to_all | solution.py:315
  15.1 41.7 %collective-permute-start.1 = (bf16[264,768]{1,0:T(8,128)(2,1)S(1)}, bf16[264,768]{1,0:T(8,128)(2,1)S(1)}, u32[]{:S(2)}, u32[]{:S(2)}) collective-permute-start(bf16[264,768]{1,0:T(8,128)(2,1)S(1)} %get-tuple-element.16.refs_0_), channel_id=1, source_target_pairs={{0,384},{128,0},{256,128},{384,256},{1,385},{129,1},{257,129},{385... | collective-permute-start | bytes 1216520 | tf_op jit(solution)/shard_map/ppermute | solution.py:327
  20.4 36.4 %collective-permute-start = (bf16[264,768]{1,0:T(8,128)(2,1)S(1)}, bf16[264,768]{1,0:T(8,128)(2,1)S(1)}, u32[]{:S(2)}, u32[]{:S(2)}) collective-permute-start(bf16[264,768]{1,0:T(8,128)(2,1)S(1)} %get-tuple-element.16.refs_0_), channel_id=1, source_target_pairs={{0,128},{128,256},{256,384},{384,0},{1,129},{129,257},{257,385},{3... | collective-permute-start | bytes 1216520 | tf_op jit(solution)/shard_map/ppermute | solution.py:327
  22.4 41.8 %copy-start.4 = (bf16[768,768]{1,0:T(8,128)(2,1)S(1)}, bf16[768,768]{1,0:T(8,128)(2,1)}, u32[]{:S(2)}) copy-start(bf16[768,768]{1,0:T(8,128)(2,1)} %param.12) | copy-start | bytes 3538948
  56.8 17.1 %collective-permute-start.2 = (bf16[8,392,128]{2,1,0:T(8,128)(2,1)S(1)}, bf16[8,392,128]{2,1,0:T(8,128)(2,1)S(1)}, u32[]{:S(2)}, u32[]{:S(2)}) collective-permute-start(bf16[8,392,128]{2,1,0:T(8,128)(2,1)S(1)} %bitcast.9), channel_id=1, source_target_pairs={{0,8},{4,124},{8,16},{12,4},{16,24},{20,12},{24,32},{28,20},{32,40... | collective-permute-start | bytes 2408456 | tf_op jit(solution)/shard_map/ppermute | solution.py:334
  61.4 12.4 %collective-permute-start.3 = (bf16[264,768]{1,0:T(8,128)(2,1)S(1)}, bf16[264,768]{1,0:T(8,128)(2,1)S(1)}, u32[]{:S(2)}, u32[]{:S(2)}) collective-permute-start(bf16[264,768]{1,0:T(8,128)(2,1)S(1)} %collective-permute-done.refs_1_), channel_id=1, source_target_pairs={{0,128},{128,256},{256,384},{384,0},{1,129},{129,257},{257,385},{3... | collective-permute-start | bytes 1216520 | tf_op jit(solution)/shard_map/ppermute | solution.py:327
  64.2 19.2 %collective-permute-start.4 = (bf16[8,392,128]{2,1,0:T(8,128)(2,1)S(1)}, bf16[8,392,128]{2,1,0:T(8,128)(2,1)S(1)}, u32[]{:S(2)}, u32[]{:S(2)}) collective-permute-start(bf16[8,392,128]{2,1,0:T(8,128)(2,1)S(1)} %bitcast.10), channel_id=1, source_target_pairs={{0,4},{4,0},{1,5},{5,1},{2,6},{6,2},{3,7},{7,3},{8,12},{12,8},{9,1... | collective-permute-start | bytes 2408456 | tf_op jit(solution)/shard_map/ppermute | solution.py:335
  73.9 10.9 %collective-permute-start.5 = (bf16[8,392,128]{2,1,0:T(8,128)(2,1)S(1)}, bf16[8,392,128]{2,1,0:T(8,128)(2,1)S(1)}, u32[]{:S(2)}, u32[]{:S(2)}) collective-permute-start(bf16[8,392,128]{2,1,0:T(8,128)(2,1)S(1)} %collective-permute-done.2.piece_ref.refs_5_), channel_id=1, source_target_pairs={{0,4},{4,0},{1,5},{5,1},{2,6},{6,2},{3,7},{7,3},{8,12},{12,8},{9,1... | collective-permute-start | bytes 2408456 | tf_op jit(solution)/shard_map/ppermute | solution.py:337
  94.0 26.6 %copy-start.1 = (bf16[768,768]{1,0:T(8,128)(2,1)S(1)}, bf16[768,768]{1,0:T(8,128)(2,1)}, u32[]{:S(2)}) copy-start(bf16[768,768]{1,0:T(8,128)(2,1)} %w_ref.3) | copy-start | bytes 3538948
  94.0 26.6 %copy-start.2 = (bf16[8,8,768]{2,1,0:T(8,128)(2,1)S(1)}, bf16[8,8,768]{2,1,0:T(8,128)(2,1)}, u32[]{:S(2)}) copy-start(bf16[8,8,768]{2,1,0:T(8,128)(2,1)} %param.7) | copy-start | bytes 294916

commit v7 on v6

--- a/solution.py
+++ b/solution.py
@@ -217,8 +217,9 @@
         lax.fori_loop(0, ref.shape[0], look, 0)
         first_block += ref.shape[0]
     found = count[1]
+    last = sides[jnp.maximum(found - 1, 0)]
     for k in range(GROUP):
-        sides[found + k] = 0
+        sides[found + k] = last
         scale[found + k] = 0.0
 
     def project(t, carry):
@@ -240,13 +241,22 @@
         mixed = attend_pair(all_queries[mine, :], keys_values[slot, 0:D], keys_values[slot, D : 2 * D], low_half)
         return mine, scale[n] * mixed
 
-    def step(g, carry):
-        results = [one_side(g * GROUP + k) for k in range(GROUP)]
+    def some_sides(first, number):
+        results = [one_side(first + k) for k in range(number)]
         for mine, mixed in results:
             acc[mine, :] = acc[mine, :] + mixed
+
+    def step(g, carry):
+        some_sides(g * GROUP, GROUP)
         return carry
 
-    lax.fori_loop(0, (found + GROUP - 1) // GROUP, step, 0)
+    full = found // GROUP
+    rest = found - full * GROUP
+    lax.fori_loop(0, full + jnp.where(rest > GROUP // 2, 1, 0), step, 0)
+
+    @pl.when((rest > 0) & (rest <= GROUP // 2))
+    def _():
+        some_sides(full * GROUP, GROUP // 2)
 
     for d in range(X):
         place = ((place_ref[0] + (X - d)) & (X - 1)) * SUB

time: 122 us -> 121 us (level)
  no operation moved by 1% of the time
where the time goes in v7:
time: 121 us
  blocking collectives  60.6 us (50%)
  starting transfers between devices  35.9 us (30%)
  Pallas kernels  17.6 us (15%)
  waiting for transfers between devices  6.43 us (5%)
    all_gather x1, blocking collectives, body(): lax.all_gather(block, 'z', axis=0, tiled=False, axis_index_groups=groups)  34.4 us
    all_to_all x1, blocking collectives, body(): lax.all_to_all(sent, ('x', 'sub'), split_axis=0, concat_axis=0, tiled=True)  26.2 us
    ppermute x3, starting transfers between devices, along_x(): return lax.ppermute(rows, 'x', [(i, (i + d) % X) for i in range(X)])  9.81 us
    pallas_call x1, Pallas kernels, attend(): pl.pallas_call(attend_kernel, out_shape=jax.ShapeDtypeStruct((X * SUB, FI...  8.8 us
    ppermute x1, starting transfers between devices, body(): same_far = lax.ppermute(same, 'core', [(0, 1), (1, 0)])  8.21 us
    ppermute x1, starting transfers between devices, body(): other_far = lax.ppermute(other, 'core', [(0, 1), (1, 0)])  8.09 us
    all_to_all x1, waiting for transfers between devices, body(): lax.all_to_all(copies, 'sub', split_axis=0, concat_axis=0, tiled=True)  6.42 us
    all_to_all x1, starting transfers between devices, body(): lax.all_to_all(copies, 'sub', split_axis=0, concat_axis=0, tiled=True)  5.14 us
  transfers between devices with their start and end apart: 7, of which 1 were waited for; matrix products, arithmetic and copies ran while one was open for 0% of the time, Pallas kernels for 3%

profile of v7, /device:TPU:1, one launch (start us, length us, event | category | flops | bytes accessed | tf_op | source)
XLA Modules:
  0.0 121.0 jit_solution(15358203088878760247)
XLA Ops:
  0.0 0.0 copy-start
  0.0 2.0 %shard_map.73 = bf16[4,72,768]{2,1,0:T(8,128)(2,1)} custom-call(bf16[64,768]{1,0:T(8,128)(2,1)} %bitcast.13, s32[2,32]{1,0:T(2,128)} %bitcast.15, s32[1,32]{1,0:T(1,128)} %bitcast.16), custom_call_target="tpu_custom_call" | custom-call | flops 2000000000 | bytes 8000000 | tf_op jit(solution)/shard_map/pallas_call | solution.py:318
  2.0 0.0 copy-start.3
  2.0 5.1 %all-to-all-start = ((bf16[4,72,768]{2,1,0:T(8,128)(2,1)}), bf16[4,72,768]{2,1,0:T(8,128)(2,1)S(1)}, u32[]{:S(2)}, u32[]{:S(2)}) async-start(bf16[4,72,768]{2,1,0:T(8,128)(2,1)} %shard_map.73), calls=%async_computation | async-start | bytes 884736 | tf_op jit(solution)/shard_map/all_to_all | solution.py:325
  7.1 0.1 pad_add_fusion.place_ref
  7.2 6.4 %all-to-all-done.normed_ref = bf16[4,72,768]{2,1,0:T(8,128)(2,1)S(1)} async-done(((bf16[4,72,768]{2,1,0:T(8,128)(2,1)}), bf16[4,72,768]{2,1,0:T(8,128)(2,1)S(1)}, u32[]{:S(2)}, u32[]{:S(2)}) %all-to-all-start) | async-done | bytes 442400 | tf_op jit(solution)/shard_map/all_to_all | solution.py:325
  13.6 0.0 copy-done
  13.6 1.5 %shard_map.74 = (bf16[264,768]{1,0:T(8,128)(2,1)S(1)}, bf16[392,128]{1,0:T(8,128)(2,1)S(1)}) custom-call(s32[4]{0:T(128)S(1)} %pad_add_fusion.place_ref, bf16[4,72,768]{2,1,0:T(8,128)(2,1)S(1)} %all-to-all-done.normed_ref, bf16[768,768]{1,0:T(8,128)(2,1)S(1)} %copy-done), custom_call_target="tpu_custom_call" | custom-call | tf_op jit(solution)/shard_map/pallas_call | solution.py:326
  15.1 5.3 %collective-permute-start.1 = (bf16[264,768]{1,0:T(8,128)(2,1)S(1)}, bf16[264,768]{1,0:T(8,128)(2,1)S(1)}, u32[]{:S(2)}, u32[]{:S(2)}) collective-permute-start(bf16[264,768]{1,0:T(8,128)(2,1)S(1)} %get-tuple-element.16.refs_0_), channel_id=1, source_target_pairs={{0,384},{128,0},{256,128},{384,256},{1,385},{129,1},{257,129},{385... | collective-permute-start | bytes 1216520 | tf_op jit(solution)/shard_map/ppermute | solution.py:337
  20.4 1.9 %collective-permute-start = (bf16[264,768]{1,0:T(8,128)(2,1)S(1)}, bf16[264,768]{1,0:T(8,128)(2,1)S(1)}, u32[]{:S(2)}, u32[]{:S(2)}) collective-permute-start(bf16[264,768]{1,0:T(8,128)(2,1)S(1)} %get-tuple-element.16.refs_0_), channel_id=1, source_target_pairs={{0,128},{128,256},{256,384},{384,0},{1,129},{129,257},{257,385},{3... | collective-permute-start | bytes 1216520 | tf_op jit(solution)/shard_map/ppermute | solution.py:337
  22.4 0.0 copy-start.4
  22.4 34.4 %all-gather = bf16[3136,128]{1,0:T(8,128)(2,1)S(1)} all-gather(bf16[392,128]{1,0:T(8,128)(2,1)S(1)} %get-tuple-element.14), channel_id=2, replica_groups={{0,16,32,48,64,80,96,112},{8,24,40,56,72,88,104,120},{1,17,33,49,65,81,..., dimensions={0}, use_global_device_ids=true | all-gather | bytes 903168 | tf_op jit(solution)/shard_map/all_gather | solution.py:341
  56.8 0.0 collective-permute-done.1.refs_3_
  56.8 0.0 collective-permute-done.refs_1_
  56.8 4.6 %collective-permute-start.2 = (bf16[8,392,128]{2,1,0:T(8,128)(2,1)S(1)}, bf16[8,392,128]{2,1,0:T(8,128)(2,1)S(1)}, u32[]{:S(2)}, u32[]{:S(2)}) collective-permute-start(bf16[8,392,128]{2,1,0:T(8,128)(2,1)S(1)} %bitcast.9), channel_id=1, source_target_pairs={{0,8},{4,124},{8,16},{12,4},{16,24},{20,12},{24,32},{28,20},{32,40... | collective-permute-start | bytes 2408456 | tf_op jit(solution)/shard_map/ppermute | solution.py:344
  61.4 2.6 %collective-permute-start.3 = (bf16[264,768]{1,0:T(8,128)(2,1)S(1)}, bf16[264,768]{1,0:T(8,128)(2,1)S(1)}, u32[]{:S(2)}, u32[]{:S(2)}) collective-permute-start(bf16[264,768]{1,0:T(8,128)(2,1)S(1)} %collective-permute-done.refs_1_), channel_id=1, source_target_pairs={{0,128},{128,256},{256,384},{384,0},{1,129},{129,257},{257,385},{3... | collective-permute-start | bytes 1216520 | tf_op jit(solution)/shard_map/ppermute | solution.py:337
  64.0 0.0 copy-done.3
  64.1 0.1 constant_dynamic-update-slice_fusion.1
  64.1 0.0 copy-done.4
  64.2 0.1 constant_dynamic-update-slice_fusion.w_ref.refs_11_
  64.2 8.2 %collective-permute-start.4 = (bf16[8,392,128]{2,1,0:T(8,128)(2,1)S(1)}, bf16[8,392,128]{2,1,0:T(8,128)(2,1)S(1)}, u32[]{:S(2)}, u32[]{:S(2)}) collective-permute-start(bf16[8,392,128]{2,1,0:T(8,128)(2,1)S(1)} %bitcast.10), channel_id=1, source_target_pairs={{0,4},{4,0},{1,5},{5,1},{2,6},{6,2},{3,7},{7,3},{8,12},{12,8},{9,1... | collective-permute-start | bytes 2408456 | tf_op jit(solution)/shard_map/ppermute | solution.py:345
  72.5 1.4 %shard_map.75.refs_8_ = bf16[512,1536]{1,0:T(8,128)(2,1)S(1)} custom-call(bf16[8,392,128]{2,1,0:T(8,128)(2,1)S(1)} %bitcast.11, bf16[768,1536]{1,0:T(8,128)(2,1)S(1)} %constant_dynamic-update-slice_fusion.w_ref.refs_11_), custom_call_target="tpu_custom_call" | custom-call | flops 1200000000 | bytes 5000000 | tf_op jit(solution)/shard_map/pallas_call | solution.py:123
  73.9 0.0 collective-permute-done.3.refs_2_
  73.9 0.0 collective-permute-done.2.piece_ref.refs_5_
  73.9 8.1 %collective-permute-start.5 = (bf16[8,392,128]{2,1,0:T(8,128)(2,1)S(1)}, bf16[8,392,128]{2,1,0:T(8,128)(2,1)S(1)}, u32[]{:S(2)}, u32[]{:S(2)}) collective-permute-start(bf16[8,392,128]{2,1,0:T(8,128)(2,1)S(1)} %collective-permute-done.2.piece_ref.refs_5_), channel_id=1, source_target_pairs={{0,4},{4,0},{1,5},{5,1},{2,6},{6,2},{3,7},{7,3},{8,12},{12,8},{9,1... | collective-permute-start | bytes 2408456 | tf_op jit(solution)/shard_map/ppermute | solution.py:347
  82.0 1.4 %shard_map.76.refs_9_ = bf16[512,1536]{1,0:T(8,128)(2,1)S(1)} custom-call(bf16[8,392,128]{2,1,0:T(8,128)(2,1)S(1)} %collective-permute-done.2.piece_ref.refs_5_, bf16[768,1536]{1,0:T(8,128)(2,1)S(1)} %constant_dynamic-update-slice_fusion.w_ref.refs_11_), custom_call_target="tpu_custom_call" | custom-call | flops 1200000000 | bytes 5000000 | tf_op jit(solution)/shard_map/pallas_call | solution.py:123
  83.4 0.0 collective-permute-done.4.piece_ref.refs_6_
  83.4 1.4 %shard_map.77.refs_10_ = bf16[512,1536]{1,0:T(8,128)(2,1)S(1)} custom-call(bf16[8,392,128]{2,1,0:T(8,128)(2,1)S(1)} %collective-permute-done.4.piece_ref.refs_6_, bf16[768,1536]{1,0:T(8,128)(2,1)S(1)} %constant_dynamic-update-slice_fusion.w_ref.refs_11_), custom_call_target="tpu_custom_call" | custom-call | flops 1200000000 | bytes 5000000 | tf_op jit(solution)/shard_map/pallas_call | solution.py:123
  84.8 0.0 collective-permute-done.5.refs_7_
  84.8 8.8 %shard_map.78 = bf16[16,392,128]{2,1,0:T(8,128)(2,1)S(1)} custom-call(s32[4]{0:T(128)S(1)} %pad_add_fusion.place_ref, bf16[264,768]{1,0:T(8,128)(2,1)S(1)} %get-tuple-element.16.refs_0_, bf16[264,768]{1,0:T(8,128)(2,1)S(1)} %collective-permute-done.refs_1_, bf16[264,768]{1,0:T(8,128)(2,1)S(1)} %collective-permute-done.3.refs_2_, ...), custom_call_target="tpu_custom_call" | custom-call | flops 4000000000 | bytes 10000000 | tf_op jit(solution)/shard_map/pallas_call | solution.py:274
  93.6 0.0 copy-start.1
  93.6 0.0 copy-start.2
  93.6 26.2 %all_to_all.10.arrived_ref = bf16[16,392,128]{2,1,0:T(8,128)(2,1)S(1)} all-to-all(bf16[16,392,128]{2,1,0:T(8,128)(2,1)S(1)} %shard_map.78), channel_id=1, replica_groups=mesh['x'=4,'z'=16,'core'=2,'sub'=4] {'x','sub'}, dimensions={0} | all-to-all | bytes 3211264 | tf_op jit(solution)/shard_map/all_to_all | solution.py:352
  119.8 0.0 copy-done.1
  119.8 0.0 copy-done.2
  119.8 1.1 shard_map.79
Async XLA Ops:
  0.0 13.6 %copy-start = (bf16[768,768]{1,0:T(8,128)(2,1)S(1)}, bf16[768,768]{1,0:T(8,128)(2,1)}, u32[]{:S(2)}) copy-start(bf16[768,768]{1,0:T(8,128)(2,1)} %w_ref.2) | copy-start | bytes 3538948
  2.0 62.1 %copy-start.3 = (bf16[768,768]{1,0:T(8,128)(2,1)S(1)}, bf16[768,768]{1,0:T(8,128)(2,1)}, u32[]{:S(2)}) copy-start(bf16[768,768]{1,0:T(8,128)(2,1)} %param.11) | copy-start | bytes 3538948
  2.0 11.6 %all-to-all-start = ((bf16[4,72,768]{2,1,0:T(8,128)(2,1)}), bf16[4,72,768]{2,1,0:T(8,128)(2,1)S(1)}, u32[]{:S(2)}, u32[]{:S(2)}) async-start(bf16[4,72,768]{2,1,0:T(8,128)(2,1)} %shard_map.73), calls=%async_computation | async-start | bytes 884736 | tf_op jit(solution)/shard_map/all_to_all | solution.py:325
  15.1 41.7 %collective-permute-start.1 = (bf16[264,768]{1,0:T(8,128)(2,1)S(1)}, bf16[264,768]{1,0:T(8,128)(2,1)S(1)}, u32[]{:S(2)}, u32[]{:S(2)}) collective-permute-start(bf16[264,768]{1,0:T(8,128)(2,1)S(1)} %get-tuple-element.16.refs_0_), channel_id=1, source_target_pairs={{0,384},{128,0},{256,128},{384,256},{1,385},{129,1},{257,129},{385... | collective-permute-start | bytes 1216520 | tf_op jit(solution)/shard_map/ppermute | solution.py:337
  20.4 36.4 %collective-permute-start = (bf16[264,768]{1,0:T(8,128)(2,1)S(1)}, bf16[264,768]{1,0:T(8,128)(2,1)S(1)}, u32[]{:S(2)}, u32[]{:S(2)}) collective-permute-start(bf16[264,768]{1,0:T(8,128)(2,1)S(1)} %get-tuple-element.16.refs_0_), channel_id=1, source_target_pairs={{0,128},{128,256},{256,384},{384,0},{1,129},{129,257},{257,385},{3... | collective-permute-start | bytes 1216520 | tf_op jit(solution)/shard_map/ppermute | solution.py:337
  22.4 41.8 %copy-start.4 = (bf16[768,768]{1,0:T(8,128)(2,1)S(1)}, bf16[768,768]{1,0:T(8,128)(2,1)}, u32[]{:S(2)}) copy-start(bf16[768,768]{1,0:T(8,128)(2,1)} %param.12) | copy-start | bytes 3538948
  56.8 17.1 %collective-permute-start.2 = (bf16[8,392,128]{2,1,0:T(8,128)(2,1)S(1)}, bf16[8,392,128]{2,1,0:T(8,128)(2,1)S(1)}, u32[]{:S(2)}, u32[]{:S(2)}) collective-permute-start(bf16[8,392,128]{2,1,0:T(8,128)(2,1)S(1)} %bitcast.9), channel_id=1, source_target_pairs={{0,8},{4,124},{8,16},{12,4},{16,24},{20,12},{24,32},{28,20},{32,40... | collective-permute-start | bytes 2408456 | tf_op jit(solution)/shard_map/ppermute | solution.py:344
  61.4 12.4 %collective-permute-start.3 = (bf16[264,768]{1,0:T(8,128)(2,1)S(1)}, bf16[264,768]{1,0:T(8,128)(2,1)S(1)}, u32[]{:S(2)}, u32[]{:S(2)}) collective-permute-start(bf16[264,768]{1,0:T(8,128)(2,1)S(1)} %collective-permute-done.refs_1_), channel_id=1, source_target_pairs={{0,128},{128,256},{256,384},{384,0},{1,129},{129,257},{257,385},{3... | collective-permute-start | bytes 1216520 | tf_op jit(solution)/shard_map/ppermute | solution.py:337
  64.2 19.2 %collective-permute-start.4 = (bf16[8,392,128]{2,1,0:T(8,128)(2,1)S(1)}, bf16[8,392,128]{2,1,0:T(8,128)(2,1)S(1)}, u32[]{:S(2)}, u32[]{:S(2)}) collective-permute-start(bf16[8,392,128]{2,1,0:T(8,128)(2,1)S(1)} %bitcast.10), channel_id=1, source_target_pairs={{0,4},{4,0},{1,5},{5,1},{2,6},{6,2},{3,7},{7,3},{8,12},{12,8},{9,1... | collective-permute-start | bytes 2408456 | tf_op jit(solution)/shard_map/ppermute | solution.py:345
  73.9 10.9 %collective-permute-start.5 = (bf16[8,392,128]{2,1,0:T(8,128)(2,1)S(1)}, bf16[8,392,128]{2,1,0:T(8,128)(2,1)S(1)}, u32[]{:S(2)}, u32[]{:S(2)}) collective-permute-start(bf16[8,392,128]{2,1,0:T(8,128)(2,1)S(1)} %collective-permute-done.2.piece_ref.refs_5_), channel_id=1, source_target_pairs={{0,4},{4,0},{1,5},{5,1},{2,6},{6,2},{3,7},{7,3},{8,12},{12,8},{9,1... | collective-permute-start | bytes 2408456 | tf_op jit(solution)/shard_map/ppermute | solution.py:347
  93.6 26.2 %copy-start.1 = (bf16[768,768]{1,0:T(8,128)(2,1)S(1)}, bf16[768,768]{1,0:T(8,128)(2,1)}, u32[]{:S(2)}) copy-start(bf16[768,768]{1,0:T(8,128)(2,1)} %w_ref.3) | copy-start | bytes 3538948
  93.6 26.2 %copy-start.2 = (bf16[8,8,768]{2,1,0:T(8,128)(2,1)S(1)}, bf16[8,8,768]{2,1,0:T(8,128)(2,1)}, u32[]{:S(2)}) copy-start(bf16[8,8,768]{2,1,0:T(8,128)(2,1)} %param.7) | copy-start | bytes 294916

commit v8 on v7

--- a/solution.py
+++ b/solution.py
@@ -336,14 +336,16 @@
     def along_x(rows, d):
         return lax.ppermute(rows, "x", [(i, (i + d) % X) for i in range(X)])
 
-    below, above = along_x(queries, 1), along_x(queries, X - 1)
+    below = along_x(queries, 1)
     groups = [[2 * k + parity for k in range(Z // 2)] for parity in range(2)]
     same = lax.all_gather(block, "z", axis=0, tiled=False, axis_index_groups=groups)
-    same, queries, below, above = lax.optimization_barrier((same, queries, below, above))
+    same, queries, below = lax.optimization_barrier((same, queries, below))
     there = [(z * CORE + c, (z + 1 - 2 * c) % Z * CORE + c) for z in range(Z) for c in range(CORE)]
     other = lax.ppermute(same, ("z", "core"), there)
     same_far = lax.ppermute(same, "core", [(0, 1), (1, 0)])
-    other, across, ready = lax.optimization_barrier((other, along_x(below, 1), project(same, w_both)))
+    other, across, above, ready = lax.optimization_barrier(
+        (other, along_x(below, 1), along_x(queries, X - 1), project(same, w_both))
+    )
     other_far = lax.ppermute(other, "core", [(0, 1), (1, 0)])
     pieces = [same, other, same_far, other_far]
     ready = [ready, project(other, w_both), project(same_far, w_both)]

time: 121 us -> 119 us (0.983)
  Pallas kernels: 17.6 us -> 16.2 us
    pallas_call x1, Pallas kernels: 8.8 us -> 7.43 us  [attend(): pl.pallas_call(attend_kernel, out_shape=jax.ShapeDtypeStruct((X * SUB, FI...]
where the time goes in v8:
time: 119 us
  blocking collectives  60.5 us (51%)
  starting transfers between devices  35.2 us (30%)
  Pallas kernels  16.2 us (14%)
  waiting for transfers between devices  6.43 us (5%)
    all_gather x1, blocking collectives, body(): lax.all_gather(block, 'z', axis=0, tiled=False, axis_index_groups=groups)  34.1 us
    all_to_all x1, blocking collectives, body(): lax.all_to_all(sent, ('x', 'sub'), split_axis=0, concat_axis=0, tiled=True)  26.4 us
    ppermute x3, starting transfers between devices, along_x(): return lax.ppermute(rows, 'x', [(i, (i + d) % X) for i in range(X)])  10.6 us
    ppermute x1, starting transfers between devices, body(): same_far = lax.ppermute(same, 'core', [(0, 1), (1, 0)])  7.74 us
    pallas_call x1, Pallas kernels, attend(): pl.pallas_call(attend_kernel, out_shape=jax.ShapeDtypeStruct((X * SUB, FI...  7.43 us
    ppermute x1, starting transfers between devices, body(): other_far = lax.ppermute(other, 'core', [(0, 1), (1, 0)])  7.41 us
    all_to_all x1, waiting for transfers between devices, body(): lax.all_to_all(copies, 'sub', split_axis=0, concat_axis=0, tiled=True)  6.42 us
    all_to_all x1, starting transfers between devices, body(): lax.all_to_all(copies, 'sub', split_axis=0, concat_axis=0, tiled=True)  5.14 us
  transfers between devices with their start and end apart: 7, of which 1 were waited for; matrix products, arithmetic and copies ran while one was open for 0% of the time, Pallas kernels for 3%

profile of v8, /device:TPU:1, one launch (start us, length us, event | category | flops | bytes accessed | tf_op | source)
XLA Modules:
  0.0 118.9 jit_solution(6540351866270030681)
XLA Ops:
  0.0 0.0 copy-start
  0.0 2.0 %shard_map.73 = bf16[4,72,768]{2,1,0:T(8,128)(2,1)} custom-call(bf16[64,768]{1,0:T(8,128)(2,1)} %bitcast.13, s32[2,32]{1,0:T(2,128)} %bitcast.15, s32[1,32]{1,0:T(1,128)} %bitcast.16), custom_call_target="tpu_custom_call" | custom-call | flops 2000000000 | bytes 8000000 | tf_op jit(solution)/shard_map/pallas_call | solution.py:318
  2.0 0.0 copy-start.3
  2.0 5.1 %all-to-all-start = ((bf16[4,72,768]{2,1,0:T(8,128)(2,1)}), bf16[4,72,768]{2,1,0:T(8,128)(2,1)S(1)}, u32[]{:S(2)}, u32[]{:S(2)}) async-start(bf16[4,72,768]{2,1,0:T(8,128)(2,1)} %shard_map.73), calls=%async_computation | async-start | bytes 884736 | tf_op jit(solution)/shard_map/all_to_all | solution.py:325
  7.1 0.1 pad_add_fusion.place_ref
  7.2 6.4 %all-to-all-done.normed_ref = bf16[4,72,768]{2,1,0:T(8,128)(2,1)S(1)} async-done(((bf16[4,72,768]{2,1,0:T(8,128)(2,1)}), bf16[4,72,768]{2,1,0:T(8,128)(2,1)S(1)}, u32[]{:S(2)}, u32[]{:S(2)}) %all-to-all-start) | async-done | bytes 442400 | tf_op jit(solution)/shard_map/all_to_all | solution.py:325
  13.6 0.0 copy-done
  13.6 1.5 %shard_map.74 = (bf16[264,768]{1,0:T(8,128)(2,1)S(1)}, bf16[392,128]{1,0:T(8,128)(2,1)S(1)}) custom-call(s32[4]{0:T(128)S(1)} %pad_add_fusion.place_ref, bf16[4,72,768]{2,1,0:T(8,128)(2,1)S(1)} %all-to-all-done.normed_ref, bf16[768,768]{1,0:T(8,128)(2,1)S(1)} %copy-done), custom_call_target="tpu_custom_call" | custom-call | tf_op jit(solution)/shard_map/pallas_call | solution.py:326
  15.1 4.0 %collective-permute-start = (bf16[264,768]{1,0:T(8,128)(2,1)S(1)}, bf16[264,768]{1,0:T(8,128)(2,1)S(1)}, u32[]{:S(2)}, u32[]{:S(2)}) collective-permute-start(bf16[264,768]{1,0:T(8,128)(2,1)S(1)} %get-tuple-element.16.refs_0_), channel_id=1, source_target_pairs={{0,128},{128,256},{256,384},{384,0},{1,129},{129,257},{257,385},{3... | collective-permute-start | bytes 1216520 | tf_op jit(solution)/shard_map/ppermute | solution.py:337
  19.2 0.0 copy-start.4
  19.2 34.1 %all-gather = bf16[3136,128]{1,0:T(8,128)(2,1)S(1)} all-gather(bf16[392,128]{1,0:T(8,128)(2,1)S(1)} %get-tuple-element.14), channel_id=2, replica_groups={{0,16,32,48,64,80,96,112},{8,24,40,56,72,88,104,120},{1,17,33,49,65,81,..., dimensions={0}, use_global_device_ids=true | all-gather | bytes 903168 | tf_op jit(solution)/shard_map/all_gather | solution.py:341
  53.3 0.0 collective-permute-done.refs_1_
  53.3 4.3 %collective-permute-start.1 = (bf16[8,392,128]{2,1,0:T(8,128)(2,1)S(1)}, bf16[8,392,128]{2,1,0:T(8,128)(2,1)S(1)}, u32[]{:S(2)}, u32[]{:S(2)}) collective-permute-start(bf16[8,392,128]{2,1,0:T(8,128)(2,1)S(1)} %bitcast.9), channel_id=1, source_target_pairs={{0,8},{4,124},{8,16},{12,4},{16,24},{20,12},{24,32},{28,20},{32,40... | collective-permute-start | bytes 2408456 | tf_op jit(solution)/shard_map/ppermute | solution.py:344
  57.6 4.0 %collective-permute-start.3 = (bf16[264,768]{1,0:T(8,128)(2,1)S(1)}, bf16[264,768]{1,0:T(8,128)(2,1)S(1)}, u32[]{:S(2)}, u32[]{:S(2)}) collective-permute-start(bf16[264,768]{1,0:T(8,128)(2,1)S(1)} %get-tuple-element.16.refs_0_), channel_id=1, source_target_pairs={{0,384},{128,0},{256,128},{384,256},{1,385},{129,1},{257,129},{385... | collective-permute-start | bytes 1216520 | tf_op jit(solution)/shard_map/ppermute | solution.py:337
  61.7 2.6 %collective-permute-start.2 = (bf16[264,768]{1,0:T(8,128)(2,1)S(1)}, bf16[264,768]{1,0:T(8,128)(2,1)S(1)}, u32[]{:S(2)}, u32[]{:S(2)}) collective-permute-start(bf16[264,768]{1,0:T(8,128)(2,1)S(1)} %collective-permute-done.refs_1_), channel_id=1, source_target_pairs={{0,128},{128,256},{256,384},{384,0},{1,129},{129,257},{257,385},{3... | collective-permute-start | bytes 1216520 | tf_op jit(solution)/shard_map/ppermute | solution.py:337
  64.2 0.0 copy-done.3
  64.3 0.1 constant_dynamic-update-slice_fusion.1
  64.3 0.0 copy-done.4
  64.4 0.1 constant_dynamic-update-slice_fusion.w_ref.refs_11_
  64.5 7.7 %collective-permute-start.4 = (bf16[8,392,128]{2,1,0:T(8,128)(2,1)S(1)}, bf16[8,392,128]{2,1,0:T(8,128)(2,1)S(1)}, u32[]{:S(2)}, u32[]{:S(2)}) collective-permute-start(bf16[8,392,128]{2,1,0:T(8,128)(2,1)S(1)} %bitcast.10), channel_id=1, source_target_pairs={{0,4},{4,0},{1,5},{5,1},{2,6},{6,2},{3,7},{7,3},{8,12},{12,8},{9,1... | collective-permute-start | bytes 2408456 | tf_op jit(solution)/shard_map/ppermute | solution.py:345
  72.2 1.4 %shard_map.75.refs_8_ = bf16[512,1536]{1,0:T(8,128)(2,1)S(1)} custom-call(bf16[8,392,128]{2,1,0:T(8,128)(2,1)S(1)} %bitcast.11, bf16[768,1536]{1,0:T(8,128)(2,1)S(1)} %constant_dynamic-update-slice_fusion.w_ref.refs_11_), custom_call_target="tpu_custom_call" | custom-call | flops 1200000000 | bytes 5000000 | tf_op jit(solution)/shard_map/pallas_call | solution.py:123
  73.6 0.0 collective-permute-done.3.refs_3_
  73.6 0.0 collective-permute-done.2.refs_2_
  73.6 0.0 collective-permute-done.1.piece_ref.refs_5_
  73.6 7.4 %collective-permute-start.5 = (bf16[8,392,128]{2,1,0:T(8,128)(2,1)S(1)}, bf16[8,392,128]{2,1,0:T(8,128)(2,1)S(1)}, u32[]{:S(2)}, u32[]{:S(2)}) collective-permute-start(bf16[8,392,128]{2,1,0:T(8,128)(2,1)S(1)} %collective-permute-done.1.piece_ref.refs_5_), channel_id=1, source_target_pairs={{0,4},{4,0},{1,5},{5,1},{2,6},{6,2},{3,7},{7,3},{8,12},{12,8},{9,1... | collective-permute-start | bytes 2408456 | tf_op jit(solution)/shard_map/ppermute | solution.py:349
  81.0 1.4 %shard_map.76.refs_9_ = bf16[512,1536]{1,0:T(8,128)(2,1)S(1)} custom-call(bf16[8,392,128]{2,1,0:T(8,128)(2,1)S(1)} %collective-permute-done.1.piece_ref.refs_5_, bf16[768,1536]{1,0:T(8,128)(2,1)S(1)} %constant_dynamic-update-slice_fusion.w_ref.refs_11_), custom_call_target="tpu_custom_call" | custom-call | flops 1200000000 | bytes 5000000 | tf_op jit(solution)/shard_map/pallas_call | solution.py:123
  82.4 0.0 collective-permute-done.4.piece_ref.refs_6_
  82.4 1.4 %shard_map.77.refs_10_ = bf16[512,1536]{1,0:T(8,128)(2,1)S(1)} custom-call(bf16[8,392,128]{2,1,0:T(8,128)(2,1)S(1)} %collective-permute-done.4.piece_ref.refs_6_, bf16[768,1536]{1,0:T(8,128)(2,1)S(1)} %constant_dynamic-update-slice_fusion.w_ref.refs_11_), custom_call_target="tpu_custom_call" | custom-call | flops 1200000000 | bytes 5000000 | tf_op jit(solution)/shard_map/pallas_call | solution.py:123
  83.8 0.0 collective-permute-done.5.refs_7_
  83.8 7.4 %shard_map.78 = bf16[16,392,128]{2,1,0:T(8,128)(2,1)S(1)} custom-call(s32[4]{0:T(128)S(1)} %pad_add_fusion.place_ref, bf16[264,768]{1,0:T(8,128)(2,1)S(1)} %get-tuple-element.16.refs_0_, bf16[264,768]{1,0:T(8,128)(2,1)S(1)} %collective-permute-done.refs_1_, bf16[264,768]{1,0:T(8,128)(2,1)S(1)} %collective-permute-done.2.refs_2_, ...), custom_call_target="tpu_custom_call" | custom-call | flops 4000000000 | bytes 10000000 | tf_op jit(solution)/shard_map/pallas_call | solution.py:274
  91.3 0.0 copy-start.1
  91.3 0.0 copy-start.2
  91.3 26.4 %all_to_all.10.arrived_ref = bf16[16,392,128]{2,1,0:T(8,128)(2,1)S(1)} all-to-all(bf16[16,392,128]{2,1,0:T(8,128)(2,1)S(1)} %shard_map.78), channel_id=1, replica_groups=mesh['x'=4,'z'=16,'core'=2,'sub'=4] {'x','sub'}, dimensions={0} | all-to-all | bytes 3211264 | tf_op jit(solution)/shard_map/all_to_all | solution.py:354
  117.7 0.0 copy-done.1
  117.7 0.0 copy-done.2
  117.7 1.1 shard_map.79
Async XLA Ops:
  0.0 13.6 %copy-start = (bf16[768,768]{1,0:T(8,128)(2,1)S(1)}, bf16[768,768]{1,0:T(8,128)(2,1)}, u32[]{:S(2)}) copy-start(bf16[768,768]{1,0:T(8,128)(2,1)} %w_ref.2) | copy-start | bytes 3538948
  2.0 62.3 %copy-start.3 = (bf16[768,768]{1,0:T(8,128)(2,1)S(1)}, bf16[768,768]{1,0:T(8,128)(2,1)}, u32[]{:S(2)}) copy-start(bf16[768,768]{1,0:T(8,128)(2,1)} %param.11) | copy-start | bytes 3538948
  2.0 11.6 %all-to-all-start = ((bf16[4,72,768]{2,1,0:T(8,128)(2,1)}), bf16[4,72,768]{2,1,0:T(8,128)(2,1)S(1)}, u32[]{:S(2)}, u32[]{:S(2)}) async-start(bf16[4,72,768]{2,1,0:T(8,128)(2,1)} %shard_map.73), calls=%async_computation | async-start | bytes 884736 | tf_op jit(solution)/shard_map/all_to_all | solution.py:325
  15.1 38.2 %collective-permute-start = (bf16[264,768]{1,0:T(8,128)(2,1)S(1)}, bf16[264,768]{1,0:T(8,128)(2,1)S(1)}, u32[]{:S(2)}, u32[]{:S(2)}) collective-permute-start(bf16[264,768]{1,0:T(8,128)(2,1)S(1)} %get-tuple-element.16.refs_0_), channel_id=1, source_target_pairs={{0,128},{128,256},{256,384},{384,0},{1,129},{129,257},{257,385},{3... | collective-permute-start | bytes 1216520 | tf_op jit(solution)/shard_map/ppermute | solution.py:337
  19.2 45.2 %copy-start.4 = (bf16[768,768]{1,0:T(8,128)(2,1)S(1)}, bf16[768,768]{1,0:T(8,128)(2,1)}, u32[]{:S(2)}) copy-start(bf16[768,768]{1,0:T(8,128)(2,1)} %param.12) | copy-start | bytes 3538948
  53.3 20.3 %collective-permute-start.1 = (bf16[8,392,128]{2,1,0:T(8,128)(2,1)S(1)}, bf16[8,392,128]{2,1,0:T(8,128)(2,1)S(1)}, u32[]{:S(2)}, u32[]{:S(2)}) collective-permute-start(bf16[8,392,128]{2,1,0:T(8,128)(2,1)S(1)} %bitcast.9), channel_id=1, source_target_pairs={{0,8},{4,124},{8,16},{12,4},{16,24},{20,12},{24,32},{28,20},{32,40... | collective-permute-start | bytes 2408456 | tf_op jit(solution)/shard_map/ppermute | solution.py:344
  57.6 16.0 %collective-permute-start.3 = (bf16[264,768]{1,0:T(8,128)(2,1)S(1)}, bf16[264,768]{1,0:T(8,128)(2,1)S(1)}, u32[]{:S(2)}, u32[]{:S(2)}) collective-permute-start(bf16[264,768]{1,0:T(8,128)(2,1)S(1)} %get-tuple-element.16.refs_0_), channel_id=1, source_target_pairs={{0,384},{128,0},{256,128},{384,256},{1,385},{129,1},{257,129},{385... | collective-permute-start | bytes 1216520 | tf_op jit(solution)/shard_map/ppermute | solution.py:337
  61.7 11.9 %collective-permute-start.2 = (bf16[264,768]{1,0:T(8,128)(2,1)S(1)}, bf16[264,768]{1,0:T(8,128)(2,1)S(1)}, u32[]{:S(2)}, u32[]{:S(2)}) collective-permute-start(bf16[264,768]{1,0:T(8,128)(2,1)S(1)} %collective-permute-done.refs_1_), channel_id=1, source_target_pairs={{0,128},{128,256},{256,384},{384,0},{1,129},{129,257},{257,385},{3... | collective-permute-start | bytes 1216520 | tf_op jit(solution)/shard_map/ppermute | solution.py:337
  64.5 18.0 %collective-permute-start.4 = (bf16[8,392,128]{2,1,0:T(8,128)(2,1)S(1)}, bf16[8,392,128]{2,1,0:T(8,128)(2,1)S(1)}, u32[]{:S(2)}, u32[]{:S(2)}) collective-permute-start(bf16[8,392,128]{2,1,0:T(8,128)(2,1)S(1)} %bitcast.10), channel_id=1, source_target_pairs={{0,4},{4,0},{1,5},{5,1},{2,6},{6,2},{3,7},{7,3},{8,12},{12,8},{9,1... | collective-permute-start | bytes 2408456 | tf_op jit(solution)/shard_map/ppermute | solution.py:345
  73.6 10.2 %collective-permute-start.5 = (bf16[8,392,128]{2,1,0:T(8,128)(2,1)S(1)}, bf16[8,392,128]{2,1,0:T(8,128)(2,1)S(1)}, u32[]{:S(2)}, u32[]{:S(2)}) collective-permute-start(bf16[8,392,128]{2,1,0:T(8,128)(2,1)S(1)} %collective-permute-done.1.piece_ref.refs_5_), channel_id=1, source_target_pairs={{0,4},{4,0},{1,5},{5,1},{2,6},{6,2},{3,7},{7,3},{8,12},{12,8},{9,1... | collective-permute-start | bytes 2408456 | tf_op jit(solution)/shard_map/ppermute | solution.py:349
  91.3 26.4 %copy-start.1 = (bf16[768,768]{1,0:T(8,128)(2,1)S(1)}, bf16[768,768]{1,0:T(8,128)(2,1)}, u32[]{:S(2)}) copy-start(bf16[768,768]{1,0:T(8,128)(2,1)} %w_ref.3) | copy-start | bytes 3538948
  91.3 26.4 %copy-start.2 = (bf16[8,8,768]{2,1,0:T(8,128)(2,1)S(1)}, bf16[8,8,768]{2,1,0:T(8,128)(2,1)}, u32[]{:S(2)}) copy-start(bf16[8,8,768]{2,1,0:T(8,128)(2,1)} %param.7) | copy-start | bytes 294916
